TPU v7x, 32 devices: a whole 2x2x4 slice. The times are simulated.
32 devices in a mesh: blk: 8 (over z, y), inner: 4 (over x, core).
Axes of the slice: x: 2, y: 2, z: 4, core: 2. Of those that a mesh axis runs over, the one named last changes fastest.
Arguments:
- density: float32 [64, 9, 128, 128], P(('blk', 'inner')), may hold values from -0.5 to 0.5
- block_cols: int32 [64, 9], P(('blk', 'inner')), may hold values from 0 to 63, as said below
- targets: int32 [64, 9, 9], P(('blk', 'inner')), may hold values from 0 to 9, as said below
Outputs:
- purified: float32 [64, 9, 128, 128], P(('blk', 'inner'))
Inputs may be any that keep to these rules, and one draw needn't show every extreme that they name: `block_cols`: strips are runs of 8 block rows. Slots 0 .. 2, 3 .. 5 and 6 .. 8 of row k hold 3 distinct columns each, ascending, from the strip before k's own (cyclically), k's own strip, and the strip after it (cyclically); the own group always contains column k. targets[k, s, t] is the slot u with block_cols[block_cols[k, s], u] == block_cols[k, t], or 9 where row block_cols[k, s] does not store that column.
All inputs are finite; a program needn't handle non-finite values.
Results may differ from a plain program's by a relative error of at most 0.0001.
Values sent between devices are 32-bit elements; how exact they have to be, the bound alone decides.
No kernel may reach another device: no remote copies, remote signals or barrier semaphores. Data moves between devices by JAX's collectives and lax.ppermute only.
A program may use at most 128 MiB of HBM per device.

v0:
```python
import functools

import jax
import jax.numpy as jnp
from jax import lax
from jax.experimental import pallas as pl
from jax.experimental.pallas import tpu as pltpu
from jax.sharding import PartitionSpec as P

TN = (((0,), (0,)), ((), ()))


def shifted(value, steps):
    count = lax.axis_size("blk")
    pairs = [(source, (source + steps) % count) for source in range(count)]
    return lax.ppermute(value, "blk", pairs)


def swapped(value, distance):
    count = lax.axis_size("inner")
    return lax.ppermute(value, "inner", [(i, i ^ distance) for i in range(count)])


def halves(value):
    held = [value]
    for bit in [1 << i for i in range(20) if (1 << i) < lax.axis_size("inner") // 2]:
        held = held + [swapped(one, bit) for one in held]
    return held


def across(value, after=()):
    count = lax.axis_size("inner")
    value = lax.optimization_barrier((value, *after))[0] if after else value
    return [swapped(value, count // 2)] if count > 1 else []


def parted(value, size):
    if size & (size - 1) == 0:
        return value >> (size.bit_length() - 1), value & (size - 1)
    return lax.div(value, size), lax.rem(value, size)


def pack_kernel(dims, density, targets, cols, inner, *refs):
    local_rows, slots, side, strip_rows, meta_rows = dims
    per = slots // 3
    data = local_rows * per * side
    outs, (targets_v, cols_s, sems, meta_sems) = refs[:3], refs[3:]
    arrivals = [
        pltpu.make_async_copy(targets, targets_v, meta_sems.at[0]),
        pltpu.make_async_copy(cols, cols_s, meta_sems.at[1]),
    ]
    for arrival in arrivals:
        arrival.start()
    copies = []
    for group in (0, 2, 1):
        for row in range(local_rows):
            source = density.at[pl.ds((row * slots + group * per) * side, per * side)]
            dest = outs[group].at[pl.ds(row * per * side, per * side)]
            copies.append(pltpu.make_async_copy(source, dest, sems.at[group, row]))
            copies[-1].start()
    for group in (0, 2, 1):
        outs[group][data : data + meta_rows, :] = jnp.zeros((meta_rows, side), jnp.float32)
    for arrival in arrivals:
        arrival.wait()
    for group in (0, 2, 1):
        for row in range(local_rows):
            for slot in range(per):
                in_strip = parted(cols_s[row, group * per + slot], strip_rows)[1]
                owner, line = parted(in_strip, local_rows)
                code = (owner ^ inner[0]) * local_rows + line
                at = data + row * per + slot
                chosen = targets_v[group * per + slot, row : row + 1, :]
                outs[group][at : at + 1, :slots] = chosen.astype(jnp.float32)
                code = jnp.full((1, 1), code, jnp.int32).astype(jnp.float32)
                outs[group][at : at + 1, slots : slots + 1] = code
    for copy in copies:
        copy.wait()


def sums_kernel(dims, plan, *refs):
    offset, parts, local_rows, slots, side, meta_rows, a_at, group_total, first, width = dims
    per = slots // 3
    data = local_rows * per * side
    payloads = [refs[g * parts : (g + 1) * parts] for g in range(group_total)]
    *base, out, meta, listed, acc, meta_sems = refs[group_total * parts :]

    fetches = []
    for part in range(parts):
        source = payloads[a_at][part].at[pl.ds(data, meta_rows)]
        fetches.append(pltpu.make_async_copy(source, meta.at[part], meta_sems.at[part]))
        fetches[-1].start()
    acc[...] = jnp.zeros_like(acc)

    def cut(block):
        high = block.astype(jnp.bfloat16)
        return high, (block - high.astype(jnp.float32)).astype(jnp.bfloat16)

    for part in range(parts):
        fetches[part].wait()
        count = jnp.int32(0)
        for line in range(local_rows * per):
            dest = meta[part, line, slots].astype(jnp.int32) - (offset + part) * local_rows
            listed[0, count] = line
            listed[1, count] = line // per
            listed[2, count] = dest
            mine = (dest >= 0) & (dest < local_rows)
            count = count + mine.astype(jnp.int32)

        def multiply(item, _, part=part):
            line, row, dest = listed[0, item], listed[1, item], listed[2, item]
            start = pl.multiple_of(line * side, side)
            a_high, a_low = cut(payloads[a_at][part][pl.ds(start, side), :])
            a = jnp.concatenate([a_high, a_high, a_low], axis=0)
            for group, lane in plan:
                blocks = []
                for t in range(per):
                    start = pl.multiple_of((row * per + t) * side, side)
                    blocks.append(payloads[group][part][pl.ds(start, side), :])
                b_high, b_low = cut(jnp.concatenate(blocks, axis=1))
                b = jnp.concatenate([b_high, b_low, b_high], axis=0)
                result = lax.dot_general(a, b, TN, preferred_element_type=jnp.float32)
                for t in range(per):
                    target = meta[part, line, lane + t].astype(jnp.int32)
                    place = jnp.minimum(target - first, width)
                    acc[dest, place] += result[:, t * side : (t + 1) * side]
            return 0

        lax.fori_loop(0, count, multiply, 0)
    for row in range(local_rows):
        for t in range(width):
            if base:
                out[row, t] = base[0][row, t] - acc[row, t]
            elif width == slots:
                start = (row * per + t % per) * side
                mine = payloads[t // per][0][start : start + side, :]
                out[row, t] = 2.0 * mine - acc[row, t]
            else:
                start = (row * width + t) * side
                out[start : start + side, :] = acc[row, t]


def finish_kernel(base, to_below, to_above_own, from_below, to_above_next, out, result, sems):
    local_rows, slots, side, _ = base.shape
    per = slots // 3
    copies = []
    for row in range(local_rows):
        for slot in range(per):
            start = (row * per + slot) * side
            lines = slice(start, start + side)
            result[row, slot] = base[row, slot] - to_below[lines, :]
            both = to_above_own[lines, :] + from_below[lines, :]
            result[row, per + slot] = base[row, per + slot] - both
            result[row, 2 * per + slot] = base[row, 2 * per + slot] - to_above_next[lines, :]
        copies.append(pltpu.make_async_copy(result.at[row], out.at[row], sems.at[row]))
        copies[-1].start()
    for copy in copies:
        copy.wait()


def shards(density, block_cols, targets):
    local_rows, slots, side, _ = density.shape
    per = slots // 3
    parts = lax.axis_size("inner")
    strip_rows = local_rows * parts
    meta_rows = local_rows * per + -(local_rows * per) % 8
    used_rows = local_rows * per * side + meta_rows
    payload_rows = used_rows + 16
    in_hbm = pl.BlockSpec(memory_space=pltpu.HBM)
    scalars = pl.BlockSpec(memory_space=pltpu.SMEM)
    vectors = pl.BlockSpec(memory_space=pltpu.VMEM)

    lower, middle, upper = pl.pallas_call(
        functools.partial(pack_kernel, (local_rows, slots, side, strip_rows, meta_rows)),
        out_shape=[jax.ShapeDtypeStruct((payload_rows, side), jnp.float32)] * 3,
        in_specs=[in_hbm, in_hbm, in_hbm, scalars],
        out_specs=[vectors] * 3,
        scratch_shapes=[
            pltpu.VMEM((slots, local_rows, slots), jnp.int32),
            pltpu.SMEM((local_rows, slots), jnp.int32),
            pltpu.SemaphoreType.DMA((3, local_rows)),
            pltpu.SemaphoreType.DMA((2,)),
        ],
        compiler_params=pltpu.CompilerParams(vmem_limit_bytes=48 << 20),
        name="pack",
    )(
        density.reshape(-1, side),
        jnp.transpose(targets, (1, 0, 2)),
        block_cols,
        lax.axis_index("inner").reshape(1),
    )

    spare = 16

    def sums(groups, a_at, plan, first, width, offset=0, base=()):
        held = len(groups[0])
        dims = (offset, held, local_rows, slots, side, meta_rows, a_at, len(groups), first, width)
        return pl.pallas_call(
            functools.partial(sums_kernel, dims, plan),
            out_shape=jax.ShapeDtypeStruct(
                (local_rows * per * side + spare, side) if width == per else density.shape,
                jnp.float32,
            ),
            in_specs=[vectors] * (held * len(groups) + len(base)),
            out_specs=vectors,
            scratch_shapes=[
                pltpu.SMEM((held, meta_rows, side), jnp.float32),
                pltpu.SMEM((3, local_rows * per + 1), jnp.int32),
                pltpu.VMEM((local_rows, width + 1, side, side), jnp.float32),
                pltpu.SemaphoreType.DMA((held,)),
            ],
            compiler_params=pltpu.CompilerParams(vmem_limit_bytes=16 << 20),
            cost_estimate=pl.CostEstimate(flops=1, bytes_accessed=1, transcendentals=0),
            name="sums",
        )(*[payload for group in groups for payload in group], *base)

    def spread(far):
        return [one for value in far for one in halves(value[:used_rows])]

    def tied(values, *after):
        return list(lax.optimization_barrier((*values, *after)))[: len(values)]

    own_plan = ((0, 0), (1, per), (2, 2 * per))
    below = shifted(upper, 1)
    lowers, middles, uppers = halves(lower), halves(middle), halves(upper)
    far_lower = across(lower)
    base = sums([lowers, middles, uppers], 1, own_plan, 0, slots)

    far_middle = across(middle, [base])
    far_lowers = spread(tied(far_lower, base))
    far_lowers = tied(far_lowers, below)
    above_own = sums([lowers + far_lowers], 0, ((0, 0),), per, per)
    to_above_own = shifted(above_own, -1)

    far_upper = across(upper, [above_own])
    far_middles = spread(tied(far_middle, above_own))
    all_middles = middles + far_middles
    above_next = sums([lowers + far_lowers, all_middles], 0, ((1, per),), 2 * per, per)
    to_above_next = shifted(above_next, -1)

    belows = halves(below)
    far_below = across(below, [above_next, to_above_own, *belows])
    far_uppers = spread(tied(far_upper, above_next))
    to_next = sums([uppers + far_uppers, all_middles], 0, ((1, per),), 0, per)
    to_below = shifted(to_next, 1)
    if far_lowers:
        near = len(lowers)
        groups = [far_lowers, far_middles, far_uppers]
        base = sums(groups, 1, own_plan, 0, slots, near, [base])
        far_below = tied(far_below, base, to_next, to_above_next)
    belows = belows + spread(far_below)
    from_below = sums([belows], 0, ((0, 2 * per),), per, per)
    return pl.pallas_call(
        finish_kernel,
        out_shape=jax.ShapeDtypeStruct(density.shape, jnp.float32),
        in_specs=[vectors] * 5,
        out_specs=in_hbm,
        scratch_shapes=[
            pltpu.VMEM(density.shape, jnp.float32),
            pltpu.SemaphoreType.DMA((local_rows,)),
        ],
        compiler_params=pltpu.CompilerParams(vmem_limit_bytes=16 << 20),
        cost_estimate=pl.CostEstimate(flops=1, bytes_accessed=1, transcendentals=0),
        name="finish",
    )(base, to_below, to_above_own, from_below, to_above_next)


def solution(mesh):
    return jax.shard_map(
        shards,
        mesh=mesh,
        in_specs=(
            P(("blk", "inner"), None, None, None),
            P(("blk", "inner"), None),
            P(("blk", "inner"), None, None),
        ),
        out_specs=P(("blk", "inner"), None, None, None),
        check_vma=False,
    )
```

profile of v0, /device:TPU:0, one launch (start us, length us, event | category | flops | bytes accessed | tf_op | source)
XLA Modules:
  0.0 62.7 jit_solution(567913924516856155)
XLA Ops:
  0.0 0.0 copy-start
  0.0 1.3 %copy-done = f32[2,9,128,128]{3,2,1,0:T(8,128)S(1)} copy-done((f32[2,9,128,128]{3,2,1,0:T(8,128)S(1)}, f32[2,9,128,128]{3,2,1,0:T(8,128)}, u32[]{:S(2)}) %copy-start) | copy-done | bytes 1179672
  1.3 0.0 copy-start.1
  1.3 0.7 %copy-done.1 = s32[2,9,9]{2,0,1:T(2,128)S(1)} copy-done((s32[2,9,9]{2,0,1:T(2,128)S(1)}, s32[2,9,9]{2,0,1:T(2,128)}, u32[]{:S(2)}) %copy-start.1) | copy-done | bytes 672
  2.0 0.0 copy-start.2
  2.0 0.7 %copy-done.2 = s32[2,9]{1,0:T(2,128)S(1)} copy-done((s32[2,9]{1,0:T(2,128)S(1)}, s32[2,9]{1,0:T(2,128)}, u32[]{:S(2)}) %copy-start.2) | copy-done | bytes 96
  2.7 1.6 %pack.1 = (f32[792,128]{1,0:T(8,128)S(1)}, f32[792,128]{1,0:T(8,128)S(1)}, f32[792,128]{1,0:T(8,128)S(1)}) custom-call(f32[2304,128]{1,0:T(8,128)S(1)} %bitcast.3, s32[9,2,9]{2,1,0:T(2,128)S(1)} %bitcast.4, s32[2,9]{1,0:T(2,128)S(1)} %copy-done.2, s32[1]{0:T(128)} %bitcast.2.inner), custom_call_target="tpu_custom_call" | custom-call | tf_op jit(solution)/shard_map/pack/pallas_call | solution.py:172
  4.3 0.5 collective-permute-start.1
  4.8 0.1 collective-permute-start.2
  4.9 0.4 collective-permute-start.3
  5.3 2.6 %collective-permute-start = (f32[792,128]{1,0:T(8,128)S(1)}, f32[792,128]{1,0:T(8,128)S(1)}, u32[]{:S(2)}, u32[]{:S(2)}) collective-permute-start(f32[792,128]{1,0:T(8,128)S(1)} %get-tuple-element.17.refs_0_), channel_id=1, source_target_pairs={{0,2},{1,3},{2,0},{3,1},{4,6},{5,7},{6,4},{7,5},{8,10},{9,11},{10,... | collective-permute-start | bytes 1216520 | tf_op jit(solution)/shard_map/ppermute | solution.py:21
  7.9 1.5 %collective-permute-start.5 = (f32[792,128]{1,0:T(8,128)S(1)}, f32[792,128]{1,0:T(8,128)S(1)}, u32[]{:S(2)}, u32[]{:S(2)}) collective-permute-start(f32[792,128]{1,0:T(8,128)S(1)} %get-tuple-element.25.refs_4_.refs_0_), channel_id=1, source_target_pairs={{0,4},{4,8},{8,12},{12,16},{16,20},{20,24},{24,28},{28,0},{1,5},{5... | collective-permute-start | bytes 1216520 | tf_op jit(solution)/shard_map/ppermute | solution.py:16
  9.4 0.0 collective-permute-done.1.refs_1_
  9.4 0.0 collective-permute-done.2.refs_3_.refs_5_
  9.4 0.0 collective-permute-done.3.refs_5_.refs_1_
  9.4 2.9 %sums.6.refs_6_ = f32[2,9,128,128]{3,2,1,0:T(8,128)S(1)} custom-call(f32[792,128]{1,0:T(8,128)S(1)} %get-tuple-element.17.refs_0_, f32[792,128]{1,0:T(8,128)S(1)} %collective-permute-done.1.refs_1_, f32[792,128]{1,0:T(8,128)S(1)} %get-tuple-element.23.refs_2_.refs_4_, f32[792,128]{1,0:T(8,128)S(1)} %collective-permute-done.2.refs_3_.refs_5_, ...), custom_call_target="tpu_custom_call" | custom-call | flops 1 | bytes 1 | tf_op jit(solution)/shard_map/sums/pallas_call | solution.py:197
  12.3 0.4 collective-permute-start.6
  12.8 5.3 %collective-permute-done = f32[792,128]{1,0:T(8,128)S(1)} collective-permute-done((f32[792,128]{1,0:T(8,128)S(1)}, f32[792,128]{1,0:T(8,128)S(1)}, u32[]{:S(2)}, u32[]{:S(2)}) %collective-permute-start) | collective-permute-done | bytes 405536 | tf_op jit(solution)/shard_map/ppermute | solution.py:21
  18.2 0.1 collective-permute-start.4
  18.2 3.9 %collective-permute-done.5.refs_0_ = f32[792,128]{1,0:T(8,128)S(1)} collective-permute-done((f32[792,128]{1,0:T(8,128)S(1)}, f32[792,128]{1,0:T(8,128)S(1)}, u32[]{:S(2)}, u32[]{:S(2)}) %collective-permute-start.5) | collective-permute-done | bytes 405536 | tf_op jit(solution)/shard_map/ppermute | solution.py:16
  22.2 0.0 collective-permute-start.12
  22.2 0.0 collective-permute-done.4.refs_3_.refs_1_
  22.2 2.7 %sums.7 = f32[784,128]{1,0:T(8,128)S(1)} custom-call(f32[792,128]{1,0:T(8,128)S(1)} %get-tuple-element.17.refs_0_, f32[792,128]{1,0:T(8,128)S(1)} %collective-permute-done.1.refs_1_, f32[776,128]{1,0:T(8,128)S(1)} %slice.12.refs_2_.refs_0_, f32[776,128]{1,0:T(8,128)S(1)} %collective-permute-done.4.refs_3_.refs_1_), custom_call_target="tpu_custom_call" | custom-call | flops 1 | bytes 1 | tf_op jit(solution)/shard_map/sums/pallas_call | solution.py:197
  24.9 2.9 %collective-permute-start.11 = (f32[784,128]{1,0:T(8,128)S(1)}, f32[784,128]{1,0:T(8,128)S(1)}, u32[]{:S(2)}, u32[]{:S(2)}) collective-permute-start(f32[784,128]{1,0:T(8,128)S(1)} %sums.7), channel_id=1, source_target_pairs={{0,28},{4,0},{8,4},{12,8},{16,12},{20,16},{24,20},{28,24},{1,29},{... | collective-permute-start | bytes 1204232 | tf_op jit(solution)/shard_map/ppermute | solution.py:16
  27.7 1.5 %collective-permute-start.8 = (f32[792,128]{1,0:T(8,128)S(1)}, f32[792,128]{1,0:T(8,128)S(1)}, u32[]{:S(2)}, u32[]{:S(2)}) collective-permute-start(f32[792,128]{1,0:T(8,128)S(1)} %get-tuple-element.25.refs_4_.refs_0_), channel_id=1, source_target_pairs={{0,2},{1,3},{2,0},{3,1},{4,6},{5,7},{6,4},{7,5},{8,10},{9,11},{10,... | collective-permute-start | bytes 1216520 | tf_op jit(solution)/shard_map/ppermute | solution.py:21
  29.2 0.0 collective-permute-done.6
  29.3 0.1 collective-permute-start.7
  29.3 1.7 %collective-permute-done.7.refs_7_.refs_3_ = f32[776,128]{1,0:T(8,128)S(1)} collective-permute-done((f32[776,128]{1,0:T(8,128)S(1)}, f32[776,128]{1,0:T(8,128)S(1)}, u32[]{:S(2)}, u32[]{:S(2)}) %collective-permute-start.7) | collective-permute-done | bytes 397344 | tf_op jit(solution)/shard_map/ppermute | solution.py:21
  31.1 2.7 %sums.8 = f32[784,128]{1,0:T(8,128)S(1)} custom-call(f32[792,128]{1,0:T(8,128)S(1)} %get-tuple-element.17.refs_0_, f32[792,128]{1,0:T(8,128)S(1)} %collective-permute-done.1.refs_1_, f32[776,128]{1,0:T(8,128)S(1)} %slice.12.refs_2_.refs_0_, f32[776,128]{1,0:T(8,128)S(1)} %collective-permute-done.4.refs_3_.refs_1_, ...), custom_call_target="tpu_custom_call" | custom-call | flops 1 | bytes 1 | tf_op jit(solution)/shard_map/sums/pallas_call | solution.py:197
  33.8 0.0 collective-permute-done.12.refs_1_
  33.8 2.6 %collective-permute-done.11.to_above_own = f32[784,128]{1,0:T(8,128)S(1)} collective-permute-done((f32[784,128]{1,0:T(8,128)S(1)}, f32[784,128]{1,0:T(8,128)S(1)}, u32[]{:S(2)}, u32[]{:S(2)}) %collective-permute-start.11) | collective-permute-done | bytes 401440 | tf_op jit(solution)/shard_map/ppermute | solution.py:16
  36.4 0.9 %collective-permute-start.13 = (f32[792,128]{1,0:T(8,128)S(1)}, f32[792,128]{1,0:T(8,128)S(1)}, u32[]{:S(2)}, u32[]{:S(2)}) collective-permute-start(f32[792,128]{1,0:T(8,128)S(1)} %collective-permute-done.5.refs_0_), channel_id=1, source_target_pairs={{0,2},{1,3},{2,0},{3,1},{4,6},{5,7},{6,4},{7,5},{8,10},{9,11},{10,... | collective-permute-start | bytes 1216520 | tf_op jit(solution)/shard_map/ppermute | solution.py:21
  37.3 5.2 %collective-permute-start.14 = (f32[784,128]{1,0:T(8,128)S(1)}, f32[784,128]{1,0:T(8,128)S(1)}, u32[]{:S(2)}, u32[]{:S(2)}) collective-permute-start(f32[784,128]{1,0:T(8,128)S(1)} %sums.8), channel_id=1, source_target_pairs={{0,28},{4,0},{8,4},{12,8},{16,12},{20,16},{24,20},{28,24},{1,29},{... | collective-permute-start | bytes 1204232 | tf_op jit(solution)/shard_map/ppermute | solution.py:16
  42.5 0.0 collective-permute-done.8
  42.5 0.1 collective-permute-start.9
  42.6 1.7 %collective-permute-done.9.refs_5_.refs_3_ = f32[776,128]{1,0:T(8,128)S(1)} collective-permute-done((f32[776,128]{1,0:T(8,128)S(1)}, f32[776,128]{1,0:T(8,128)S(1)}, u32[]{:S(2)}, u32[]{:S(2)}) %collective-permute-start.9) | collective-permute-done | bytes 397344 | tf_op jit(solution)/shard_map/ppermute | solution.py:21
  44.3 2.4 %sums.10 = f32[784,128]{1,0:T(8,128)S(1)} custom-call(f32[792,128]{1,0:T(8,128)S(1)} %get-tuple-element.25.refs_4_.refs_0_, f32[792,128]{1,0:T(8,128)S(1)} %collective-permute-done.3.refs_5_.refs_1_, f32[776,128]{1,0:T(8,128)S(1)} %slice.14.refs_4_.refs_2_, f32[776,128]{1,0:T(8,128)S(1)} %collective-permute-done.9.refs_5_.refs_3_, ...), custom_call_target="tpu_custom_call" | custom-call | flops 1 | bytes 1 | tf_op jit(solution)/shard_map/sums/pallas_call | solution.py:197
  46.7 0.1 collective-permute-start.10
  46.8 1.3 %sums.9.base = f32[2,9,128,128]{3,2,1,0:T(8,128)S(1)} custom-call(f32[776,128]{1,0:T(8,128)S(1)} %slice.12.refs_2_.refs_0_, f32[776,128]{1,0:T(8,128)S(1)} %collective-permute-done.4.refs_3_.refs_1_, f32[776,128]{1,0:T(8,128)S(1)} %slice.13.refs_6_.refs_2_, f32[776,128]{1,0:T(8,128)S(1)} %collective-permute-done.7.refs_7_.refs_3_, ...), custom_call_target="tpu_custom_call" | custom-call | flops 1 | bytes 1 | tf_op jit(solution)/shard_map/sums/pallas_call | solution.py:197
  48.1 1.2 %collective-permute-done.14.to_above_next = f32[784,128]{1,0:T(8,128)S(1)} collective-permute-done((f32[784,128]{1,0:T(8,128)S(1)}, f32[784,128]{1,0:T(8,128)S(1)}, u32[]{:S(2)}, u32[]{:S(2)}) %collective-permute-start.14) | collective-permute-done | bytes 401440 | tf_op jit(solution)/shard_map/ppermute | solution.py:16
  49.3 0.0 collective-permute-done.13
  49.3 0.6 collective-permute-start.15
  49.9 1.4 %collective-permute-done.15.refs_3_ = f32[776,128]{1,0:T(8,128)S(1)} collective-permute-done((f32[776,128]{1,0:T(8,128)S(1)}, f32[776,128]{1,0:T(8,128)S(1)}, u32[]{:S(2)}, u32[]{:S(2)}) %collective-permute-start.15) | collective-permute-done | bytes 397344 | tf_op jit(solution)/shard_map/ppermute | solution.py:21
  51.3 1.9 %sums.11.from_below = f32[784,128]{1,0:T(8,128)S(1)} custom-call(f32[792,128]{1,0:T(8,128)S(1)} %collective-permute-done.5.refs_0_, f32[792,128]{1,0:T(8,128)S(1)} %collective-permute-done.12.refs_1_, f32[776,128]{1,0:T(8,128)S(1)} %slice.15.refs_2_, f32[776,128]{1,0:T(8,128)S(1)} %collective-permute-done.15.refs_3_), custom_call_target="tpu_custom_call" | custom-call | flops 1 | bytes 1 | tf_op jit(solution)/shard_map/sums/pallas_call | solution.py:197
  53.2 8.4 %collective-permute-done.10.to_below = f32[784,128]{1,0:T(8,128)S(1)} collective-permute-done((f32[784,128]{1,0:T(8,128)S(1)}, f32[784,128]{1,0:T(8,128)S(1)}, u32[]{:S(2)}, u32[]{:S(2)}) %collective-permute-start.10) | collective-permute-done | bytes 401440 | tf_op jit(solution)/shard_map/ppermute | solution.py:16
  61.6 1.1 %finish.1 = f32[2,9,128,128]{3,2,1,0:T(8,128)} custom-call(f32[2,9,128,128]{3,2,1,0:T(8,128)S(1)} %sums.9.base, f32[784,128]{1,0:T(8,128)S(1)} %collective-permute-done.10.to_below, f32[784,128]{1,0:T(8,128)S(1)} %collective-permute-done.11.to_above_own, f32[784,128]{1,0:T(8,128)S(1)} %sums.11.from_below, f32[784,128]{1,0:T(8,128)S(1)} %collective-permute-done.14.to_above_next), custom_call_target="tpu_custom_call" | custom-call | flops 1 | bytes 1 | tf_op jit(solution)/shard_map/finish/pallas_call | solution.py:252
  (4 shorter events, 0.1 us)
Async XLA Ops:
  0.0 1.3 %copy-start = (f32[2,9,128,128]{3,2,1,0:T(8,128)S(1)}, f32[2,9,128,128]{3,2,1,0:T(8,128)}, u32[]{:S(2)}) copy-start(f32[2,9,128,128]{3,2,1,0:T(8,128)} %param.3) | copy-start | bytes 3538948
  1.3 0.7 %copy-start.1 = (s32[2,9,9]{2,0,1:T(2,128)S(1)}, s32[2,9,9]{2,0,1:T(2,128)}, u32[]{:S(2)}) copy-start(s32[2,9,9]{2,0,1:T(2,128)} %param.5) | copy-start | bytes 1948
  2.0 0.7 %copy-start.2 = (s32[2,9]{1,0:T(2,128)S(1)}, s32[2,9]{1,0:T(2,128)}, u32[]{:S(2)}) copy-start(s32[2,9]{1,0:T(2,128)} %cols.1) | copy-start | bytes 220
  4.3 5.1 %collective-permute-start.1 = (f32[792,128]{1,0:T(8,128)S(1)}, f32[792,128]{1,0:T(8,128)S(1)}, u32[]{:S(2)}, u32[]{:S(2)}) collective-permute-start(f32[792,128]{1,0:T(8,128)S(1)} %get-tuple-element.17.refs_0_), channel_id=1, source_target_pairs={{0,1},{1,0},{2,3},{3,2},{4,5},{5,4},{6,7},{7,6},{8,9},{9,8},{10,11... | collective-permute-start | bytes 1216520 | tf_op jit(solution)/shard_map/ppermute | solution.py:21
  4.8 4.6 %collective-permute-start.2 = (f32[792,128]{1,0:T(8,128)S(1)}, f32[792,128]{1,0:T(8,128)S(1)}, u32[]{:S(2)}, u32[]{:S(2)}) collective-permute-start(f32[792,128]{1,0:T(8,128)S(1)} %get-tuple-element.23.refs_2_.refs_4_), channel_id=1, source_target_pairs={{0,1},{1,0},{2,3},{3,2},{4,5},{5,4},{6,7},{7,6},{8,9},{9,8},{10,11... | collective-permute-start | bytes 1216520 | tf_op jit(solution)/shard_map/ppermute | solution.py:21
  4.9 4.5 %collective-permute-start.3 = (f32[792,128]{1,0:T(8,128)S(1)}, f32[792,128]{1,0:T(8,128)S(1)}, u32[]{:S(2)}, u32[]{:S(2)}) collective-permute-start(f32[792,128]{1,0:T(8,128)S(1)} %get-tuple-element.25.refs_4_.refs_0_), channel_id=1, source_target_pairs={{0,1},{1,0},{2,3},{3,2},{4,5},{5,4},{6,7},{7,6},{8,9},{9,8},{10,11... | collective-permute-start | bytes 1216520 | tf_op jit(solution)/shard_map/ppermute | solution.py:21
  5.3 12.8 %collective-permute-start = (f32[792,128]{1,0:T(8,128)S(1)}, f32[792,128]{1,0:T(8,128)S(1)}, u32[]{:S(2)}, u32[]{:S(2)}) collective-permute-start(f32[792,128]{1,0:T(8,128)S(1)} %get-tuple-element.17.refs_0_), channel_id=1, source_target_pairs={{0,2},{1,3},{2,0},{3,1},{4,6},{5,7},{6,4},{7,5},{8,10},{9,11},{10,... | collective-permute-start | bytes 1216520 | tf_op jit(solution)/shard_map/ppermute | solution.py:21
  7.9 14.3 %collective-permute-start.5 = (f32[792,128]{1,0:T(8,128)S(1)}, f32[792,128]{1,0:T(8,128)S(1)}, u32[]{:S(2)}, u32[]{:S(2)}) collective-permute-start(f32[792,128]{1,0:T(8,128)S(1)} %get-tuple-element.25.refs_4_.refs_0_), channel_id=1, source_target_pairs={{0,4},{4,8},{8,12},{12,16},{16,20},{20,24},{24,28},{28,0},{1,5},{5... | collective-permute-start | bytes 1216520 | tf_op jit(solution)/shard_map/ppermute | solution.py:16
  12.3 16.9 %collective-permute-start.6 = (f32[792,128]{1,0:T(8,128)S(1)}, f32[792,128]{1,0:T(8,128)S(1)}, u32[]{:S(2)}, u32[]{:S(2)}) collective-permute-start(f32[792,128]{1,0:T(8,128)S(1)} %get-tuple-element.23.refs_2_.refs_4_), channel_id=1, source_target_pairs={{0,2},{1,3},{2,0},{3,1},{4,6},{5,7},{6,4},{7,5},{8,10},{9,11},{10,... | collective-permute-start | bytes 1216520 | tf_op jit(solution)/shard_map/ppermute | solution.py:21
  18.2 4.0 %collective-permute-start.4 = (f32[776,128]{1,0:T(8,128)S(1)}, f32[776,128]{1,0:T(8,128)S(1)}, u32[]{:S(2)}, u32[]{:S(2)}) collective-permute-start(f32[776,128]{1,0:T(8,128)S(1)} %slice.12.refs_2_.refs_0_), channel_id=1, source_target_pairs={{0,1},{1,0},{2,3},{3,2},{4,5},{5,4},{6,7},{7,6},{8,9},{9,8},{10,11... | collective-permute-start | bytes 1191944 | tf_op jit(solution)/shard_map/ppermute | solution.py:21
  22.2 11.6 %collective-permute-start.12 = (f32[792,128]{1,0:T(8,128)S(1)}, f32[792,128]{1,0:T(8,128)S(1)}, u32[]{:S(2)}, u32[]{:S(2)}) collective-permute-start(f32[792,128]{1,0:T(8,128)S(1)} %collective-permute-done.5.refs_0_), channel_id=1, source_target_pairs={{0,1},{1,0},{2,3},{3,2},{4,5},{5,4},{6,7},{7,6},{8,9},{9,8},{10,11... | collective-permute-start | bytes 1216520 | tf_op jit(solution)/shard_map/ppermute | solution.py:21
  24.9 11.5 %collective-permute-start.11 = (f32[784,128]{1,0:T(8,128)S(1)}, f32[784,128]{1,0:T(8,128)S(1)}, u32[]{:S(2)}, u32[]{:S(2)}) collective-permute-start(f32[784,128]{1,0:T(8,128)S(1)} %sums.7), channel_id=1, source_target_pairs={{0,28},{4,0},{8,4},{12,8},{16,12},{20,16},{24,20},{28,24},{1,29},{... | collective-permute-start | bytes 1204232 | tf_op jit(solution)/shard_map/ppermute | solution.py:16
  27.7 14.7 %collective-permute-start.8 = (f32[792,128]{1,0:T(8,128)S(1)}, f32[792,128]{1,0:T(8,128)S(1)}, u32[]{:S(2)}, u32[]{:S(2)}) collective-permute-start(f32[792,128]{1,0:T(8,128)S(1)} %get-tuple-element.25.refs_4_.refs_0_), channel_id=1, source_target_pairs={{0,2},{1,3},{2,0},{3,1},{4,6},{5,7},{6,4},{7,5},{8,10},{9,11},{10,... | collective-permute-start | bytes 1216520 | tf_op jit(solution)/shard_map/ppermute | solution.py:21
  29.3 1.8 %collective-permute-start.7 = (f32[776,128]{1,0:T(8,128)S(1)}, f32[776,128]{1,0:T(8,128)S(1)}, u32[]{:S(2)}, u32[]{:S(2)}) collective-permute-start(f32[776,128]{1,0:T(8,128)S(1)} %slice.13.refs_6_.refs_2_), channel_id=1, source_target_pairs={{0,1},{1,0},{2,3},{3,2},{4,5},{5,4},{6,7},{7,6},{8,9},{9,8},{10,11... | collective-permute-start | bytes 1191944 | tf_op jit(solution)/shard_map/ppermute | solution.py:21
  36.4 12.9 %collective-permute-start.13 = (f32[792,128]{1,0:T(8,128)S(1)}, f32[792,128]{1,0:T(8,128)S(1)}, u32[]{:S(2)}, u32[]{:S(2)}) collective-permute-start(f32[792,128]{1,0:T(8,128)S(1)} %collective-permute-done.5.refs_0_), channel_id=1, source_target_pairs={{0,2},{1,3},{2,0},{3,1},{4,6},{5,7},{6,4},{7,5},{8,10},{9,11},{10,... | collective-permute-start | bytes 1216520 | tf_op jit(solution)/shard_map/ppermute | solution.py:21
  37.3 12.0 %collective-permute-start.14 = (f32[784,128]{1,0:T(8,128)S(1)}, f32[784,128]{1,0:T(8,128)S(1)}, u32[]{:S(2)}, u32[]{:S(2)}) collective-permute-start(f32[784,128]{1,0:T(8,128)S(1)} %sums.8), channel_id=1, source_target_pairs={{0,28},{4,0},{8,4},{12,8},{16,12},{20,16},{24,20},{28,24},{1,29},{... | collective-permute-start | bytes 1204232 | tf_op jit(solution)/shard_map/ppermute | solution.py:16
  42.5 1.8 %collective-permute-start.9 = (f32[776,128]{1,0:T(8,128)S(1)}, f32[776,128]{1,0:T(8,128)S(1)}, u32[]{:S(2)}, u32[]{:S(2)}) collective-permute-start(f32[776,128]{1,0:T(8,128)S(1)} %slice.14.refs_4_.refs_2_), channel_id=1, source_target_pairs={{0,1},{1,0},{2,3},{3,2},{4,5},{5,4},{6,7},{7,6},{8,9},{9,8},{10,11... | collective-permute-start | bytes 1191944 | tf_op jit(solution)/shard_map/ppermute | solution.py:21
  46.7 14.9 %collective-permute-start.10 = (f32[784,128]{1,0:T(8,128)S(1)}, f32[784,128]{1,0:T(8,128)S(1)}, u32[]{:S(2)}, u32[]{:S(2)}) collective-permute-start(f32[784,128]{1,0:T(8,128)S(1)} %sums.10), channel_id=1, source_target_pairs={{0,4},{4,8},{8,12},{12,16},{16,20},{20,24},{24,28},{28,0},{1,5},{5... | collective-permute-start | bytes 1204232 | tf_op jit(solution)/shard_map/ppermute | solution.py:16
  49.3 1.9 %collective-permute-start.15 = (f32[776,128]{1,0:T(8,128)S(1)}, f32[776,128]{1,0:T(8,128)S(1)}, u32[]{:S(2)}, u32[]{:S(2)}) collective-permute-start(f32[776,128]{1,0:T(8,128)S(1)} %slice.15.refs_2_), channel_id=1, source_target_pairs={{0,1},{1,0},{2,3},{3,2},{4,5},{5,4},{6,7},{7,6},{8,9},{9,8},{10,11... | collective-permute-start | bytes 1191944 | tf_op jit(solution)/shard_map/ppermute | solution.py:21
where the time goes:
time: 62.6 us; the launch traced here: 62.7 us
  waiting for transfers between devices  26.3 us (42%)
  starting transfers between devices  16.8 us (27%)
  Pallas kernels  16.7 us (27%)
  local copies, waits for them, and re-layouts  2.75 us (4%)
    ppermute x4, waiting for transfers between devices, shifted(): return lax.ppermute(value, 'blk', pairs)  16.1 us
    pallas_call x6, Pallas kernels, sums(): pl.pallas_call(functools.partial(sums_kernel, dims, plan), out_shape=jax....  14 us
    ppermute x12, waiting for transfers between devices, swapped(): lax.ppermute(value, 'inner', [(i, i ^ distance) for i in range(count)])  10.1 us
    ppermute x4, starting transfers between devices, shifted(): return lax.ppermute(value, 'blk', pairs)  9.61 us
    ppermute x12, starting transfers between devices, swapped(): lax.ppermute(value, 'inner', [(i, i ^ distance) for i in range(count)])  7.23 us
    unnamed x6, local copies, waits for them, and re-layouts  2.65 us
    pallas_call x1, Pallas kernels, shards(): pl.pallas_call(functools.partial(pack_kernel, (local_rows, slots, side, s...  1.64 us
  transfers between devices with their start and end apart: 16, of which 8 were waited for; matrix products, arithmetic and copies ran while one was open for 0% of the time, Pallas kernels for 22%

commit v1 on v0

--- a/solution.py
+++ b/solution.py
@@ -164,7 +164,7 @@
     strip_rows = local_rows * parts
     meta_rows = local_rows * per + -(local_rows * per) % 8
     used_rows = local_rows * per * side + meta_rows
-    payload_rows = used_rows + 16
+    payload_rows = used_rows + 24
     in_hbm = pl.BlockSpec(memory_space=pltpu.HBM)
     scalars = pl.BlockSpec(memory_space=pltpu.SMEM)
     vectors = pl.BlockSpec(memory_space=pltpu.VMEM)
@@ -180,7 +180,7 @@
             pltpu.SemaphoreType.DMA((3, local_rows)),
             pltpu.SemaphoreType.DMA((2,)),
         ],
-        compiler_params=pltpu.CompilerParams(vmem_limit_bytes=48 << 20),
+        compiler_params=pltpu.CompilerParams(vmem_limit_bytes=52 << 20),
         name="pack",
     )(
         density.reshape(-1, side),
@@ -189,7 +189,7 @@
         lax.axis_index("inner").reshape(1),
     )
 
-    spare = 16
+    spare = 24
 
     def sums(groups, a_at, plan, first, width, offset=0, base=()):
         held = len(groups[0])
@@ -238,8 +238,8 @@
     to_above_next = shifted(above_next, -1)
 
     belows = halves(below)
-    far_below = across(below, [above_next, to_above_own, *belows])
-    far_uppers = spread(tied(far_upper, above_next))
+    far_below = across(below, [above_next, *belows])
+    far_uppers = spread(tied(far_upper, above_next, to_above_own))
     to_next = sums([uppers + far_uppers, all_middles], 0, ((1, per),), 0, per)
     to_below = shifted(to_next, 1)
     if far_lowers:

time: 62.6 us -> 56.8 us (0.907)
  waiting for transfers between devices: 26.3 us -> 23.1 us
  local copies, waits for them, and re-layouts: 2.75 us -> 1.48 us
  Pallas kernels: 16.7 us -> 15.8 us
    ppermute x4, waiting for transfers between devices: 16.1 us -> 12.1 us  [shifted(): return lax.ppermute(value, 'blk', pairs)]
    ppermute x12, starting transfers between devices: 7.23 us -> 5.46 us  [swapped(): lax.ppermute(value, 'inner', [(i, i ^ distance) for i in range(count)])]
    unnamed x6 -> x4, local copies, waits for them, and re-layouts: 2.65 us -> 1.38 us
    ppermute x4, starting transfers between devices: 9.61 us -> 10.8 us  [shifted(): return lax.ppermute(value, 'blk', pairs)]
    ppermute x12, waiting for transfers between devices: 10.1 us -> 11 us  [swapped(): lax.ppermute(value, 'inner', [(i, i ^ distance) for i in range(count)])]
    pallas_call x6, Pallas kernels: 14 us -> 13.3 us  [sums(): pl.pallas_call(functools.partial(sums_kernel, dims, plan), out_shape=jax....]
  transfers between devices with their start and end apart: 16 -> 16, of which waited for: 8 -> 7; matrix products, arithmetic and copies ran while one was open for 0% -> 0% of each run, Pallas kernels for 22% -> 23%
where the time goes in v1:
time: 56.8 us; the launch traced here: 56.7 us
  waiting for transfers between devices  23.1 us (41%)
  starting transfers between devices  16.2 us (29%)
  Pallas kernels  15.8 us (28%)
  local copies, waits for them, and re-layouts  1.48 us (3%)
    pallas_call x6, Pallas kernels, sums(): pl.pallas_call(functools.partial(sums_kernel, dims, plan), out_shape=jax....  13.3 us
    ppermute x4, waiting for transfers between devices, shifted(): return lax.ppermute(value, 'blk', pairs)  12.1 us
    ppermute x12, waiting for transfers between devices, swapped(): lax.ppermute(value, 'inner', [(i, i ^ distance) for i in range(count)])  11 us
    ppermute x4, starting transfers between devices, shifted(): return lax.ppermute(value, 'blk', pairs)  10.8 us
    ppermute x12, starting transfers between devices, swapped(): lax.ppermute(value, 'inner', [(i, i ^ distance) for i in range(count)])  5.46 us
    pallas_call x1, Pallas kernels, shards(): pl.pallas_call(functools.partial(pack_kernel, (local_rows, slots, side, s...  1.41 us
    unnamed x4, local copies, waits for them, and re-layouts  1.38 us
  transfers between devices with their start and end apart: 16, of which 7 were waited for; matrix products, arithmetic and copies ran while one was open for 0% of the time, Pallas kernels for 23%

profile of v1, /device:TPU:0, one launch (start us, length us, event | category | flops | bytes accessed | tf_op | source)
XLA Modules:
  0.0 56.7 jit_solution(5175882544373230428)
XLA Ops:
  0.0 0.0 copy-start
  0.0 0.7 %copy-done = s32[2,9,9]{2,0,1:T(2,128)S(1)} copy-done((s32[2,9,9]{2,0,1:T(2,128)S(1)}, s32[2,9,9]{2,0,1:T(2,128)}, u32[]{:S(2)}) %copy-start) | copy-done | bytes 672
  0.7 0.0 copy-start.1
  0.7 0.7 %copy-done.1 = s32[2,9]{1,0:T(2,128)S(1)} copy-done((s32[2,9]{1,0:T(2,128)S(1)}, s32[2,9]{1,0:T(2,128)}, u32[]{:S(2)}) %copy-start.1) | copy-done | bytes 96
  1.4 1.4 %pack.1 = (f32[800,128]{1,0:T(8,128)S(1)}, f32[800,128]{1,0:T(8,128)S(1)}, f32[800,128]{1,0:T(8,128)S(1)}) custom-call(f32[2304,128]{1,0:T(8,128)} %bitcast.4, s32[9,2,9]{2,1,0:T(2,128)S(1)} %bitcast.3, s32[2,9]{1,0:T(2,128)S(1)} %copy-done.1, s32[1]{0:T(128)} %bitcast.2.inner), custom_call_target="tpu_custom_call" | custom-call | tf_op jit(solution)/shard_map/pack/pallas_call | solution.py:172
  2.8 0.5 collective-permute-start.1
  3.3 0.1 collective-permute-start.2
  3.4 0.4 collective-permute-start.3
  3.8 2.6 %collective-permute-start = (f32[800,128]{1,0:T(8,128)S(1)}, f32[800,128]{1,0:T(8,128)S(1)}, u32[]{:S(2)}, u32[]{:S(2)}) collective-permute-start(f32[800,128]{1,0:T(8,128)S(1)} %get-tuple-element.17.refs_0_), channel_id=1, source_target_pairs={{0,2},{1,3},{2,0},{3,1},{4,6},{5,7},{6,4},{7,5},{8,10},{9,11},{10,... | collective-permute-start | bytes 1228808 | tf_op jit(solution)/shard_map/ppermute | solution.py:21
  6.4 1.5 %collective-permute-start.5 = (f32[800,128]{1,0:T(8,128)S(1)}, f32[800,128]{1,0:T(8,128)S(1)}, u32[]{:S(2)}, u32[]{:S(2)}) collective-permute-start(f32[800,128]{1,0:T(8,128)S(1)} %get-tuple-element.25.refs_4_.refs_0_), channel_id=1, source_target_pairs={{0,4},{4,8},{8,12},{12,16},{16,20},{20,24},{24,28},{28,0},{1,5},{5... | collective-permute-start | bytes 1228808 | tf_op jit(solution)/shard_map/ppermute | solution.py:16
  7.9 0.0 collective-permute-done.1.refs_1_
  7.9 0.0 collective-permute-done.2.refs_3_.refs_5_
  7.9 0.0 collective-permute-done.3.refs_5_.refs_1_
  7.9 2.1 %sums.6.refs_6_ = f32[2,9,128,128]{3,2,1,0:T(8,128)S(1)} custom-call(f32[800,128]{1,0:T(8,128)S(1)} %get-tuple-element.17.refs_0_, f32[800,128]{1,0:T(8,128)S(1)} %collective-permute-done.1.refs_1_, f32[800,128]{1,0:T(8,128)S(1)} %get-tuple-element.23.refs_2_.refs_4_, f32[800,128]{1,0:T(8,128)S(1)} %collective-permute-done.2.refs_3_.refs_5_, ...), custom_call_target="tpu_custom_call" | custom-call | flops 1 | bytes 1 | tf_op jit(solution)/shard_map/sums/pallas_call | solution.py:197
  10.0 0.8 %collective-permute-start.6 = (f32[800,128]{1,0:T(8,128)S(1)}, f32[800,128]{1,0:T(8,128)S(1)}, u32[]{:S(2)}, u32[]{:S(2)}) collective-permute-start(f32[800,128]{1,0:T(8,128)S(1)} %get-tuple-element.23.refs_2_.refs_4_), channel_id=1, source_target_pairs={{0,2},{1,3},{2,0},{3,1},{4,6},{5,7},{6,4},{7,5},{8,10},{9,11},{10,... | collective-permute-start | bytes 1228808 | tf_op jit(solution)/shard_map/ppermute | solution.py:21
  10.9 5.9 %collective-permute-done = f32[800,128]{1,0:T(8,128)S(1)} collective-permute-done((f32[800,128]{1,0:T(8,128)S(1)}, f32[800,128]{1,0:T(8,128)S(1)}, u32[]{:S(2)}, u32[]{:S(2)}) %collective-permute-start) | collective-permute-done | bytes 409632 | tf_op jit(solution)/shard_map/ppermute | solution.py:21
  16.7 0.1 collective-permute-start.4
  16.8 3.9 %collective-permute-done.5.refs_0_ = f32[800,128]{1,0:T(8,128)S(1)} collective-permute-done((f32[800,128]{1,0:T(8,128)S(1)}, f32[800,128]{1,0:T(8,128)S(1)}, u32[]{:S(2)}, u32[]{:S(2)}) %collective-permute-start.5) | collective-permute-done | bytes 409632 | tf_op jit(solution)/shard_map/ppermute | solution.py:16
  20.7 0.0 collective-permute-start.12
  20.7 0.0 collective-permute-done.4.refs_3_.refs_1_
  20.7 2.2 %sums.7 = f32[792,128]{1,0:T(8,128)S(1)} custom-call(f32[800,128]{1,0:T(8,128)S(1)} %get-tuple-element.17.refs_0_, f32[800,128]{1,0:T(8,128)S(1)} %collective-permute-done.1.refs_1_, f32[776,128]{1,0:T(8,128)S(1)} %slice.12.refs_2_.refs_0_, f32[776,128]{1,0:T(8,128)S(1)} %collective-permute-done.4.refs_3_.refs_1_), custom_call_target="tpu_custom_call" | custom-call | flops 1 | bytes 1 | tf_op jit(solution)/shard_map/sums/pallas_call | solution.py:197
  22.9 0.6 %collective-permute-start.8 = (f32[800,128]{1,0:T(8,128)S(1)}, f32[800,128]{1,0:T(8,128)S(1)}, u32[]{:S(2)}, u32[]{:S(2)}) collective-permute-start(f32[800,128]{1,0:T(8,128)S(1)} %get-tuple-element.25.refs_4_.refs_0_), channel_id=1, source_target_pairs={{0,2},{1,3},{2,0},{3,1},{4,6},{5,7},{6,4},{7,5},{8,10},{9,11},{10,... | collective-permute-start | bytes 1228808 | tf_op jit(solution)/shard_map/ppermute | solution.py:21
  23.5 4.5 %collective-permute-start.9 = (f32[792,128]{1,0:T(8,128)S(1)}, f32[792,128]{1,0:T(8,128)S(1)}, u32[]{:S(2)}, u32[]{:S(2)}) collective-permute-start(f32[792,128]{1,0:T(8,128)S(1)} %sums.7), channel_id=1, source_target_pairs={{0,28},{4,0},{8,4},{12,8},{16,12},{20,16},{24,20},{28,24},{1,29},{... | collective-permute-start | bytes 1216520 | tf_op jit(solution)/shard_map/ppermute | solution.py:16
  28.1 0.0 collective-permute-done.6
  28.1 0.1 collective-permute-start.7
  28.2 1.7 %collective-permute-done.7.refs_7_.refs_3_ = f32[776,128]{1,0:T(8,128)S(1)} collective-permute-done((f32[776,128]{1,0:T(8,128)S(1)}, f32[776,128]{1,0:T(8,128)S(1)}, u32[]{:S(2)}, u32[]{:S(2)}) %collective-permute-start.7) | collective-permute-done | bytes 397344 | tf_op jit(solution)/shard_map/ppermute | solution.py:21
  29.9 2.2 %sums.8 = f32[792,128]{1,0:T(8,128)S(1)} custom-call(f32[800,128]{1,0:T(8,128)S(1)} %get-tuple-element.17.refs_0_, f32[800,128]{1,0:T(8,128)S(1)} %collective-permute-done.1.refs_1_, f32[776,128]{1,0:T(8,128)S(1)} %slice.12.refs_2_.refs_0_, f32[776,128]{1,0:T(8,128)S(1)} %collective-permute-done.4.refs_3_.refs_1_, ...), custom_call_target="tpu_custom_call" | custom-call | flops 1 | bytes 1 | tf_op jit(solution)/shard_map/sums/pallas_call | solution.py:197
  32.1 0.0 collective-permute-done.12.refs_1_
  32.1 0.1 collective-permute-start.13
  32.2 4.6 %collective-permute-start.14 = (f32[792,128]{1,0:T(8,128)S(1)}, f32[792,128]{1,0:T(8,128)S(1)}, u32[]{:S(2)}, u32[]{:S(2)}) collective-permute-start(f32[792,128]{1,0:T(8,128)S(1)} %sums.8), channel_id=1, source_target_pairs={{0,28},{4,0},{8,4},{12,8},{16,12},{20,16},{24,20},{28,24},{1,29},{... | collective-permute-start | bytes 1216520 | tf_op jit(solution)/shard_map/ppermute | solution.py:16
  36.9 0.0 collective-permute-done.9.to_above_own
  36.9 0.0 collective-permute-done.8
  36.9 0.1 collective-permute-start.10
  37.0 1.7 %collective-permute-done.10.refs_5_.refs_3_ = f32[776,128]{1,0:T(8,128)S(1)} collective-permute-done((f32[776,128]{1,0:T(8,128)S(1)}, f32[776,128]{1,0:T(8,128)S(1)}, u32[]{:S(2)}, u32[]{:S(2)}) %collective-permute-start.10) | collective-permute-done | bytes 397344 | tf_op jit(solution)/shard_map/ppermute | solution.py:21
  38.7 2.2 %sums.10 = f32[792,128]{1,0:T(8,128)S(1)} custom-call(f32[800,128]{1,0:T(8,128)S(1)} %get-tuple-element.25.refs_4_.refs_0_, f32[800,128]{1,0:T(8,128)S(1)} %collective-permute-done.3.refs_5_.refs_1_, f32[776,128]{1,0:T(8,128)S(1)} %slice.14.refs_4_.refs_2_, f32[776,128]{1,0:T(8,128)S(1)} %collective-permute-done.10.refs_5_.refs_3_, ...), custom_call_target="tpu_custom_call" | custom-call | flops 1 | bytes 1 | tf_op jit(solution)/shard_map/sums/pallas_call | solution.py:197
  40.9 0.1 collective-permute-start.11
  41.0 1.7 %sums.9.base = f32[2,9,128,128]{3,2,1,0:T(8,128)S(1)} custom-call(f32[776,128]{1,0:T(8,128)S(1)} %slice.12.refs_2_.refs_0_, f32[776,128]{1,0:T(8,128)S(1)} %collective-permute-done.4.refs_3_.refs_1_, f32[776,128]{1,0:T(8,128)S(1)} %slice.13.refs_6_.refs_2_, f32[776,128]{1,0:T(8,128)S(1)} %collective-permute-done.7.refs_7_.refs_3_, ...), custom_call_target="tpu_custom_call" | custom-call | flops 1 | bytes 1 | tf_op jit(solution)/shard_map/sums/pallas_call | solution.py:197
  42.7 2.1 %collective-permute-done.14.to_above_next = f32[792,128]{1,0:T(8,128)S(1)} collective-permute-done((f32[792,128]{1,0:T(8,128)S(1)}, f32[792,128]{1,0:T(8,128)S(1)}, u32[]{:S(2)}, u32[]{:S(2)}) %collective-permute-start.14) | collective-permute-done | bytes 405536 | tf_op jit(solution)/shard_map/ppermute | solution.py:16
  44.7 0.0 collective-permute-done.13
  44.8 0.1 collective-permute-start.15
  44.9 1.7 %collective-permute-done.15.refs_3_ = f32[776,128]{1,0:T(8,128)S(1)} collective-permute-done((f32[776,128]{1,0:T(8,128)S(1)}, f32[776,128]{1,0:T(8,128)S(1)}, u32[]{:S(2)}, u32[]{:S(2)}) %collective-permute-start.15) | collective-permute-done | bytes 397344 | tf_op jit(solution)/shard_map/ppermute | solution.py:21
  46.6 3.0 %sums.11.from_below = f32[792,128]{1,0:T(8,128)S(1)} custom-call(f32[800,128]{1,0:T(8,128)S(1)} %collective-permute-done.5.refs_0_, f32[800,128]{1,0:T(8,128)S(1)} %collective-permute-done.12.refs_1_, f32[776,128]{1,0:T(8,128)S(1)} %slice.15.refs_2_, f32[776,128]{1,0:T(8,128)S(1)} %collective-permute-done.15.refs_3_), custom_call_target="tpu_custom_call" | custom-call | flops 1 | bytes 1 | tf_op jit(solution)/shard_map/sums/pallas_call | solution.py:197
  49.6 6.0 %collective-permute-done.11.to_below = f32[792,128]{1,0:T(8,128)S(1)} collective-permute-done((f32[792,128]{1,0:T(8,128)S(1)}, f32[792,128]{1,0:T(8,128)S(1)}, u32[]{:S(2)}, u32[]{:S(2)}) %collective-permute-start.11) | collective-permute-done | bytes 405536 | tf_op jit(solution)/shard_map/ppermute | solution.py:16
  55.6 1.1 %finish.1 = f32[2,9,128,128]{3,2,1,0:T(8,128)} custom-call(f32[2,9,128,128]{3,2,1,0:T(8,128)S(1)} %sums.9.base, f32[792,128]{1,0:T(8,128)S(1)} %collective-permute-done.11.to_below, f32[792,128]{1,0:T(8,128)S(1)} %collective-permute-done.9.to_above_own, f32[792,128]{1,0:T(8,128)S(1)} %sums.11.from_below, f32[792,128]{1,0:T(8,128)S(1)} %collective-permute-done.14.to_above_next), custom_call_target="tpu_custom_call" | custom-call | flops 1 | bytes 1 | tf_op jit(solution)/shard_map/finish/pallas_call | solution.py:252
  (4 shorter events, 0.1 us)
Async XLA Ops:
  0.0 0.7 %copy-start = (s32[2,9,9]{2,0,1:T(2,128)S(1)}, s32[2,9,9]{2,0,1:T(2,128)}, u32[]{:S(2)}) copy-start(s32[2,9,9]{2,0,1:T(2,128)} %param.5) | copy-start | bytes 1948
  0.7 0.7 %copy-start.1 = (s32[2,9]{1,0:T(2,128)S(1)}, s32[2,9]{1,0:T(2,128)}, u32[]{:S(2)}) copy-start(s32[2,9]{1,0:T(2,128)} %cols.1) | copy-start | bytes 220
  2.8 5.1 %collective-permute-start.1 = (f32[800,128]{1,0:T(8,128)S(1)}, f32[800,128]{1,0:T(8,128)S(1)}, u32[]{:S(2)}, u32[]{:S(2)}) collective-permute-start(f32[800,128]{1,0:T(8,128)S(1)} %get-tuple-element.17.refs_0_), channel_id=1, source_target_pairs={{0,1},{1,0},{2,3},{3,2},{4,5},{5,4},{6,7},{7,6},{8,9},{9,8},{10,11... | collective-permute-start | bytes 1228808 | tf_op jit(solution)/shard_map/ppermute | solution.py:21
  3.3 4.6 %collective-permute-start.2 = (f32[800,128]{1,0:T(8,128)S(1)}, f32[800,128]{1,0:T(8,128)S(1)}, u32[]{:S(2)}, u32[]{:S(2)}) collective-permute-start(f32[800,128]{1,0:T(8,128)S(1)} %get-tuple-element.23.refs_2_.refs_4_), channel_id=1, source_target_pairs={{0,1},{1,0},{2,3},{3,2},{4,5},{5,4},{6,7},{7,6},{8,9},{9,8},{10,11... | collective-permute-start | bytes 1228808 | tf_op jit(solution)/shard_map/ppermute | solution.py:21
  3.4 4.5 %collective-permute-start.3 = (f32[800,128]{1,0:T(8,128)S(1)}, f32[800,128]{1,0:T(8,128)S(1)}, u32[]{:S(2)}, u32[]{:S(2)}) collective-permute-start(f32[800,128]{1,0:T(8,128)S(1)} %get-tuple-element.25.refs_4_.refs_0_), channel_id=1, source_target_pairs={{0,1},{1,0},{2,3},{3,2},{4,5},{5,4},{6,7},{7,6},{8,9},{9,8},{10,11... | collective-permute-start | bytes 1228808 | tf_op jit(solution)/shard_map/ppermute | solution.py:21
  3.8 12.9 %collective-permute-start = (f32[800,128]{1,0:T(8,128)S(1)}, f32[800,128]{1,0:T(8,128)S(1)}, u32[]{:S(2)}, u32[]{:S(2)}) collective-permute-start(f32[800,128]{1,0:T(8,128)S(1)} %get-tuple-element.17.refs_0_), channel_id=1, source_target_pairs={{0,2},{1,3},{2,0},{3,1},{4,6},{5,7},{6,4},{7,5},{8,10},{9,11},{10,... | collective-permute-start | bytes 1228808 | tf_op jit(solution)/shard_map/ppermute | solution.py:21
  6.4 14.4 %collective-permute-start.5 = (f32[800,128]{1,0:T(8,128)S(1)}, f32[800,128]{1,0:T(8,128)S(1)}, u32[]{:S(2)}, u32[]{:S(2)}) collective-permute-start(f32[800,128]{1,0:T(8,128)S(1)} %get-tuple-element.25.refs_4_.refs_0_), channel_id=1, source_target_pairs={{0,4},{4,8},{8,12},{12,16},{16,20},{20,24},{24,28},{28,0},{1,5},{5... | collective-permute-start | bytes 1228808 | tf_op jit(solution)/shard_map/ppermute | solution.py:16
  10.0 18.1 %collective-permute-start.6 = (f32[800,128]{1,0:T(8,128)S(1)}, f32[800,128]{1,0:T(8,128)S(1)}, u32[]{:S(2)}, u32[]{:S(2)}) collective-permute-start(f32[800,128]{1,0:T(8,128)S(1)} %get-tuple-element.23.refs_2_.refs_4_), channel_id=1, source_target_pairs={{0,2},{1,3},{2,0},{3,1},{4,6},{5,7},{6,4},{7,5},{8,10},{9,11},{10,... | collective-permute-start | bytes 1228808 | tf_op jit(solution)/shard_map/ppermute | solution.py:21
  16.7 4.0 %collective-permute-start.4 = (f32[776,128]{1,0:T(8,128)S(1)}, f32[776,128]{1,0:T(8,128)S(1)}, u32[]{:S(2)}, u32[]{:S(2)}) collective-permute-start(f32[776,128]{1,0:T(8,128)S(1)} %slice.12.refs_2_.refs_0_), channel_id=1, source_target_pairs={{0,1},{1,0},{2,3},{3,2},{4,5},{5,4},{6,7},{7,6},{8,9},{9,8},{10,11... | collective-permute-start | bytes 1191944 | tf_op jit(solution)/shard_map/ppermute | solution.py:21
  20.7 11.4 %collective-permute-start.12 = (f32[800,128]{1,0:T(8,128)S(1)}, f32[800,128]{1,0:T(8,128)S(1)}, u32[]{:S(2)}, u32[]{:S(2)}) collective-permute-start(f32[800,128]{1,0:T(8,128)S(1)} %collective-permute-done.5.refs_0_), channel_id=1, source_target_pairs={{0,1},{1,0},{2,3},{3,2},{4,5},{5,4},{6,7},{7,6},{8,9},{9,8},{10,11... | collective-permute-start | bytes 1228808 | tf_op jit(solution)/shard_map/ppermute | solution.py:21
  22.9 13.9 %collective-permute-start.8 = (f32[800,128]{1,0:T(8,128)S(1)}, f32[800,128]{1,0:T(8,128)S(1)}, u32[]{:S(2)}, u32[]{:S(2)}) collective-permute-start(f32[800,128]{1,0:T(8,128)S(1)} %get-tuple-element.25.refs_4_.refs_0_), channel_id=1, source_target_pairs={{0,2},{1,3},{2,0},{3,1},{4,6},{5,7},{6,4},{7,5},{8,10},{9,11},{10,... | collective-permute-start | bytes 1228808 | tf_op jit(solution)/shard_map/ppermute | solution.py:21
  23.5 13.3 %collective-permute-start.9 = (f32[792,128]{1,0:T(8,128)S(1)}, f32[792,128]{1,0:T(8,128)S(1)}, u32[]{:S(2)}, u32[]{:S(2)}) collective-permute-start(f32[792,128]{1,0:T(8,128)S(1)} %sums.7), channel_id=1, source_target_pairs={{0,28},{4,0},{8,4},{12,8},{16,12},{20,16},{24,20},{28,24},{1,29},{... | collective-permute-start | bytes 1216520 | tf_op jit(solution)/shard_map/ppermute | solution.py:16
  28.1 1.8 %collective-permute-start.7 = (f32[776,128]{1,0:T(8,128)S(1)}, f32[776,128]{1,0:T(8,128)S(1)}, u32[]{:S(2)}, u32[]{:S(2)}) collective-permute-start(f32[776,128]{1,0:T(8,128)S(1)} %slice.13.refs_6_.refs_2_), channel_id=1, source_target_pairs={{0,1},{1,0},{2,3},{3,2},{4,5},{5,4},{6,7},{7,6},{8,9},{9,8},{10,11... | collective-permute-start | bytes 1191944 | tf_op jit(solution)/shard_map/ppermute | solution.py:21
  32.1 12.6 %collective-permute-start.13 = (f32[800,128]{1,0:T(8,128)S(1)}, f32[800,128]{1,0:T(8,128)S(1)}, u32[]{:S(2)}, u32[]{:S(2)}) collective-permute-start(f32[800,128]{1,0:T(8,128)S(1)} %collective-permute-done.5.refs_0_), channel_id=1, source_target_pairs={{0,2},{1,3},{2,0},{3,1},{4,6},{5,7},{6,4},{7,5},{8,10},{9,11},{10,... | collective-permute-start | bytes 1228808 | tf_op jit(solution)/shard_map/ppermute | solution.py:21
  32.2 12.5 %collective-permute-start.14 = (f32[792,128]{1,0:T(8,128)S(1)}, f32[792,128]{1,0:T(8,128)S(1)}, u32[]{:S(2)}, u32[]{:S(2)}) collective-permute-start(f32[792,128]{1,0:T(8,128)S(1)} %sums.8), channel_id=1, source_target_pairs={{0,28},{4,0},{8,4},{12,8},{16,12},{20,16},{24,20},{28,24},{1,29},{... | collective-permute-start | bytes 1216520 | tf_op jit(solution)/shard_map/ppermute | solution.py:16
  36.9 1.8 %collective-permute-start.10 = (f32[776,128]{1,0:T(8,128)S(1)}, f32[776,128]{1,0:T(8,128)S(1)}, u32[]{:S(2)}, u32[]{:S(2)}) collective-permute-start(f32[776,128]{1,0:T(8,128)S(1)} %slice.14.refs_4_.refs_2_), channel_id=1, source_target_pairs={{0,1},{1,0},{2,3},{3,2},{4,5},{5,4},{6,7},{7,6},{8,9},{9,8},{10,11... | collective-permute-start | bytes 1191944 | tf_op jit(solution)/shard_map/ppermute | solution.py:21
  40.9 14.7 %collective-permute-start.11 = (f32[792,128]{1,0:T(8,128)S(1)}, f32[792,128]{1,0:T(8,128)S(1)}, u32[]{:S(2)}, u32[]{:S(2)}) collective-permute-start(f32[792,128]{1,0:T(8,128)S(1)} %sums.10), channel_id=1, source_target_pairs={{0,4},{4,8},{8,12},{12,16},{16,20},{20,24},{24,28},{28,0},{1,5},{5... | collective-permute-start | bytes 1216520 | tf_op jit(solution)/shard_map/ppermute | solution.py:16
  44.8 1.8 %collective-permute-start.15 = (f32[776,128]{1,0:T(8,128)S(1)}, f32[776,128]{1,0:T(8,128)S(1)}, u32[]{:S(2)}, u32[]{:S(2)}) collective-permute-start(f32[776,128]{1,0:T(8,128)S(1)} %slice.15.refs_2_), channel_id=1, source_target_pairs={{0,1},{1,0},{2,3},{3,2},{4,5},{5,4},{6,7},{7,6},{8,9},{9,8},{10,11... | collective-permute-start | bytes 1191944 | tf_op jit(solution)/shard_map/ppermute | solution.py:21

commit v2 on v1

--- a/solution.py
+++ b/solution.py
@@ -139,7 +139,7 @@
                 out[start : start + side, :] = acc[row, t]
 
 
-def finish_kernel(base, to_below, to_above_own, from_below, to_above_next, out, result, sems):
+def finish_kernel(base, lower, middle, own_middle, upper, out, result, sems):
     local_rows, slots, side, _ = base.shape
     per = slots // 3
     copies = []
@@ -147,10 +147,10 @@
         for slot in range(per):
             start = (row * per + slot) * side
             lines = slice(start, start + side)
-            result[row, slot] = base[row, slot] - to_below[lines, :]
-            both = to_above_own[lines, :] + from_below[lines, :]
+            result[row, slot] = base[row, slot] - lower[lines, :]
+            both = middle[lines, :] + own_middle[lines, :]
             result[row, per + slot] = base[row, per + slot] - both
-            result[row, 2 * per + slot] = base[row, 2 * per + slot] - to_above_next[lines, :]
+            result[row, 2 * per + slot] = base[row, 2 * per + slot] - upper[lines, :]
         copies.append(pltpu.make_async_copy(result.at[row], out.at[row], sems.at[row]))
         copies[-1].start()
     for copy in copies:
@@ -164,7 +164,7 @@
     strip_rows = local_rows * parts
     meta_rows = local_rows * per + -(local_rows * per) % 8
     used_rows = local_rows * per * side + meta_rows
-    payload_rows = used_rows + 24
+    payload_rows = used_rows + 3
     in_hbm = pl.BlockSpec(memory_space=pltpu.HBM)
     scalars = pl.BlockSpec(memory_space=pltpu.SMEM)
     vectors = pl.BlockSpec(memory_space=pltpu.VMEM)
@@ -189,7 +189,7 @@
         lax.axis_index("inner").reshape(1),
     )
 
-    spare = 24
+    spare = 10
 
     def sums(groups, a_at, plan, first, width, offset=0, base=()):
         held = len(groups[0])
@@ -220,35 +220,34 @@
         return list(lax.optimization_barrier((*values, *after)))[: len(values)]
 
     own_plan = ((0, 0), (1, per), (2, 2 * per))
-    below = shifted(upper, 1)
+    above = shifted(lower, -1)
     lowers, middles, uppers = halves(lower), halves(middle), halves(upper)
-    far_lower = across(lower)
+    far_upper = across(upper)
     base = sums([lowers, middles, uppers], 1, own_plan, 0, slots)
 
     far_middle = across(middle, [base])
-    far_lowers = spread(tied(far_lower, base))
-    far_lowers = tied(far_lowers, below)
-    above_own = sums([lowers + far_lowers], 0, ((0, 0),), per, per)
-    to_above_own = shifted(above_own, -1)
-
-    far_upper = across(upper, [above_own])
-    far_middles = spread(tied(far_middle, above_own))
+    far_uppers = tied(spread(far_upper), above) if far_upper else []
+    below_own = sums([uppers + far_uppers], 0, ((0, 2 * per),), per, per)
+
+    far_lower = across(lower, [below_own])
+    to_below_own = shifted(below_own, 1)
+    far_middles = spread(tied(far_middle, below_own))
     all_middles = middles + far_middles
+    below_next = sums([uppers + far_uppers, all_middles], 0, ((1, per),), 0, per)
+
+    aboves = halves(above)
+    far_above = across(above, [below_next, *aboves])
+    to_below_next = shifted(below_next, 1)
+    far_lowers = spread(tied(far_lower, below_next, to_below_own))
     above_next = sums([lowers + far_lowers, all_middles], 0, ((1, per),), 2 * per, per)
     to_above_next = shifted(above_next, -1)
-
-    belows = halves(below)
-    far_below = across(below, [above_next, *belows])
-    far_uppers = spread(tied(far_upper, above_next, to_above_own))
-    to_next = sums([uppers + far_uppers, all_middles], 0, ((1, per),), 0, per)
-    to_below = shifted(to_next, 1)
     if far_lowers:
         near = len(lowers)
         groups = [far_lowers, far_middles, far_uppers]
         base = sums(groups, 1, own_plan, 0, slots, near, [base])
-        far_below = tied(far_below, base, to_next, to_above_next)
-    belows = belows + spread(far_below)
-    from_below = sums([belows], 0, ((0, 2 * per),), per, per)
+        far_above = tied(far_above, base, above_next, to_below_next)
+    aboves = aboves + spread(far_above)
+    from_above = sums([aboves], 0, ((0, 0),), per, per)
     return pl.pallas_call(
         finish_kernel,
         out_shape=jax.ShapeDtypeStruct(density.shape, jnp.float32),
@@ -261,7 +260,7 @@
         compiler_params=pltpu.CompilerParams(vmem_limit_bytes=16 << 20),
         cost_estimate=pl.CostEstimate(flops=1, bytes_accessed=1, transcendentals=0),
         name="finish",
-    )(base, to_below, to_above_own, from_below, to_above_next)
+    )(base, to_below_next, to_below_own, from_above, to_above_next)
 
 
 def solution(mesh):

time: 56.8 us -> 56.5 us (level)
  Pallas kernels: 15.8 us -> 17.5 us
  starting transfers between devices: 16.2 us -> 15.1 us
  waiting for transfers between devices: 23.1 us -> 22.1 us
    ppermute x12, waiting for transfers between devices: 11 us -> 8.29 us  [swapped(): lax.ppermute(value, 'inner', [(i, i ^ distance) for i in range(count)])]
    ppermute x4, waiting for transfers between devices: 12.1 us -> 13.8 us  [shifted(): return lax.ppermute(value, 'blk', pairs)]
    pallas_call x6, Pallas kernels: 13.3 us -> 15 us  [sums(): pl.pallas_call(functools.partial(sums_kernel, dims, plan), out_shape=jax....]
    ppermute x4, starting transfers between devices: 10.8 us -> 9.7 us  [shifted(): return lax.ppermute(value, 'blk', pairs)]
  transfers between devices with their start and end apart: 16 -> 16, of which waited for: 7 -> 8; matrix products, arithmetic and copies ran while one was open for 0% -> 0% of each run, Pallas kernels for 23% -> 27%
where the time goes in v2:
time: 56.5 us; the launch traced here: 56.4 us
  waiting for transfers between devices  22.1 us (39%)
  Pallas kernels  17.5 us (31%)
  starting transfers between devices  15.1 us (27%)
  local copies, waits for them, and re-layouts  1.48 us (3%)
    pallas_call x6, Pallas kernels, sums(): pl.pallas_call(functools.partial(sums_kernel, dims, plan), out_shape=jax....  15 us
    ppermute x4, waiting for transfers between devices, shifted(): return lax.ppermute(value, 'blk', pairs)  13.8 us
    ppermute x4, starting transfers between devices, shifted(): return lax.ppermute(value, 'blk', pairs)  9.7 us
    ppermute x12, waiting for transfers between devices, swapped(): lax.ppermute(value, 'inner', [(i, i ^ distance) for i in range(count)])  8.29 us
    ppermute x12, starting transfers between devices, swapped(): lax.ppermute(value, 'inner', [(i, i ^ distance) for i in range(count)])  5.39 us
    pallas_call x1, Pallas kernels, shards(): pl.pallas_call(functools.partial(pack_kernel, (local_rows, slots, side, s...  1.41 us
    unnamed x4, local copies, waits for them, and re-layouts  1.38 us
  transfers between devices with their start and end apart: 16, of which 8 were waited for; matrix products, arithmetic and copies ran while one was open for 0% of the time, Pallas kernels for 27%

profile of v2, /device:TPU:0, one launch (start us, length us, event | category | flops | bytes accessed | tf_op | source)
XLA Modules:
  0.0 56.4 jit_solution(12423691242211151629)
XLA Ops:
  0.0 0.0 copy-start
  0.0 0.7 %copy-done = s32[2,9,9]{2,0,1:T(2,128)S(1)} copy-done((s32[2,9,9]{2,0,1:T(2,128)S(1)}, s32[2,9,9]{2,0,1:T(2,128)}, u32[]{:S(2)}) %copy-start) | copy-done | bytes 672
  0.7 0.0 copy-start.1
  0.7 0.7 %copy-done.1 = s32[2,9]{1,0:T(2,128)S(1)} copy-done((s32[2,9]{1,0:T(2,128)S(1)}, s32[2,9]{1,0:T(2,128)}, u32[]{:S(2)}) %copy-start.1) | copy-done | bytes 96
  1.4 1.4 %pack.1 = (f32[779,128]{1,0:T(8,128)S(1)}, f32[779,128]{1,0:T(8,128)S(1)}, f32[779,128]{1,0:T(8,128)S(1)}) custom-call(f32[2304,128]{1,0:T(8,128)} %bitcast.4, s32[9,2,9]{2,1,0:T(2,128)S(1)} %bitcast.3, s32[2,9]{1,0:T(2,128)S(1)} %copy-done.1, s32[1]{0:T(128)} %bitcast.2.inner), custom_call_target="tpu_custom_call" | custom-call | tf_op jit(solution)/shard_map/pack/pallas_call | solution.py:172
  2.8 0.5 collective-permute-start
  3.3 0.1 collective-permute-start.5
  3.4 0.4 collective-permute-start.6
  3.8 2.6 %collective-permute-start.1 = (f32[779,128]{1,0:T(8,128)S(1)}, f32[779,128]{1,0:T(8,128)S(1)}, u32[]{:S(2)}, u32[]{:S(2)}) collective-permute-start(f32[779,128]{1,0:T(8,128)S(1)} %get-tuple-element.17.refs_0_.refs_4_), channel_id=1, source_target_pairs={{0,2},{1,3},{2,0},{3,1},{4,6},{5,7},{6,4},{7,5},{8,10},{9,11},{10,... | collective-permute-start | bytes 1196552 | tf_op jit(solution)/shard_map/ppermute | solution.py:21
  6.4 4.6 %collective-permute-start.3 = (f32[779,128]{1,0:T(8,128)S(1)}, f32[779,128]{1,0:T(8,128)S(1)}, u32[]{:S(2)}, u32[]{:S(2)}) collective-permute-start(f32[779,128]{1,0:T(8,128)S(1)} %get-tuple-element.20.refs_0_), channel_id=1, source_target_pairs={{0,28},{4,0},{8,4},{12,8},{16,12},{20,16},{24,20},{28,24},{1,29},{... | collective-permute-start | bytes 1196552 | tf_op jit(solution)/shard_map/ppermute | solution.py:16
  10.9 0.0 collective-permute-done.refs_1_.refs_5_
  11.0 0.0 collective-permute-done.5.refs_3_.refs_5_
  11.0 0.0 collective-permute-done.6.refs_1_
  11.0 2.9 %sums.7.refs_6_ = f32[2,9,128,128]{3,2,1,0:T(8,128)S(1)} custom-call(f32[779,128]{1,0:T(8,128)S(1)} %get-tuple-element.20.refs_0_, f32[779,128]{1,0:T(8,128)S(1)} %collective-permute-done.6.refs_1_, f32[779,128]{1,0:T(8,128)S(1)} %get-tuple-element.22.refs_2_.refs_4_, f32[779,128]{1,0:T(8,128)S(1)} %collective-permute-done.5.refs_3_.refs_5_, ...), custom_call_target="tpu_custom_call" | custom-call | flops 1 | bytes 1 | tf_op jit(solution)/shard_map/sums/pallas_call | solution.py:197
  13.9 0.2 collective-permute-start.7
  14.1 2.4 %collective-permute-done.1 = f32[779,128]{1,0:T(8,128)S(1)} collective-permute-done((f32[779,128]{1,0:T(8,128)S(1)}, f32[779,128]{1,0:T(8,128)S(1)}, u32[]{:S(2)}, u32[]{:S(2)}) %collective-permute-start.1) | collective-permute-done | bytes 398880 | tf_op jit(solution)/shard_map/ppermute | solution.py:21
  16.5 0.1 collective-permute-start.2
  16.5 3.3 %collective-permute-done.3.refs_0_ = f32[779,128]{1,0:T(8,128)S(1)} collective-permute-done((f32[779,128]{1,0:T(8,128)S(1)}, f32[779,128]{1,0:T(8,128)S(1)}, u32[]{:S(2)}, u32[]{:S(2)}) %collective-permute-start.3) | collective-permute-done | bytes 398880 | tf_op jit(solution)/shard_map/ppermute | solution.py:16
  19.8 0.0 collective-permute-start.12
  19.8 0.0 collective-permute-done.2.refs_3_.refs_5_
  19.8 3.0 %sums.6 = f32[778,128]{1,0:T(8,128)S(1)} custom-call(f32[779,128]{1,0:T(8,128)S(1)} %get-tuple-element.17.refs_0_.refs_4_, f32[779,128]{1,0:T(8,128)S(1)} %collective-permute-done.refs_1_.refs_5_, f32[776,128]{1,0:T(8,128)S(1)} %slice.16.refs_2_.refs_4_, f32[776,128]{1,0:T(8,128)S(1)} %collective-permute-done.2.refs_3_.refs_5_), custom_call_target="tpu_custom_call" | custom-call | flops 1 | bytes 1 | tf_op jit(solution)/shard_map/sums/pallas_call | solution.py:197
  22.8 0.1 collective-permute-start.4
  22.9 1.2 %collective-permute-start.9 = (f32[778,128]{1,0:T(8,128)S(1)}, f32[778,128]{1,0:T(8,128)S(1)}, u32[]{:S(2)}, u32[]{:S(2)}) collective-permute-start(f32[778,128]{1,0:T(8,128)S(1)} %sums.6), channel_id=1, source_target_pairs={{0,4},{4,8},{8,12},{12,16},{16,20},{20,24},{24,28},{28,0},{1,5},{5... | collective-permute-start | bytes 1195016 | tf_op jit(solution)/shard_map/ppermute | solution.py:16
  24.1 0.8 %collective-permute-done.7 = f32[779,128]{1,0:T(8,128)S(1)} collective-permute-done((f32[779,128]{1,0:T(8,128)S(1)}, f32[779,128]{1,0:T(8,128)S(1)}, u32[]{:S(2)}, u32[]{:S(2)}) %collective-permute-start.7) | collective-permute-done | bytes 398880 | tf_op jit(solution)/shard_map/ppermute | solution.py:21
  24.9 0.1 collective-permute-start.8
  25.0 1.7 %collective-permute-done.8.refs_7_.refs_3_ = f32[776,128]{1,0:T(8,128)S(1)} collective-permute-done((f32[776,128]{1,0:T(8,128)S(1)}, f32[776,128]{1,0:T(8,128)S(1)}, u32[]{:S(2)}, u32[]{:S(2)}) %collective-permute-start.8) | collective-permute-done | bytes 397344 | tf_op jit(solution)/shard_map/ppermute | solution.py:21
  26.7 3.0 %sums.8 = f32[778,128]{1,0:T(8,128)S(1)} custom-call(f32[779,128]{1,0:T(8,128)S(1)} %get-tuple-element.17.refs_0_.refs_4_, f32[779,128]{1,0:T(8,128)S(1)} %collective-permute-done.refs_1_.refs_5_, f32[776,128]{1,0:T(8,128)S(1)} %slice.16.refs_2_.refs_4_, f32[776,128]{1,0:T(8,128)S(1)} %collective-permute-done.2.refs_3_.refs_5_, ...), custom_call_target="tpu_custom_call" | custom-call | flops 1 | bytes 1 | tf_op jit(solution)/shard_map/sums/pallas_call | solution.py:197
  29.7 0.0 collective-permute-done.12.refs_1_
  29.7 1.2 %collective-permute-start.13 = (f32[779,128]{1,0:T(8,128)S(1)}, f32[779,128]{1,0:T(8,128)S(1)}, u32[]{:S(2)}, u32[]{:S(2)}) collective-permute-start(f32[779,128]{1,0:T(8,128)S(1)} %collective-permute-done.3.refs_0_), channel_id=1, source_target_pairs={{0,2},{1,3},{2,0},{3,1},{4,6},{5,7},{6,4},{7,5},{8,10},{9,11},{10,... | collective-permute-start | bytes 1196552 | tf_op jit(solution)/shard_map/ppermute | solution.py:21
  30.9 1.6 %collective-permute-start.11 = (f32[778,128]{1,0:T(8,128)S(1)}, f32[778,128]{1,0:T(8,128)S(1)}, u32[]{:S(2)}, u32[]{:S(2)}) collective-permute-start(f32[778,128]{1,0:T(8,128)S(1)} %sums.8), channel_id=1, source_target_pairs={{0,4},{4,8},{8,12},{12,16},{16,20},{20,24},{24,28},{28,0},{1,5},{5... | collective-permute-start | bytes 1195016 | tf_op jit(solution)/shard_map/ppermute | solution.py:16
  32.5 5.9 %collective-permute-done.9.middle = f32[778,128]{1,0:T(8,128)S(1)} collective-permute-done((f32[778,128]{1,0:T(8,128)S(1)}, f32[778,128]{1,0:T(8,128)S(1)}, u32[]{:S(2)}, u32[]{:S(2)}) %collective-permute-start.9) | collective-permute-done | bytes 398368 | tf_op jit(solution)/shard_map/ppermute | solution.py:16
  38.4 0.0 collective-permute-done.4
  38.4 0.1 collective-permute-start.10
  38.5 1.7 %collective-permute-done.10.refs_1_.refs_3_ = f32[776,128]{1,0:T(8,128)S(1)} collective-permute-done((f32[776,128]{1,0:T(8,128)S(1)}, f32[776,128]{1,0:T(8,128)S(1)}, u32[]{:S(2)}, u32[]{:S(2)}) %collective-permute-start.10) | collective-permute-done | bytes 397344 | tf_op jit(solution)/shard_map/ppermute | solution.py:21
  40.2 1.7 %sums.10 = f32[778,128]{1,0:T(8,128)S(1)} custom-call(f32[779,128]{1,0:T(8,128)S(1)} %get-tuple-element.20.refs_0_, f32[779,128]{1,0:T(8,128)S(1)} %collective-permute-done.6.refs_1_, f32[776,128]{1,0:T(8,128)S(1)} %slice.14.refs_0_.refs_2_, f32[776,128]{1,0:T(8,128)S(1)} %collective-permute-done.10.refs_1_.refs_3_, ...), custom_call_target="tpu_custom_call" | custom-call | flops 1 | bytes 1 | tf_op jit(solution)/shard_map/sums/pallas_call | solution.py:197
  41.9 2.4 %collective-permute-start.15 = (f32[778,128]{1,0:T(8,128)S(1)}, f32[778,128]{1,0:T(8,128)S(1)}, u32[]{:S(2)}, u32[]{:S(2)}) collective-permute-start(f32[778,128]{1,0:T(8,128)S(1)} %sums.10), channel_id=1, source_target_pairs={{0,28},{4,0},{8,4},{12,8},{16,12},{20,16},{24,20},{28,24},{1,29},{... | collective-permute-start | bytes 1195016 | tf_op jit(solution)/shard_map/ppermute | solution.py:16
  44.3 2.1 %sums.9.base = f32[2,9,128,128]{3,2,1,0:T(8,128)S(1)} custom-call(f32[776,128]{1,0:T(8,128)S(1)} %slice.14.refs_0_.refs_2_, f32[776,128]{1,0:T(8,128)S(1)} %collective-permute-done.10.refs_1_.refs_3_, f32[776,128]{1,0:T(8,128)S(1)} %slice.13.refs_6_.refs_2_, f32[776,128]{1,0:T(8,128)S(1)} %collective-permute-done.8.refs_7_.refs_3_, ...), custom_call_target="tpu_custom_call" | custom-call | flops 1 | bytes 1 | tf_op jit(solution)/shard_map/sums/pallas_call | solution.py:197
  46.3 4.6 %collective-permute-done.11.lower = f32[778,128]{1,0:T(8,128)S(1)} collective-permute-done((f32[778,128]{1,0:T(8,128)S(1)}, f32[778,128]{1,0:T(8,128)S(1)}, u32[]{:S(2)}, u32[]{:S(2)}) %collective-permute-start.11) | collective-permute-done | bytes 398368 | tf_op jit(solution)/shard_map/ppermute | solution.py:16
  50.9 0.0 collective-permute-done.13
  51.0 0.1 collective-permute-start.14
  51.1 1.7 %collective-permute-done.14.refs_3_ = f32[776,128]{1,0:T(8,128)S(1)} collective-permute-done((f32[776,128]{1,0:T(8,128)S(1)}, f32[776,128]{1,0:T(8,128)S(1)}, u32[]{:S(2)}, u32[]{:S(2)}) %collective-permute-start.14) | collective-permute-done | bytes 397344 | tf_op jit(solution)/shard_map/ppermute | solution.py:21
  52.8 2.4 %sums.11.own_middle = f32[778,128]{1,0:T(8,128)S(1)} custom-call(f32[779,128]{1,0:T(8,128)S(1)} %collective-permute-done.3.refs_0_, f32[779,128]{1,0:T(8,128)S(1)} %collective-permute-done.12.refs_1_, f32[776,128]{1,0:T(8,128)S(1)} %slice.15.refs_2_, f32[776,128]{1,0:T(8,128)S(1)} %collective-permute-done.14.refs_3_), custom_call_target="tpu_custom_call" | custom-call | flops 1 | bytes 1 | tf_op jit(solution)/shard_map/sums/pallas_call | solution.py:197
  55.2 0.1 collective-permute-done.15.upper
  55.3 1.1 %finish.1 = f32[2,9,128,128]{3,2,1,0:T(8,128)} custom-call(f32[2,9,128,128]{3,2,1,0:T(8,128)S(1)} %sums.9.base, f32[778,128]{1,0:T(8,128)S(1)} %collective-permute-done.11.lower, f32[778,128]{1,0:T(8,128)S(1)} %collective-permute-done.9.middle, f32[778,128]{1,0:T(8,128)S(1)} %sums.11.own_middle, f32[778,128]{1,0:T(8,128)S(1)} %collective-permute-done.15.upper), custom_call_target="tpu_custom_call" | custom-call | flops 1 | bytes 1 | tf_op jit(solution)/shard_map/finish/pallas_call | solution.py:251
  (4 shorter events, 0.1 us)
Async XLA Ops:
  0.0 0.7 %copy-start = (s32[2,9,9]{2,0,1:T(2,128)S(1)}, s32[2,9,9]{2,0,1:T(2,128)}, u32[]{:S(2)}) copy-start(s32[2,9,9]{2,0,1:T(2,128)} %param.5) | copy-start | bytes 1948
  0.7 0.7 %copy-start.1 = (s32[2,9]{1,0:T(2,128)S(1)}, s32[2,9]{1,0:T(2,128)}, u32[]{:S(2)}) copy-start(s32[2,9]{1,0:T(2,128)} %cols.1) | copy-start | bytes 220
  2.8 8.2 %collective-permute-start = (f32[779,128]{1,0:T(8,128)S(1)}, f32[779,128]{1,0:T(8,128)S(1)}, u32[]{:S(2)}, u32[]{:S(2)}) collective-permute-start(f32[779,128]{1,0:T(8,128)S(1)} %get-tuple-element.17.refs_0_.refs_4_), channel_id=1, source_target_pairs={{0,1},{1,0},{2,3},{3,2},{4,5},{5,4},{6,7},{7,6},{8,9},{9,8},{10,11... | collective-permute-start | bytes 1196552 | tf_op jit(solution)/shard_map/ppermute | solution.py:21
  3.3 7.6 %collective-permute-start.5 = (f32[779,128]{1,0:T(8,128)S(1)}, f32[779,128]{1,0:T(8,128)S(1)}, u32[]{:S(2)}, u32[]{:S(2)}) collective-permute-start(f32[779,128]{1,0:T(8,128)S(1)} %get-tuple-element.22.refs_2_.refs_4_), channel_id=1, source_target_pairs={{0,1},{1,0},{2,3},{3,2},{4,5},{5,4},{6,7},{7,6},{8,9},{9,8},{10,11... | collective-permute-start | bytes 1196552 | tf_op jit(solution)/shard_map/ppermute | solution.py:21
  3.4 7.6 %collective-permute-start.6 = (f32[779,128]{1,0:T(8,128)S(1)}, f32[779,128]{1,0:T(8,128)S(1)}, u32[]{:S(2)}, u32[]{:S(2)}) collective-permute-start(f32[779,128]{1,0:T(8,128)S(1)} %get-tuple-element.20.refs_0_), channel_id=1, source_target_pairs={{0,1},{1,0},{2,3},{3,2},{4,5},{5,4},{6,7},{7,6},{8,9},{9,8},{10,11... | collective-permute-start | bytes 1196552 | tf_op jit(solution)/shard_map/ppermute | solution.py:21
  3.8 12.6 %collective-permute-start.1 = (f32[779,128]{1,0:T(8,128)S(1)}, f32[779,128]{1,0:T(8,128)S(1)}, u32[]{:S(2)}, u32[]{:S(2)}) collective-permute-start(f32[779,128]{1,0:T(8,128)S(1)} %get-tuple-element.17.refs_0_.refs_4_), channel_id=1, source_target_pairs={{0,2},{1,3},{2,0},{3,1},{4,6},{5,7},{6,4},{7,5},{8,10},{9,11},{10,... | collective-permute-start | bytes 1196552 | tf_op jit(solution)/shard_map/ppermute | solution.py:21
  6.4 13.4 %collective-permute-start.3 = (f32[779,128]{1,0:T(8,128)S(1)}, f32[779,128]{1,0:T(8,128)S(1)}, u32[]{:S(2)}, u32[]{:S(2)}) collective-permute-start(f32[779,128]{1,0:T(8,128)S(1)} %get-tuple-element.20.refs_0_), channel_id=1, source_target_pairs={{0,28},{4,0},{8,4},{12,8},{16,12},{20,16},{24,20},{28,24},{1,29},{... | collective-permute-start | bytes 1196552 | tf_op jit(solution)/shard_map/ppermute | solution.py:16
  13.9 11.0 %collective-permute-start.7 = (f32[779,128]{1,0:T(8,128)S(1)}, f32[779,128]{1,0:T(8,128)S(1)}, u32[]{:S(2)}, u32[]{:S(2)}) collective-permute-start(f32[779,128]{1,0:T(8,128)S(1)} %get-tuple-element.22.refs_2_.refs_4_), channel_id=1, source_target_pairs={{0,2},{1,3},{2,0},{3,1},{4,6},{5,7},{6,4},{7,5},{8,10},{9,11},{10,... | collective-permute-start | bytes 1196552 | tf_op jit(solution)/shard_map/ppermute | solution.py:21
  16.5 3.4 %collective-permute-start.2 = (f32[776,128]{1,0:T(8,128)S(1)}, f32[776,128]{1,0:T(8,128)S(1)}, u32[]{:S(2)}, u32[]{:S(2)}) collective-permute-start(f32[776,128]{1,0:T(8,128)S(1)} %slice.16.refs_2_.refs_4_), channel_id=1, source_target_pairs={{0,1},{1,0},{2,3},{3,2},{4,5},{5,4},{6,7},{7,6},{8,9},{9,8},{10,11... | collective-permute-start | bytes 1191944 | tf_op jit(solution)/shard_map/ppermute | solution.py:21
  19.8 9.9 %collective-permute-start.12 = (f32[779,128]{1,0:T(8,128)S(1)}, f32[779,128]{1,0:T(8,128)S(1)}, u32[]{:S(2)}, u32[]{:S(2)}) collective-permute-start(f32[779,128]{1,0:T(8,128)S(1)} %collective-permute-done.3.refs_0_), channel_id=1, source_target_pairs={{0,1},{1,0},{2,3},{3,2},{4,5},{5,4},{6,7},{7,6},{8,9},{9,8},{10,11... | collective-permute-start | bytes 1196552 | tf_op jit(solution)/shard_map/ppermute | solution.py:21
  22.8 15.6 %collective-permute-start.4 = (f32[779,128]{1,0:T(8,128)S(1)}, f32[779,128]{1,0:T(8,128)S(1)}, u32[]{:S(2)}, u32[]{:S(2)}) collective-permute-start(f32[779,128]{1,0:T(8,128)S(1)} %get-tuple-element.20.refs_0_), channel_id=1, source_target_pairs={{0,2},{1,3},{2,0},{3,1},{4,6},{5,7},{6,4},{7,5},{8,10},{9,11},{10,... | collective-permute-start | bytes 1196552 | tf_op jit(solution)/shard_map/ppermute | solution.py:21
  22.9 15.5 %collective-permute-start.9 = (f32[778,128]{1,0:T(8,128)S(1)}, f32[778,128]{1,0:T(8,128)S(1)}, u32[]{:S(2)}, u32[]{:S(2)}) collective-permute-start(f32[778,128]{1,0:T(8,128)S(1)} %sums.6), channel_id=1, source_target_pairs={{0,4},{4,8},{8,12},{12,16},{16,20},{20,24},{24,28},{28,0},{1,5},{5... | collective-permute-start | bytes 1195016 | tf_op jit(solution)/shard_map/ppermute | solution.py:16
  24.9 1.8 %collective-permute-start.8 = (f32[776,128]{1,0:T(8,128)S(1)}, f32[776,128]{1,0:T(8,128)S(1)}, u32[]{:S(2)}, u32[]{:S(2)}) collective-permute-start(f32[776,128]{1,0:T(8,128)S(1)} %slice.13.refs_6_.refs_2_), channel_id=1, source_target_pairs={{0,1},{1,0},{2,3},{3,2},{4,5},{5,4},{6,7},{7,6},{8,9},{9,8},{10,11... | collective-permute-start | bytes 1191944 | tf_op jit(solution)/shard_map/ppermute | solution.py:21
  29.7 21.2 %collective-permute-start.13 = (f32[779,128]{1,0:T(8,128)S(1)}, f32[779,128]{1,0:T(8,128)S(1)}, u32[]{:S(2)}, u32[]{:S(2)}) collective-permute-start(f32[779,128]{1,0:T(8,128)S(1)} %collective-permute-done.3.refs_0_), channel_id=1, source_target_pairs={{0,2},{1,3},{2,0},{3,1},{4,6},{5,7},{6,4},{7,5},{8,10},{9,11},{10,... | collective-permute-start | bytes 1196552 | tf_op jit(solution)/shard_map/ppermute | solution.py:21
  30.9 20.0 %collective-permute-start.11 = (f32[778,128]{1,0:T(8,128)S(1)}, f32[778,128]{1,0:T(8,128)S(1)}, u32[]{:S(2)}, u32[]{:S(2)}) collective-permute-start(f32[778,128]{1,0:T(8,128)S(1)} %sums.8), channel_id=1, source_target_pairs={{0,4},{4,8},{8,12},{12,16},{16,20},{20,24},{24,28},{28,0},{1,5},{5... | collective-permute-start | bytes 1195016 | tf_op jit(solution)/shard_map/ppermute | solution.py:16
  38.4 1.8 %collective-permute-start.10 = (f32[776,128]{1,0:T(8,128)S(1)}, f32[776,128]{1,0:T(8,128)S(1)}, u32[]{:S(2)}, u32[]{:S(2)}) collective-permute-start(f32[776,128]{1,0:T(8,128)S(1)} %slice.14.refs_0_.refs_2_), channel_id=1, source_target_pairs={{0,1},{1,0},{2,3},{3,2},{4,5},{5,4},{6,7},{7,6},{8,9},{9,8},{10,11... | collective-permute-start | bytes 1191944 | tf_op jit(solution)/shard_map/ppermute | solution.py:21
  41.9 13.4 %collective-permute-start.15 = (f32[778,128]{1,0:T(8,128)S(1)}, f32[778,128]{1,0:T(8,128)S(1)}, u32[]{:S(2)}, u32[]{:S(2)}) collective-permute-start(f32[778,128]{1,0:T(8,128)S(1)} %sums.10), channel_id=1, source_target_pairs={{0,28},{4,0},{8,4},{12,8},{16,12},{20,16},{24,20},{28,24},{1,29},{... | collective-permute-start | bytes 1195016 | tf_op jit(solution)/shard_map/ppermute | solution.py:16
  51.0 1.8 %collective-permute-start.14 = (f32[776,128]{1,0:T(8,128)S(1)}, f32[776,128]{1,0:T(8,128)S(1)}, u32[]{:S(2)}, u32[]{:S(2)}) collective-permute-start(f32[776,128]{1,0:T(8,128)S(1)} %slice.15.refs_2_), channel_id=1, source_target_pairs={{0,1},{1,0},{2,3},{3,2},{4,5},{5,4},{6,7},{7,6},{8,9},{9,8},{10,11... | collective-permute-start | bytes 1191944 | tf_op jit(solution)/shard_map/ppermute | solution.py:21

commit v3 on v2

--- a/solution.py
+++ b/solution.py
@@ -128,7 +128,7 @@
         lax.fori_loop(0, count, multiply, 0)
     for row in range(local_rows):
         for t in range(width):
-            if base:
+            if base and width == slots:
                 out[row, t] = base[0][row, t] - acc[row, t]
             elif width == slots:
                 start = (row * per + t % per) * side
@@ -136,7 +136,8 @@
                 out[row, t] = 2.0 * mine - acc[row, t]
             else:
                 start = (row * width + t) * side
-                out[start : start + side, :] = acc[row, t]
+                lines = slice(start, start + side)
+                out[lines, :] = base[0][lines, :] + acc[row, t] if base else acc[row, t]
 
 
 def finish_kernel(base, lower, middle, own_middle, upper, out, result, sems):
@@ -213,6 +214,14 @@
             name="sums",
         )(*[payload for group in groups for payload in group], *base)
 
+    def strip_sums(groups, a_at, plan, first):
+        early = parts // 2 + 1
+        total = sums([group[:early] for group in groups], a_at, plan, first, per)
+        if parts > early:
+            rest = [group[early:] for group in groups]
+            total = sums(rest, a_at, plan, first, per, early, [total])
+        return total
+
     def spread(far):
         return [one for value in far for one in halves(value[:used_rows])]
 
@@ -226,20 +235,21 @@
     base = sums([lowers, middles, uppers], 1, own_plan, 0, slots)
 
     far_middle = across(middle, [base])
-    far_uppers = tied(spread(far_upper), above) if far_upper else []
-    below_own = sums([uppers + far_uppers], 0, ((0, 2 * per),), per, per)
+    far_uppers = spread(far_upper)
+    far_uppers = far_uppers[:1] + [tied([one], above)[0] for one in far_uppers[1:]]
+    below_own = strip_sums([uppers + far_uppers], 0, ((0, 2 * per),), per)
 
     far_lower = across(lower, [below_own])
     to_below_own = shifted(below_own, 1)
     far_middles = spread(tied(far_middle, below_own))
     all_middles = middles + far_middles
-    below_next = sums([uppers + far_uppers, all_middles], 0, ((1, per),), 0, per)
+    below_next = strip_sums([uppers + far_uppers, all_middles], 0, ((1, per),), 0)
 
     aboves = halves(above)
     far_above = across(above, [below_next, *aboves])
     to_below_next = shifted(below_next, 1)
     far_lowers = spread(tied(far_lower, below_next, to_below_own))
-    above_next = sums([lowers + far_lowers, all_middles], 0, ((1, per),), 2 * per, per)
+    above_next = strip_sums([lowers + far_lowers, all_middles], 0, ((1, per),), 2 * per)
     to_above_next = shifted(above_next, -1)
     if far_lowers:
         near = len(lowers)
@@ -247,7 +257,7 @@
         base = sums(groups, 1, own_plan, 0, slots, near, [base])
         far_above = tied(far_above, base, above_next, to_below_next)
     aboves = aboves + spread(far_above)
-    from_above = sums([aboves], 0, ((0, 0),), per, per)
+    from_above = strip_sums([aboves], 0, ((0, 0),), per)
     return pl.pallas_call(
         finish_kernel,
         out_shape=jax.ShapeDtypeStruct(density.shape, jnp.float32),

time: 56.5 us -> 56.8 us (level)
  Pallas kernels: 17.5 us -> 21.6 us
  waiting for transfers between devices: 22.1 us -> 19.5 us
  starting transfers between devices: 15.1 us -> 13.9 us
    ppermute x12, waiting for transfers between devices: 8.29 us -> 3.4 us  [swapped(): lax.ppermute(value, 'inner', [(i, i ^ distance) for i in range(count)])]
    pallas_call x6 -> x10, Pallas kernels: 15 us -> 19 us  [sums(): pl.pallas_call(functools.partial(sums_kernel, dims, plan), out_shape=jax....]
    ppermute x4, waiting for transfers between devices: 13.8 us -> 16.1 us  [shifted(): return lax.ppermute(value, 'blk', pairs)]
    ppermute x4, starting transfers between devices: 9.7 us -> 8.6 us  [shifted(): return lax.ppermute(value, 'blk', pairs)]
  transfers between devices with their start and end apart: 16 -> 16, of which waited for: 8 -> 6; matrix products, arithmetic and copies ran while one was open for 0% -> 0% of each run, Pallas kernels for 27% -> 34%
where the time goes in v3:
time: 56.8 us; the launch traced here: 56.7 us
  Pallas kernels  21.6 us (38%)
  waiting for transfers between devices  19.5 us (34%)
  starting transfers between devices  13.9 us (24%)
  local copies, waits for them, and re-layouts  1.48 us (3%)
    pallas_call x10, Pallas kernels, sums(): pl.pallas_call(functools.partial(sums_kernel, dims, plan), out_shape=jax....  19 us
    ppermute x4, waiting for transfers between devices, shifted(): return lax.ppermute(value, 'blk', pairs)  16.1 us
    ppermute x4, starting transfers between devices, shifted(): return lax.ppermute(value, 'blk', pairs)  8.6 us
    ppermute x12, starting transfers between devices, swapped(): lax.ppermute(value, 'inner', [(i, i ^ distance) for i in range(count)])  5.33 us
    ppermute x12, waiting for transfers between devices, swapped(): lax.ppermute(value, 'inner', [(i, i ^ distance) for i in range(count)])  3.4 us
    pallas_call x1, Pallas kernels, shards(): pl.pallas_call(functools.partial(pack_kernel, (local_rows, slots, side, s...  1.41 us
    unnamed x4, local copies, waits for them, and re-layouts  1.38 us
  transfers between devices with their start and end apart: 16, of which 6 were waited for; matrix products, arithmetic and copies ran while one was open for 0% of the time, Pallas kernels for 34%

profile of v3, /device:TPU:0, one launch (start us, length us, event | category | flops | bytes accessed | tf_op | source)
XLA Modules:
  0.0 56.7 jit_solution(1000625444599113599)
XLA Ops:
  0.0 0.0 copy-start
  0.0 0.7 %copy-done = s32[2,9,9]{2,0,1:T(2,128)S(1)} copy-done((s32[2,9,9]{2,0,1:T(2,128)S(1)}, s32[2,9,9]{2,0,1:T(2,128)}, u32[]{:S(2)}) %copy-start) | copy-done | bytes 672
  0.7 0.0 copy-start.1
  0.7 0.7 %copy-done.1 = s32[2,9]{1,0:T(2,128)S(1)} copy-done((s32[2,9]{1,0:T(2,128)S(1)}, s32[2,9]{1,0:T(2,128)}, u32[]{:S(2)}) %copy-start.1) | copy-done | bytes 96
  1.4 1.4 %pack.1 = (f32[779,128]{1,0:T(8,128)S(1)}, f32[779,128]{1,0:T(8,128)S(1)}, f32[779,128]{1,0:T(8,128)S(1)}) custom-call(f32[2304,128]{1,0:T(8,128)} %bitcast.4, s32[9,2,9]{2,1,0:T(2,128)S(1)} %bitcast.3, s32[2,9]{1,0:T(2,128)S(1)} %copy-done.1, s32[1]{0:T(128)} %bitcast.2.inner), custom_call_target="tpu_custom_call" | custom-call | tf_op jit(solution)/shard_map/pack/pallas_call | solution.py:173
  2.8 0.5 collective-permute-start.5
  3.3 0.1 collective-permute-start.3
  3.4 0.4 collective-permute-start.6
  3.8 2.6 %collective-permute-start = (f32[779,128]{1,0:T(8,128)S(1)}, f32[779,128]{1,0:T(8,128)S(1)}, u32[]{:S(2)}, u32[]{:S(2)}) collective-permute-start(f32[779,128]{1,0:T(8,128)S(1)} %get-tuple-element.16.refs_0_.refs_4_), channel_id=1, source_target_pairs={{0,2},{1,3},{2,0},{3,1},{4,6},{5,7},{6,4},{7,5},{8,10},{9,11},{10,... | collective-permute-start | bytes 1196552 | tf_op jit(solution)/shard_map/ppermute | solution.py:21
  6.4 4.6 %collective-permute-start.2 = (f32[779,128]{1,0:T(8,128)S(1)}, f32[779,128]{1,0:T(8,128)S(1)}, u32[]{:S(2)}, u32[]{:S(2)}) collective-permute-start(f32[779,128]{1,0:T(8,128)S(1)} %get-tuple-element.18.refs_0_), channel_id=1, source_target_pairs={{0,28},{4,0},{8,4},{12,8},{16,12},{20,16},{24,20},{28,24},{1,29},{... | collective-permute-start | bytes 1196552 | tf_op jit(solution)/shard_map/ppermute | solution.py:16
  10.9 0.0 collective-permute-done.5.refs_1_
  11.0 0.0 collective-permute-done.3.refs_1_.refs_5_
  11.0 0.0 collective-permute-done.6.refs_3_.refs_4_
  11.0 2.5 %sums.12.refs_6_ = f32[2,9,128,128]{3,2,1,0:T(8,128)S(1)} custom-call(f32[779,128]{1,0:T(8,128)S(1)} %get-tuple-element.18.refs_0_, f32[779,128]{1,0:T(8,128)S(1)} %collective-permute-done.5.refs_1_, f32[779,128]{1,0:T(8,128)S(1)} %get-tuple-element.20.refs_2_.refs_3_, f32[779,128]{1,0:T(8,128)S(1)} %collective-permute-done.6.refs_3_.refs_4_, ...), custom_call_target="tpu_custom_call" | custom-call | flops 1 | bytes 1 | tf_op jit(solution)/shard_map/sums/pallas_call | solution.py:198
  13.5 0.6 %collective-permute-start.7 = (f32[779,128]{1,0:T(8,128)S(1)}, f32[779,128]{1,0:T(8,128)S(1)}, u32[]{:S(2)}, u32[]{:S(2)}) collective-permute-start(f32[779,128]{1,0:T(8,128)S(1)} %get-tuple-element.20.refs_2_.refs_3_), channel_id=1, source_target_pairs={{0,2},{1,3},{2,0},{3,1},{4,6},{5,7},{6,4},{7,5},{8,10},{9,11},{10,... | collective-permute-start | bytes 1196552 | tf_op jit(solution)/shard_map/ppermute | solution.py:21
  14.1 2.4 %collective-permute-done = f32[779,128]{1,0:T(8,128)S(1)} collective-permute-done((f32[779,128]{1,0:T(8,128)S(1)}, f32[779,128]{1,0:T(8,128)S(1)}, u32[]{:S(2)}, u32[]{:S(2)}) %collective-permute-start) | collective-permute-done | bytes 398880 | tf_op jit(solution)/shard_map/ppermute | solution.py:21
  16.6 0.1 collective-permute-start.1
  16.6 3.2 %collective-permute-done.2.refs_0_ = f32[779,128]{1,0:T(8,128)S(1)} collective-permute-done((f32[779,128]{1,0:T(8,128)S(1)}, f32[779,128]{1,0:T(8,128)S(1)}, u32[]{:S(2)}, u32[]{:S(2)}) %collective-permute-start.2) | collective-permute-done | bytes 398880 | tf_op jit(solution)/shard_map/ppermute | solution.py:16
  19.8 0.0 collective-permute-start.12
  19.8 2.4 %sums.10.refs_1_ = f32[778,128]{1,0:T(8,128)S(1)} custom-call(f32[779,128]{1,0:T(8,128)S(1)} %get-tuple-element.16.refs_0_.refs_4_, f32[779,128]{1,0:T(8,128)S(1)} %collective-permute-done.3.refs_1_.refs_5_, f32[776,128]{1,0:T(8,128)S(1)} %slice.16.refs_2_.refs_4_), custom_call_target="tpu_custom_call" | custom-call | flops 1 | bytes 1 | tf_op jit(solution)/shard_map/sums/pallas_call | solution.py:198
  22.2 0.0 collective-permute-done.1.refs_0_.refs_5_
  22.2 1.5 %sums.11 = f32[778,128]{1,0:T(8,128)S(1)} custom-call(f32[776,128]{1,0:T(8,128)S(1)} %collective-permute-done.1.refs_0_.refs_5_, f32[778,128]{1,0:T(8,128)S(1)} %sums.10.refs_1_), custom_call_target="tpu_custom_call" | custom-call | flops 1 | bytes 1 | tf_op jit(solution)/shard_map/sums/pallas_call | solution.py:198
  23.7 0.1 collective-permute-start.4
  23.8 0.1 collective-permute-start.9
  23.9 0.9 %collective-permute-done.7 = f32[779,128]{1,0:T(8,128)S(1)} collective-permute-done((f32[779,128]{1,0:T(8,128)S(1)}, f32[779,128]{1,0:T(8,128)S(1)}, u32[]{:S(2)}, u32[]{:S(2)}) %collective-permute-start.7) | collective-permute-done | bytes 398880 | tf_op jit(solution)/shard_map/ppermute | solution.py:21
  24.9 0.1 collective-permute-start.8
  25.0 2.4 %sums.13.refs_2_ = f32[778,128]{1,0:T(8,128)S(1)} custom-call(f32[779,128]{1,0:T(8,128)S(1)} %get-tuple-element.16.refs_0_.refs_4_, f32[779,128]{1,0:T(8,128)S(1)} %collective-permute-done.3.refs_1_.refs_5_, f32[776,128]{1,0:T(8,128)S(1)} %slice.16.refs_2_.refs_4_, f32[779,128]{1,0:T(8,128)S(1)} %get-tuple-element.20.refs_2_.refs_3_, ...), custom_call_target="tpu_custom_call" | custom-call | flops 1 | bytes 1 | tf_op jit(solution)/shard_map/sums/pallas_call | solution.py:198
  27.4 0.0 collective-permute-done.8.refs_1_.refs_3_
  27.4 1.5 %sums.14 = f32[778,128]{1,0:T(8,128)S(1)} custom-call(f32[776,128]{1,0:T(8,128)S(1)} %collective-permute-done.1.refs_0_.refs_5_, f32[776,128]{1,0:T(8,128)S(1)} %collective-permute-done.8.refs_1_.refs_3_, f32[778,128]{1,0:T(8,128)S(1)} %sums.13.refs_2_), custom_call_target="tpu_custom_call" | custom-call | flops 1 | bytes 1 | tf_op jit(solution)/shard_map/sums/pallas_call | solution.py:198
  28.9 0.0 collective-permute-done.12.refs_1_
  28.9 0.8 %collective-permute-start.13 = (f32[779,128]{1,0:T(8,128)S(1)}, f32[779,128]{1,0:T(8,128)S(1)}, u32[]{:S(2)}, u32[]{:S(2)}) collective-permute-start(f32[779,128]{1,0:T(8,128)S(1)} %collective-permute-done.2.refs_0_), channel_id=1, source_target_pairs={{0,2},{1,3},{2,0},{3,1},{4,6},{5,7},{6,4},{7,5},{8,10},{9,11},{10,... | collective-permute-start | bytes 1196552 | tf_op jit(solution)/shard_map/ppermute | solution.py:21
  29.7 2.0 %collective-permute-start.11 = (f32[778,128]{1,0:T(8,128)S(1)}, f32[778,128]{1,0:T(8,128)S(1)}, u32[]{:S(2)}, u32[]{:S(2)}) collective-permute-start(f32[778,128]{1,0:T(8,128)S(1)} %sums.14), channel_id=1, source_target_pairs={{0,4},{4,8},{8,12},{12,16},{16,20},{20,24},{24,28},{28,0},{1,5},{5... | collective-permute-start | bytes 1195016 | tf_op jit(solution)/shard_map/ppermute | solution.py:16
  31.6 8.0 %collective-permute-done.9.middle = f32[778,128]{1,0:T(8,128)S(1)} collective-permute-done((f32[778,128]{1,0:T(8,128)S(1)}, f32[778,128]{1,0:T(8,128)S(1)}, u32[]{:S(2)}, u32[]{:S(2)}) %collective-permute-start.9) | collective-permute-done | bytes 398368 | tf_op jit(solution)/shard_map/ppermute | solution.py:16
  39.7 0.0 collective-permute-done.4
  39.7 0.1 collective-permute-start.10
  39.8 1.9 %sums.16.refs_2_ = f32[778,128]{1,0:T(8,128)S(1)} custom-call(f32[779,128]{1,0:T(8,128)S(1)} %get-tuple-element.18.refs_0_, f32[779,128]{1,0:T(8,128)S(1)} %collective-permute-done.5.refs_1_, f32[776,128]{1,0:T(8,128)S(1)} %slice.14.refs_0_.refs_2_, f32[779,128]{1,0:T(8,128)S(1)} %get-tuple-element.20.refs_2_.refs_3_, ...), custom_call_target="tpu_custom_call" | custom-call | flops 1 | bytes 1 | tf_op jit(solution)/shard_map/sums/pallas_call | solution.py:198
  41.7 0.0 collective-permute-done.10.refs_1_.refs_0_
  41.7 0.7 %sums.17 = f32[778,128]{1,0:T(8,128)S(1)} custom-call(f32[776,128]{1,0:T(8,128)S(1)} %collective-permute-done.10.refs_1_.refs_0_, f32[776,128]{1,0:T(8,128)S(1)} %collective-permute-done.8.refs_1_.refs_3_, f32[778,128]{1,0:T(8,128)S(1)} %sums.16.refs_2_), custom_call_target="tpu_custom_call" | custom-call | flops 1 | bytes 1 | tf_op jit(solution)/shard_map/sums/pallas_call | solution.py:198
  42.4 1.9 %collective-permute-start.15 = (f32[778,128]{1,0:T(8,128)S(1)}, f32[778,128]{1,0:T(8,128)S(1)}, u32[]{:S(2)}, u32[]{:S(2)}) collective-permute-start(f32[778,128]{1,0:T(8,128)S(1)} %sums.17), channel_id=1, source_target_pairs={{0,28},{4,0},{8,4},{12,8},{16,12},{20,16},{24,20},{28,24},{1,29},{... | collective-permute-start | bytes 1195016 | tf_op jit(solution)/shard_map/ppermute | solution.py:16
  44.3 2.1 %sums.15.base = f32[2,9,128,128]{3,2,1,0:T(8,128)S(1)} custom-call(f32[776,128]{1,0:T(8,128)S(1)} %slice.14.refs_0_.refs_2_, f32[776,128]{1,0:T(8,128)S(1)} %collective-permute-done.10.refs_1_.refs_0_, f32[776,128]{1,0:T(8,128)S(1)} %slice.13.refs_5_.refs_2_, f32[776,128]{1,0:T(8,128)S(1)} %collective-permute-done.8.refs_1_.refs_3_, ...), custom_call_target="tpu_custom_call" | custom-call | flops 1 | bytes 1 | tf_op jit(solution)/shard_map/sums/pallas_call | solution.py:198
  46.4 3.7 %collective-permute-done.11.lower = f32[778,128]{1,0:T(8,128)S(1)} collective-permute-done((f32[778,128]{1,0:T(8,128)S(1)}, f32[778,128]{1,0:T(8,128)S(1)}, u32[]{:S(2)}, u32[]{:S(2)}) %collective-permute-start.11) | collective-permute-done | bytes 398368 | tf_op jit(solution)/shard_map/ppermute | solution.py:16
  50.1 0.0 collective-permute-done.13
  50.1 0.1 collective-permute-start.14
  50.2 2.9 %sums.18.refs_1_ = f32[778,128]{1,0:T(8,128)S(1)} custom-call(f32[779,128]{1,0:T(8,128)S(1)} %collective-permute-done.2.refs_0_, f32[779,128]{1,0:T(8,128)S(1)} %collective-permute-done.12.refs_1_, f32[776,128]{1,0:T(8,128)S(1)} %slice.15.refs_2_), custom_call_target="tpu_custom_call" | custom-call | flops 1 | bytes 1 | tf_op jit(solution)/shard_map/sums/pallas_call | solution.py:198
  53.1 0.0 collective-permute-done.14.refs_0_
  53.1 1.2 %sums.19.own_middle = f32[778,128]{1,0:T(8,128)S(1)} custom-call(f32[776,128]{1,0:T(8,128)S(1)} %collective-permute-done.14.refs_0_, f32[778,128]{1,0:T(8,128)S(1)} %sums.18.refs_1_), custom_call_target="tpu_custom_call" | custom-call | flops 1 | bytes 1 | tf_op jit(solution)/shard_map/sums/pallas_call | solution.py:198
  54.4 1.2 %collective-permute-done.15.upper = f32[778,128]{1,0:T(8,128)S(1)} collective-permute-done((f32[778,128]{1,0:T(8,128)S(1)}, f32[778,128]{1,0:T(8,128)S(1)}, u32[]{:S(2)}, u32[]{:S(2)}) %collective-permute-start.15) | collective-permute-done | bytes 398368 | tf_op jit(solution)/shard_map/ppermute | solution.py:16
  55.6 1.1 %finish.1 = f32[2,9,128,128]{3,2,1,0:T(8,128)} custom-call(f32[2,9,128,128]{3,2,1,0:T(8,128)S(1)} %sums.15.base, f32[778,128]{1,0:T(8,128)S(1)} %collective-permute-done.11.lower, f32[778,128]{1,0:T(8,128)S(1)} %collective-permute-done.9.middle, f32[778,128]{1,0:T(8,128)S(1)} %sums.19.own_middle, f32[778,128]{1,0:T(8,128)S(1)} %collective-permute-done.15.upper), custom_call_target="tpu_custom_call" | custom-call | flops 1 | bytes 1 | tf_op jit(solution)/shard_map/finish/pallas_call | solution.py:261
  (4 shorter events, 0.1 us)
Async XLA Ops:
  0.0 0.7 %copy-start = (s32[2,9,9]{2,0,1:T(2,128)S(1)}, s32[2,9,9]{2,0,1:T(2,128)}, u32[]{:S(2)}) copy-start(s32[2,9,9]{2,0,1:T(2,128)} %param.5) | copy-start | bytes 1948
  0.7 0.7 %copy-start.1 = (s32[2,9]{1,0:T(2,128)S(1)}, s32[2,9]{1,0:T(2,128)}, u32[]{:S(2)}) copy-start(s32[2,9]{1,0:T(2,128)} %cols.1) | copy-start | bytes 220
  2.8 8.2 %collective-permute-start.5 = (f32[779,128]{1,0:T(8,128)S(1)}, f32[779,128]{1,0:T(8,128)S(1)}, u32[]{:S(2)}, u32[]{:S(2)}) collective-permute-start(f32[779,128]{1,0:T(8,128)S(1)} %get-tuple-element.18.refs_0_), channel_id=1, source_target_pairs={{0,1},{1,0},{2,3},{3,2},{4,5},{5,4},{6,7},{7,6},{8,9},{9,8},{10,11... | collective-permute-start | bytes 1196552 | tf_op jit(solution)/shard_map/ppermute | solution.py:21
  3.3 7.6 %collective-permute-start.3 = (f32[779,128]{1,0:T(8,128)S(1)}, f32[779,128]{1,0:T(8,128)S(1)}, u32[]{:S(2)}, u32[]{:S(2)}) collective-permute-start(f32[779,128]{1,0:T(8,128)S(1)} %get-tuple-element.16.refs_0_.refs_4_), channel_id=1, source_target_pairs={{0,1},{1,0},{2,3},{3,2},{4,5},{5,4},{6,7},{7,6},{8,9},{9,8},{10,11... | collective-permute-start | bytes 1196552 | tf_op jit(solution)/shard_map/ppermute | solution.py:21
  3.4 7.6 %collective-permute-start.6 = (f32[779,128]{1,0:T(8,128)S(1)}, f32[779,128]{1,0:T(8,128)S(1)}, u32[]{:S(2)}, u32[]{:S(2)}) collective-permute-start(f32[779,128]{1,0:T(8,128)S(1)} %get-tuple-element.20.refs_2_.refs_3_), channel_id=1, source_target_pairs={{0,1},{1,0},{2,3},{3,2},{4,5},{5,4},{6,7},{7,6},{8,9},{9,8},{10,11... | collective-permute-start | bytes 1196552 | tf_op jit(solution)/shard_map/ppermute | solution.py:21
  3.8 12.7 %collective-permute-start = (f32[779,128]{1,0:T(8,128)S(1)}, f32[779,128]{1,0:T(8,128)S(1)}, u32[]{:S(2)}, u32[]{:S(2)}) collective-permute-start(f32[779,128]{1,0:T(8,128)S(1)} %get-tuple-element.16.refs_0_.refs_4_), channel_id=1, source_target_pairs={{0,2},{1,3},{2,0},{3,1},{4,6},{5,7},{6,4},{7,5},{8,10},{9,11},{10,... | collective-permute-start | bytes 1196552 | tf_op jit(solution)/shard_map/ppermute | solution.py:21
  6.4 13.4 %collective-permute-start.2 = (f32[779,128]{1,0:T(8,128)S(1)}, f32[779,128]{1,0:T(8,128)S(1)}, u32[]{:S(2)}, u32[]{:S(2)}) collective-permute-start(f32[779,128]{1,0:T(8,128)S(1)} %get-tuple-element.18.refs_0_), channel_id=1, source_target_pairs={{0,28},{4,0},{8,4},{12,8},{16,12},{20,16},{24,20},{28,24},{1,29},{... | collective-permute-start | bytes 1196552 | tf_op jit(solution)/shard_map/ppermute | solution.py:16
  13.5 11.4 %collective-permute-start.7 = (f32[779,128]{1,0:T(8,128)S(1)}, f32[779,128]{1,0:T(8,128)S(1)}, u32[]{:S(2)}, u32[]{:S(2)}) collective-permute-start(f32[779,128]{1,0:T(8,128)S(1)} %get-tuple-element.20.refs_2_.refs_3_), channel_id=1, source_target_pairs={{0,2},{1,3},{2,0},{3,1},{4,6},{5,7},{6,4},{7,5},{8,10},{9,11},{10,... | collective-permute-start | bytes 1196552 | tf_op jit(solution)/shard_map/ppermute | solution.py:21
  16.6 5.7 %collective-permute-start.1 = (f32[776,128]{1,0:T(8,128)S(1)}, f32[776,128]{1,0:T(8,128)S(1)}, u32[]{:S(2)}, u32[]{:S(2)}) collective-permute-start(f32[776,128]{1,0:T(8,128)S(1)} %slice.16.refs_2_.refs_4_), channel_id=1, source_target_pairs={{0,1},{1,0},{2,3},{3,2},{4,5},{5,4},{6,7},{7,6},{8,9},{9,8},{10,11... | collective-permute-start | bytes 1191944 | tf_op jit(solution)/shard_map/ppermute | solution.py:21
  19.8 9.1 %collective-permute-start.12 = (f32[779,128]{1,0:T(8,128)S(1)}, f32[779,128]{1,0:T(8,128)S(1)}, u32[]{:S(2)}, u32[]{:S(2)}) collective-permute-start(f32[779,128]{1,0:T(8,128)S(1)} %collective-permute-done.2.refs_0_), channel_id=1, source_target_pairs={{0,1},{1,0},{2,3},{3,2},{4,5},{5,4},{6,7},{7,6},{8,9},{9,8},{10,11... | collective-permute-start | bytes 1196552 | tf_op jit(solution)/shard_map/ppermute | solution.py:21
  23.7 16.0 %collective-permute-start.4 = (f32[779,128]{1,0:T(8,128)S(1)}, f32[779,128]{1,0:T(8,128)S(1)}, u32[]{:S(2)}, u32[]{:S(2)}) collective-permute-start(f32[779,128]{1,0:T(8,128)S(1)} %get-tuple-element.18.refs_0_), channel_id=1, source_target_pairs={{0,2},{1,3},{2,0},{3,1},{4,6},{5,7},{6,4},{7,5},{8,10},{9,11},{10,... | collective-permute-start | bytes 1196552 | tf_op jit(solution)/shard_map/ppermute | solution.py:21
  23.8 15.9 %collective-permute-start.9 = (f32[778,128]{1,0:T(8,128)S(1)}, f32[778,128]{1,0:T(8,128)S(1)}, u32[]{:S(2)}, u32[]{:S(2)}) collective-permute-start(f32[778,128]{1,0:T(8,128)S(1)} %sums.11), channel_id=1, source_target_pairs={{0,4},{4,8},{8,12},{12,16},{16,20},{20,24},{24,28},{28,0},{1,5},{5... | collective-permute-start | bytes 1195016 | tf_op jit(solution)/shard_map/ppermute | solution.py:16
  24.9 2.5 %collective-permute-start.8 = (f32[776,128]{1,0:T(8,128)S(1)}, f32[776,128]{1,0:T(8,128)S(1)}, u32[]{:S(2)}, u32[]{:S(2)}) collective-permute-start(f32[776,128]{1,0:T(8,128)S(1)} %slice.13.refs_5_.refs_2_), channel_id=1, source_target_pairs={{0,1},{1,0},{2,3},{3,2},{4,5},{5,4},{6,7},{7,6},{8,9},{9,8},{10,11... | collective-permute-start | bytes 1191944 | tf_op jit(solution)/shard_map/ppermute | solution.py:21
  28.9 21.2 %collective-permute-start.13 = (f32[779,128]{1,0:T(8,128)S(1)}, f32[779,128]{1,0:T(8,128)S(1)}, u32[]{:S(2)}, u32[]{:S(2)}) collective-permute-start(f32[779,128]{1,0:T(8,128)S(1)} %collective-permute-done.2.refs_0_), channel_id=1, source_target_pairs={{0,2},{1,3},{2,0},{3,1},{4,6},{5,7},{6,4},{7,5},{8,10},{9,11},{10,... | collective-permute-start | bytes 1196552 | tf_op jit(solution)/shard_map/ppermute | solution.py:21
  29.7 20.4 %collective-permute-start.11 = (f32[778,128]{1,0:T(8,128)S(1)}, f32[778,128]{1,0:T(8,128)S(1)}, u32[]{:S(2)}, u32[]{:S(2)}) collective-permute-start(f32[778,128]{1,0:T(8,128)S(1)} %sums.14), channel_id=1, source_target_pairs={{0,4},{4,8},{8,12},{12,16},{16,20},{20,24},{24,28},{28,0},{1,5},{5... | collective-permute-start | bytes 1195016 | tf_op jit(solution)/shard_map/ppermute | solution.py:16
  39.7 1.9 %collective-permute-start.10 = (f32[776,128]{1,0:T(8,128)S(1)}, f32[776,128]{1,0:T(8,128)S(1)}, u32[]{:S(2)}, u32[]{:S(2)}) collective-permute-start(f32[776,128]{1,0:T(8,128)S(1)} %slice.14.refs_0_.refs_2_), channel_id=1, source_target_pairs={{0,1},{1,0},{2,3},{3,2},{4,5},{5,4},{6,7},{7,6},{8,9},{9,8},{10,11... | collective-permute-start | bytes 1191944 | tf_op jit(solution)/shard_map/ppermute | solution.py:21
  42.4 13.2 %collective-permute-start.15 = (f32[778,128]{1,0:T(8,128)S(1)}, f32[778,128]{1,0:T(8,128)S(1)}, u32[]{:S(2)}, u32[]{:S(2)}) collective-permute-start(f32[778,128]{1,0:T(8,128)S(1)} %sums.17), channel_id=1, source_target_pairs={{0,28},{4,0},{8,4},{12,8},{16,12},{20,16},{24,20},{28,24},{1,29},{... | collective-permute-start | bytes 1195016 | tf_op jit(solution)/shard_map/ppermute | solution.py:16
  50.1 3.0 %collective-permute-start.14 = (f32[776,128]{1,0:T(8,128)S(1)}, f32[776,128]{1,0:T(8,128)S(1)}, u32[]{:S(2)}, u32[]{:S(2)}) collective-permute-start(f32[776,128]{1,0:T(8,128)S(1)} %slice.15.refs_2_), channel_id=1, source_target_pairs={{0,1},{1,0},{2,3},{3,2},{4,5},{5,4},{6,7},{7,6},{8,9},{9,8},{10,11... | collective-permute-start | bytes 1191944 | tf_op jit(solution)/shard_map/ppermute | solution.py:21

commit v4 on v3

--- a/solution.py
+++ b/solution.py
@@ -14,6 +14,18 @@
     count = lax.axis_size("blk")
     pairs = [(source, (source + steps) % count) for source in range(count)]
     return lax.ppermute(value, "blk", pairs)
+
+
+def shifted_aslant(value, steps):
+    count, width = lax.axis_size("blk"), lax.axis_size("inner")
+    if width == 1:
+        return shifted(value, steps)
+    pairs = [
+        (s * width + i, (s + steps) % count * width + (i ^ 1))
+        for s in range(count)
+        for i in range(width)
+    ]
+    return lax.ppermute(value, ("blk", "inner"), pairs)
 
 
 def swapped(value, distance):
@@ -77,6 +89,48 @@
         copy.wait()
 
 
+def cut(block):
+    high = block.astype(jnp.bfloat16)
+    return high, (block - high.astype(jnp.float32)).astype(jnp.bfloat16)
+
+
+def multiplied(a, blocks):
+    a_high, a_low = cut(a)
+    b_high, b_low = cut(jnp.concatenate(blocks, axis=1))
+    a = jnp.concatenate([a_high, a_high, a_low], axis=0)
+    b = jnp.concatenate([b_high, b_low, b_high], axis=0)
+    return lax.dot_general(a, b, TN, preferred_element_type=jnp.float32)
+
+
+def partial_kernel(dims, below, above, *refs):
+    parts, local_rows, slots, side, meta_rows = dims
+    per = slots // 3
+    data = local_rows * per * side
+    outs, (meta, acc, meta_sems) = refs[:parts], refs[parts:]
+    fetches = []
+    for index, payload in enumerate((below, above)):
+        source = payload.at[pl.ds(data, meta_rows)]
+        fetches.append(pltpu.make_async_copy(source, meta.at[index], meta_sems.at[index]))
+        fetches[-1].start()
+    acc[...] = jnp.zeros_like(acc)
+    for index, (payload, lane) in enumerate(((below, 2 * per), (above, 0))):
+        fetches[index].wait()
+        for line in range(local_rows * per):
+            first = line // per * per
+            blocks = [payload[t * side : (t + 1) * side, :] for t in range(first, first + per)]
+            result = multiplied(payload[line * side : (line + 1) * side, :], blocks)
+            dest = meta[index, line, slots].astype(jnp.int32)
+            for t in range(per):
+                target = meta[index, line, lane + t].astype(jnp.int32)
+                place = jnp.minimum(target - per, per)
+                acc[dest, place] += result[:, t * side : (t + 1) * side]
+    for part in range(parts):
+        for row in range(local_rows):
+            for t in range(per):
+                start = (row * per + t) * side
+                outs[part][start : start + side, :] = acc[part * local_rows + row, t]
+
+
 def sums_kernel(dims, plan, *refs):
     offset, parts, local_rows, slots, side, meta_rows, a_at, group_total, first, width = dims
     per = slots // 3
@@ -90,10 +144,6 @@
         fetches.append(pltpu.make_async_copy(source, meta.at[part], meta_sems.at[part]))
         fetches[-1].start()
     acc[...] = jnp.zeros_like(acc)
-
-    def cut(block):
-        high = block.astype(jnp.bfloat16)
-        return high, (block - high.astype(jnp.float32)).astype(jnp.bfloat16)
 
     for part in range(parts):
         fetches[part].wait()
@@ -109,16 +159,13 @@
         def multiply(item, _, part=part):
             line, row, dest = listed[0, item], listed[1, item], listed[2, item]
             start = pl.multiple_of(line * side, side)
-            a_high, a_low = cut(payloads[a_at][part][pl.ds(start, side), :])
-            a = jnp.concatenate([a_high, a_high, a_low], axis=0)
+            a = payloads[a_at][part][pl.ds(start, side), :]
             for group, lane in plan:
                 blocks = []
                 for t in range(per):
                     start = pl.multiple_of((row * per + t) * side, side)
                     blocks.append(payloads[group][part][pl.ds(start, side), :])
-                b_high, b_low = cut(jnp.concatenate(blocks, axis=1))
-                b = jnp.concatenate([b_high, b_low, b_high], axis=0)
-                result = lax.dot_general(a, b, TN, preferred_element_type=jnp.float32)
+                result = multiplied(a, blocks)
                 for t in range(per):
                     target = meta[part, line, lane + t].astype(jnp.int32)
                     place = jnp.minimum(target - first, width)
@@ -140,7 +187,8 @@
                 out[lines, :] = base[0][lines, :] + acc[row, t] if base else acc[row, t]
 
 
-def finish_kernel(base, lower, middle, own_middle, upper, out, result, sems):
+def finish_kernel(base, lower, upper, *refs):
+    middles, (out, result, sems) = refs[:-3], refs[-3:]
     local_rows, slots, side, _ = base.shape
     per = slots // 3
     copies = []
@@ -149,8 +197,8 @@
             start = (row * per + slot) * side
             lines = slice(start, start + side)
             result[row, slot] = base[row, slot] - lower[lines, :]
-            both = middle[lines, :] + own_middle[lines, :]
-            result[row, per + slot] = base[row, per + slot] - both
+            total = sum(middle[lines, :] for middle in middles)
+            result[row, per + slot] = base[row, per + slot] - total
             result[row, 2 * per + slot] = base[row, 2 * per + slot] - upper[lines, :]
         copies.append(pltpu.make_async_copy(result.at[row], out.at[row], sems.at[row]))
         copies[-1].start()
@@ -228,40 +276,59 @@
     def tied(values, *after):
         return list(lax.optimization_barrier((*values, *after)))[: len(values)]
 
+    def partials(below, above):
+        return pl.pallas_call(
+            functools.partial(partial_kernel, (parts, local_rows, slots, side, meta_rows)),
+            out_shape=[
+                jax.ShapeDtypeStruct((local_rows * per * side + spare, side), jnp.float32)
+            ] * parts,
+            in_specs=[vectors] * 2,
+            out_specs=[vectors] * parts,
+            scratch_shapes=[
+                pltpu.SMEM((2, meta_rows, side), jnp.float32),
+                pltpu.VMEM((strip_rows, per + 1, side, side), jnp.float32),
+                pltpu.SemaphoreType.DMA((2,)),
+            ],
+            compiler_params=pltpu.CompilerParams(vmem_limit_bytes=16 << 20),
+            cost_estimate=pl.CostEstimate(flops=1, bytes_accessed=1, transcendentals=0),
+            name="partials",
+        )(below, above)
+
     own_plan = ((0, 0), (1, per), (2, 2 * per))
-    above = shifted(lower, -1)
+    below, above = shifted(upper, 1), shifted(lower, -1)
     lowers, middles, uppers = halves(lower), halves(middle), halves(upper)
-    far_upper = across(upper)
+    far_middle = across(middle)
     base = sums([lowers, middles, uppers], 1, own_plan, 0, slots)
 
-    far_middle = across(middle, [base])
+    far_upper = across(upper, [base])
+    far_middles = spread(far_middle)
+    far_lower = across(lower, [*far_middles, below, above])
+    all_middles = middles + far_middles
     far_uppers = spread(far_upper)
-    far_uppers = far_uppers[:1] + [tied([one], above)[0] for one in far_uppers[1:]]
-    below_own = strip_sums([uppers + far_uppers], 0, ((0, 2 * per),), per)
-
-    far_lower = across(lower, [below_own])
-    to_below_own = shifted(below_own, 1)
-    far_middles = spread(tied(far_middle, below_own))
-    all_middles = middles + far_middles
     below_next = strip_sums([uppers + far_uppers, all_middles], 0, ((1, per),), 0)
-
-    aboves = halves(above)
-    far_above = across(above, [below_next, *aboves])
-    to_below_next = shifted(below_next, 1)
-    far_lowers = spread(tied(far_lower, below_next, to_below_own))
+    to_below_next = shifted_aslant(below_next, 1)
+
+    shares = dict(enumerate(partials(below, above)))
+    for bit in [1 << i for i in range(20) if (1 << i) < parts // 2]:
+        shares = {
+            distance: share + swapped(shares[distance ^ bit], bit)
+            for distance, share in shares.items()
+            if not distance & bit
+        }
+    far_share = across(shares[parts // 2], [below_next]) if parts > 1 else []
+    far_lowers = spread(tied(far_lower, below_next)) if far_lower else []
     above_next = strip_sums([lowers + far_lowers, all_middles], 0, ((1, per),), 2 * per)
     to_above_next = shifted(above_next, -1)
     if far_lowers:
         near = len(lowers)
         groups = [far_lowers, far_middles, far_uppers]
         base = sums(groups, 1, own_plan, 0, slots, near, [base])
-        far_above = tied(far_above, base, above_next, to_below_next)
-    aboves = aboves + spread(far_above)
-    from_above = strip_sums([aboves], 0, ((0, 0),), per)
+        to_below_next = swapped(to_below_next, 1)
+    middle_shares = [shares[0], *far_share]
     return pl.pallas_call(
         finish_kernel,
         out_shape=jax.ShapeDtypeStruct(density.shape, jnp.float32),
-        in_specs=[vectors] * 5,
+        in_specs=[vectors] * (3 + len(middle_shares)),
         out_specs=in_hbm,
         scratch_shapes=[
             pltpu.VMEM(density.shape, jnp.float32),
@@ -270,7 +337,7 @@
         compiler_params=pltpu.CompilerParams(vmem_limit_bytes=16 << 20),
         cost_estimate=pl.CostEstimate(flops=1, bytes_accessed=1, transcendentals=0),
         name="finish",
-    )(base, to_below_next, to_below_own, from_above, to_above_next)
+    )(base, to_below_next, to_above_next, *middle_shares)
 
 
 def solution(mesh):

time: 56.8 us -> 57.5 us (1.012)
  Pallas kernels: 21.6 us -> 14.7 us
  starting transfers between devices: 13.9 us -> 18.2 us
  waiting for transfers between devices: 19.5 us -> 22.6 us
    pallas_call x10 -> x6, Pallas kernels: 19 us -> 10.3 us  [sums(): pl.pallas_call(functools.partial(sums_kernel, dims, plan), out_shape=jax....]
    ppermute x0 -> x1, starting transfers between devices: none -> 2.15 us  [shifted_aslant(): return lax.ppermute(value, ('blk', 'inner'), pairs)]
    pallas_call x0 -> x1, Pallas kernels: none -> 1.94 us  [partials(): pl.pallas_call(functools.partial(partial_kernel, (parts, local_rows, slot...]
    ppermute x12 -> x13, starting transfers between devices: 5.33 us -> 7.01 us  [swapped(): lax.ppermute(value, 'inner', [(i, i ^ distance) for i in range(count)])]
    ppermute x12 -> x13, waiting for transfers between devices: 3.4 us -> 4.9 us  [swapped(): lax.ppermute(value, 'inner', [(i, i ^ distance) for i in range(count)])]
    ppermute x0 -> x1, waiting for transfers between devices: none -> 1.35 us  [shifted_aslant(): return lax.ppermute(value, ('blk', 'inner'), pairs)]
    ppermute x4 -> x3, starting transfers between devices: 8.6 us -> 9.09 us  [shifted(): return lax.ppermute(value, 'blk', pairs)]
    ppermute x4 -> x3, waiting for transfers between devices: 16.1 us -> 16.4 us  [shifted(): return lax.ppermute(value, 'blk', pairs)]
  transfers between devices with their start and end apart: 16 -> 17, of which waited for: 6 -> 6; matrix products, arithmetic and copies ran while one was open for 0% -> 0% of each run, Pallas kernels for 34% -> 21%
where the time goes in v4:
time: 57.5 us; the launch traced here: 57.3 us
  waiting for transfers between devices  22.6 us (39%)
  starting transfers between devices  18.2 us (32%)
  Pallas kernels  14.7 us (26%)
  local copies, waits for them, and re-layouts  1.46 us (3%)
    ppermute x3, waiting for transfers between devices, shifted(): return lax.ppermute(value, 'blk', pairs)  16.4 us
    pallas_call x6, Pallas kernels, sums(): pl.pallas_call(functools.partial(sums_kernel, dims, plan), out_shape=jax....  10.3 us
    ppermute x3, starting transfers between devices, shifted(): return lax.ppermute(value, 'blk', pairs)  9.09 us
    ppermute x13, starting transfers between devices, swapped(): lax.ppermute(value, 'inner', [(i, i ^ distance) for i in range(count)])  7.01 us
    ppermute x13, waiting for transfers between devices, swapped(): lax.ppermute(value, 'inner', [(i, i ^ distance) for i in range(count)])  4.9 us
    ppermute x1, starting transfers between devices, shifted_aslant(): return lax.ppermute(value, ('blk', 'inner'), pairs)  2.15 us
    pallas_call x1, Pallas kernels, partials(): pl.pallas_call(functools.partial(partial_kernel, (parts, local_rows, slot...  1.94 us
    pallas_call x1, Pallas kernels, shards(): pl.pallas_call(functools.partial(pack_kernel, (local_rows, slots, side, s...  1.41 us
  transfers between devices with their start and end apart: 17, of which 6 were waited for; matrix products, arithmetic and copies ran while one was open for 0% of the time, Pallas kernels for 21%

profile of v4, /device:TPU:0, one launch (start us, length us, event | category | flops | bytes accessed | tf_op | source)
XLA Modules:
  0.0 57.3 jit_solution(9442066651646949903)
XLA Ops:
  0.0 0.0 copy-start
  0.0 0.7 %copy-done = s32[2,9,9]{2,0,1:T(2,128)S(1)} copy-done((s32[2,9,9]{2,0,1:T(2,128)S(1)}, s32[2,9,9]{2,0,1:T(2,128)}, u32[]{:S(2)}) %copy-start) | copy-done | bytes 672
  0.7 0.0 copy-start.1
  0.7 0.7 %copy-done.1 = s32[2,9]{1,0:T(2,128)S(1)} copy-done((s32[2,9]{1,0:T(2,128)S(1)}, s32[2,9]{1,0:T(2,128)}, u32[]{:S(2)}) %copy-start.1) | copy-done | bytes 96
  1.4 1.4 %pack.1 = (f32[779,128]{1,0:T(8,128)S(1)}, f32[779,128]{1,0:T(8,128)S(1)}, f32[779,128]{1,0:T(8,128)S(1)}) custom-call(f32[2304,128]{1,0:T(8,128)} %bitcast.4, s32[9,2,9]{2,1,0:T(2,128)S(1)} %bitcast.3, s32[2,9]{1,0:T(2,128)S(1)} %copy-done.1, s32[1]{0:T(128)} %bitcast.2.inner), custom_call_target="tpu_custom_call" | custom-call | tf_op jit(solution)/shard_map/pack/pallas_call | solution.py:221
  2.8 0.5 collective-permute-start.5
  3.3 0.1 collective-permute-start.6
  3.4 0.4 collective-permute-start.7
  3.8 2.6 %collective-permute-start = (f32[779,128]{1,0:T(8,128)S(1)}, f32[779,128]{1,0:T(8,128)S(1)}, u32[]{:S(2)}, u32[]{:S(2)}) collective-permute-start(f32[779,128]{1,0:T(8,128)S(1)} %get-tuple-element.17.refs_2_.refs_3_), channel_id=1, source_target_pairs={{0,2},{1,3},{2,0},{3,1},{4,6},{5,7},{6,4},{7,5},{8,10},{9,11},{10,... | collective-permute-start | bytes 1196552 | tf_op jit(solution)/shard_map/ppermute | solution.py:33
  6.4 4.6 %collective-permute-start.3 = (f32[779,128]{1,0:T(8,128)S(1)}, f32[779,128]{1,0:T(8,128)S(1)}, u32[]{:S(2)}, u32[]{:S(2)}) collective-permute-start(f32[779,128]{1,0:T(8,128)S(1)} %get-tuple-element.19.refs_0_), channel_id=1, source_target_pairs={{0,28},{4,0},{8,4},{12,8},{16,12},{20,16},{24,20},{28,24},{1,29},{... | collective-permute-start | bytes 1196552 | tf_op jit(solution)/shard_map/ppermute | solution.py:16
  10.9 0.0 collective-permute-done.5.refs_1_
  11.0 0.0 collective-permute-start.2
  11.0 0.0 collective-permute-done.6.refs_3_.refs_4_
  11.0 0.0 collective-permute-done.7.refs_5_.refs_1_
  11.0 2.5 %sums.6.refs_6_ = f32[2,9,128,128]{3,2,1,0:T(8,128)S(1)} custom-call(f32[779,128]{1,0:T(8,128)S(1)} %get-tuple-element.19.refs_0_, f32[779,128]{1,0:T(8,128)S(1)} %collective-permute-done.5.refs_1_, f32[779,128]{1,0:T(8,128)S(1)} %get-tuple-element.17.refs_2_.refs_3_, f32[779,128]{1,0:T(8,128)S(1)} %collective-permute-done.6.refs_3_.refs_4_, ...), custom_call_target="tpu_custom_call" | custom-call | flops 1 | bytes 1 | tf_op jit(solution)/shard_map/sums/pallas_call | solution.py:246
  13.5 1.0 %collective-permute-start.8 = (f32[779,128]{1,0:T(8,128)S(1)}, f32[779,128]{1,0:T(8,128)S(1)}, u32[]{:S(2)}, u32[]{:S(2)}) collective-permute-start(f32[779,128]{1,0:T(8,128)S(1)} %get-tuple-element.20.refs_4_.refs_0_), channel_id=1, source_target_pairs={{0,2},{1,3},{2,0},{3,1},{4,6},{5,7},{6,4},{7,5},{8,10},{9,11},{10,... | collective-permute-start | bytes 1196552 | tf_op jit(solution)/shard_map/ppermute | solution.py:33
  14.5 2.0 %collective-permute-done = f32[779,128]{1,0:T(8,128)S(1)} collective-permute-done((f32[779,128]{1,0:T(8,128)S(1)}, f32[779,128]{1,0:T(8,128)S(1)}, u32[]{:S(2)}, u32[]{:S(2)}) %collective-permute-start) | collective-permute-done | bytes 398880 | tf_op jit(solution)/shard_map/ppermute | solution.py:33
  16.6 0.1 collective-permute-start.1
  16.6 9.7 %collective-permute-done.3.above = f32[779,128]{1,0:T(8,128)S(1)} collective-permute-done((f32[779,128]{1,0:T(8,128)S(1)}, f32[779,128]{1,0:T(8,128)S(1)}, u32[]{:S(2)}, u32[]{:S(2)}) %collective-permute-start.3) | collective-permute-done | bytes 398880 | tf_op jit(solution)/shard_map/ppermute | solution.py:16
  26.4 0.0 collective-permute-done.2.below
  26.4 0.0 collective-permute-done.1.refs_1_.refs_3_
  26.4 0.5 collective-permute-start.4
  26.8 0.0 collective-permute-done.8
  26.9 0.1 collective-permute-start.9
  27.0 1.9 %partials.1 = (f32[778,128]{1,0:T(8,128)S(1)}, f32[778,128]{1,0:T(8,128)S(1)}, f32[778,128]{1,0:T(8,128)S(1)}, f32[778,128]{1,0:T(8,128)S(1)}) custom-call(f32[779,128]{1,0:T(8,128)S(1)} %collective-permute-done.2.below, f32[779,128]{1,0:T(8,128)S(1)} %collective-permute-done.3.above), custom_call_target="tpu_custom_call" | custom-call | flops 1 | bytes 1 | tf_op jit(solution)/shard_map/partials/pallas_call | solution.py:280
  28.9 0.6 collective-permute-start.15
  29.5 2.4 %sums.7.refs_2_ = f32[778,128]{1,0:T(8,128)S(1)} custom-call(f32[779,128]{1,0:T(8,128)S(1)} %get-tuple-element.20.refs_4_.refs_0_, f32[779,128]{1,0:T(8,128)S(1)} %collective-permute-done.7.refs_5_.refs_1_, f32[776,128]{1,0:T(8,128)S(1)} %slice.13.refs_2_.refs_4_, f32[779,128]{1,0:T(8,128)S(1)} %get-tuple-element.17.refs_2_.refs_3_, ...), custom_call_target="tpu_custom_call" | custom-call | flops 1 | bytes 1 | tf_op jit(solution)/shard_map/sums/pallas_call | solution.py:246
  31.9 0.0 collective-permute-done.9.refs_0_.refs_5_
  31.9 1.2 %sums.8 = f32[778,128]{1,0:T(8,128)S(1)} custom-call(f32[776,128]{1,0:T(8,128)S(1)} %collective-permute-done.9.refs_0_.refs_5_, f32[776,128]{1,0:T(8,128)S(1)} %collective-permute-done.1.refs_1_.refs_3_, f32[778,128]{1,0:T(8,128)S(1)} %sums.7.refs_2_), custom_call_target="tpu_custom_call" | custom-call | flops 1 | bytes 1 | tf_op jit(solution)/shard_map/sums/pallas_call | solution.py:246
  33.1 2.1 %collective-permute-start.11 = (f32[778,128]{1,0:T(8,128)S(1)}, f32[778,128]{1,0:T(8,128)S(1)}, u32[]{:S(2)}, u32[]{:S(2)}) collective-permute-start(f32[778,128]{1,0:T(8,128)S(1)} %sums.8), channel_id=1, source_target_pairs={{0,5},{1,4},{2,7},{3,6},{4,9},{5,8},{6,11},{7,10},{8,13},{9,12},{1... | collective-permute-start | bytes 1195016 | tf_op jit(solution)/shard_map/ppermute | solution.py:28
  35.3 2.3 %collective-permute-done.4 = f32[779,128]{1,0:T(8,128)S(1)} collective-permute-done((f32[779,128]{1,0:T(8,128)S(1)}, f32[779,128]{1,0:T(8,128)S(1)}, u32[]{:S(2)}, u32[]{:S(2)}) %collective-permute-start.4) | collective-permute-done | bytes 398880 | tf_op jit(solution)/shard_map/ppermute | solution.py:33
  37.6 0.1 collective-permute-start.10
  37.6 0.5 collective-permute-start.14
  38.1 0.0 collective-permute-done.15
  38.2 0.6 %collective-permute-start.16 = (f32[778,128]{1,0:T(8,128)S(1)}, f32[778,128]{1,0:T(8,128)S(1)}, u32[]{:S(2)}, u32[]{:S(2)}) collective-permute-start(f32[778,128]{1,0:T(8,128)S(1)} %add.7), channel_id=1, source_target_pairs={{0,2},{1,3},{2,0},{3,1},{4,6},{5,7},{6,4},{7,5},{8,10},{9,11},{10,... | collective-permute-start | bytes 1195016 | tf_op jit(solution)/shard_map/ppermute | solution.py:33
  38.8 1.9 %sums.10.refs_2_ = f32[778,128]{1,0:T(8,128)S(1)} custom-call(f32[779,128]{1,0:T(8,128)S(1)} %get-tuple-element.19.refs_0_, f32[779,128]{1,0:T(8,128)S(1)} %collective-permute-done.5.refs_1_, f32[776,128]{1,0:T(8,128)S(1)} %slice.11.refs_0_.refs_2_, f32[779,128]{1,0:T(8,128)S(1)} %get-tuple-element.17.refs_2_.refs_3_, ...), custom_call_target="tpu_custom_call" | custom-call | flops 1 | bytes 1 | tf_op jit(solution)/shard_map/sums/pallas_call | solution.py:246
  40.7 0.0 collective-permute-done.10.refs_1_.refs_0_
  40.7 1.0 %sums.11 = f32[778,128]{1,0:T(8,128)S(1)} custom-call(f32[776,128]{1,0:T(8,128)S(1)} %collective-permute-done.10.refs_1_.refs_0_, f32[776,128]{1,0:T(8,128)S(1)} %collective-permute-done.1.refs_1_.refs_3_, f32[778,128]{1,0:T(8,128)S(1)} %sums.10.refs_2_), custom_call_target="tpu_custom_call" | custom-call | flops 1 | bytes 1 | tf_op jit(solution)/shard_map/sums/pallas_call | solution.py:246
  41.6 4.5 %collective-permute-start.13 = (f32[778,128]{1,0:T(8,128)S(1)}, f32[778,128]{1,0:T(8,128)S(1)}, u32[]{:S(2)}, u32[]{:S(2)}) collective-permute-start(f32[778,128]{1,0:T(8,128)S(1)} %sums.11), channel_id=1, source_target_pairs={{0,28},{4,0},{8,4},{12,8},{16,12},{20,16},{24,20},{28,24},{1,29},{... | collective-permute-start | bytes 1195016 | tf_op jit(solution)/shard_map/ppermute | solution.py:16
  46.2 1.4 %collective-permute-done.11 = f32[778,128]{1,0:T(8,128)S(1)} collective-permute-done((f32[778,128]{1,0:T(8,128)S(1)}, f32[778,128]{1,0:T(8,128)S(1)}, u32[]{:S(2)}, u32[]{:S(2)}) %collective-permute-start.11) | collective-permute-done | bytes 398368 | tf_op jit(solution)/shard_map/ppermute | solution.py:28
  47.5 0.0 collective-permute-start.12
  47.5 0.0 collective-permute-done.14
  47.5 0.1 add.6.refs_0_
  47.6 1.3 %sums.9.base = f32[2,9,128,128]{3,2,1,0:T(8,128)S(1)} custom-call(f32[776,128]{1,0:T(8,128)S(1)} %slice.11.refs_0_.refs_2_, f32[776,128]{1,0:T(8,128)S(1)} %collective-permute-done.10.refs_1_.refs_0_, f32[776,128]{1,0:T(8,128)S(1)} %slice.12.refs_5_.refs_2_, f32[776,128]{1,0:T(8,128)S(1)} %collective-permute-done.1.refs_1_.refs_3_, ...), custom_call_target="tpu_custom_call" | custom-call | flops 1 | bytes 1 | tf_op jit(solution)/shard_map/sums/pallas_call | solution.py:246
  48.9 0.6 %collective-permute-done.16.refs_1_ = f32[778,128]{1,0:T(8,128)S(1)} collective-permute-done((f32[778,128]{1,0:T(8,128)S(1)}, f32[778,128]{1,0:T(8,128)S(1)}, u32[]{:S(2)}, u32[]{:S(2)}) %collective-permute-start.16) | collective-permute-done | bytes 398368 | tf_op jit(solution)/shard_map/ppermute | solution.py:33
  49.5 6.6 %collective-permute-done.13.upper = f32[778,128]{1,0:T(8,128)S(1)} collective-permute-done((f32[778,128]{1,0:T(8,128)S(1)}, f32[778,128]{1,0:T(8,128)S(1)}, u32[]{:S(2)}, u32[]{:S(2)}) %collective-permute-start.13) | collective-permute-done | bytes 398368 | tf_op jit(solution)/shard_map/ppermute | solution.py:16
  56.2 0.0 collective-permute-done.12.lower
  56.2 1.1 %finish.1 = f32[2,9,128,128]{3,2,1,0:T(8,128)} custom-call(f32[2,9,128,128]{3,2,1,0:T(8,128)S(1)} %sums.9.base, f32[778,128]{1,0:T(8,128)S(1)} %collective-permute-done.12.lower, f32[778,128]{1,0:T(8,128)S(1)} %collective-permute-done.13.upper, f32[778,128]{1,0:T(8,128)S(1)} %add.6.refs_0_, f32[778,128]{1,0:T(8,128)S(1)} %collective-permute-done.16.refs_1_), custom_call_target="tpu_custom_call" | custom-call | flops 1 | bytes 1 | tf_op jit(solution)/shard_map/finish/pallas_call | solution.py:328
  (4 shorter events, 0.1 us)
Async XLA Ops:
  0.0 0.7 %copy-start = (s32[2,9,9]{2,0,1:T(2,128)S(1)}, s32[2,9,9]{2,0,1:T(2,128)}, u32[]{:S(2)}) copy-start(s32[2,9,9]{2,0,1:T(2,128)} %param.5) | copy-start | bytes 1948
  0.7 0.7 %copy-start.1 = (s32[2,9]{1,0:T(2,128)S(1)}, s32[2,9]{1,0:T(2,128)}, u32[]{:S(2)}) copy-start(s32[2,9]{1,0:T(2,128)} %cols.1) | copy-start | bytes 220
  2.8 8.2 %collective-permute-start.5 = (f32[779,128]{1,0:T(8,128)S(1)}, f32[779,128]{1,0:T(8,128)S(1)}, u32[]{:S(2)}, u32[]{:S(2)}) collective-permute-start(f32[779,128]{1,0:T(8,128)S(1)} %get-tuple-element.19.refs_0_), channel_id=1, source_target_pairs={{0,1},{1,0},{2,3},{3,2},{4,5},{5,4},{6,7},{7,6},{8,9},{9,8},{10,11... | collective-permute-start | bytes 1196552 | tf_op jit(solution)/shard_map/ppermute | solution.py:33
  3.3 7.6 %collective-permute-start.6 = (f32[779,128]{1,0:T(8,128)S(1)}, f32[779,128]{1,0:T(8,128)S(1)}, u32[]{:S(2)}, u32[]{:S(2)}) collective-permute-start(f32[779,128]{1,0:T(8,128)S(1)} %get-tuple-element.17.refs_2_.refs_3_), channel_id=1, source_target_pairs={{0,1},{1,0},{2,3},{3,2},{4,5},{5,4},{6,7},{7,6},{8,9},{9,8},{10,11... | collective-permute-start | bytes 1196552 | tf_op jit(solution)/shard_map/ppermute | solution.py:33
  3.4 7.6 %collective-permute-start.7 = (f32[779,128]{1,0:T(8,128)S(1)}, f32[779,128]{1,0:T(8,128)S(1)}, u32[]{:S(2)}, u32[]{:S(2)}) collective-permute-start(f32[779,128]{1,0:T(8,128)S(1)} %get-tuple-element.20.refs_4_.refs_0_), channel_id=1, source_target_pairs={{0,1},{1,0},{2,3},{3,2},{4,5},{5,4},{6,7},{7,6},{8,9},{9,8},{10,11... | collective-permute-start | bytes 1196552 | tf_op jit(solution)/shard_map/ppermute | solution.py:33
  3.8 12.7 %collective-permute-start = (f32[779,128]{1,0:T(8,128)S(1)}, f32[779,128]{1,0:T(8,128)S(1)}, u32[]{:S(2)}, u32[]{:S(2)}) collective-permute-start(f32[779,128]{1,0:T(8,128)S(1)} %get-tuple-element.17.refs_2_.refs_3_), channel_id=1, source_target_pairs={{0,2},{1,3},{2,0},{3,1},{4,6},{5,7},{6,4},{7,5},{8,10},{9,11},{10,... | collective-permute-start | bytes 1196552 | tf_op jit(solution)/shard_map/ppermute | solution.py:33
  6.4 20.0 %collective-permute-start.3 = (f32[779,128]{1,0:T(8,128)S(1)}, f32[779,128]{1,0:T(8,128)S(1)}, u32[]{:S(2)}, u32[]{:S(2)}) collective-permute-start(f32[779,128]{1,0:T(8,128)S(1)} %get-tuple-element.19.refs_0_), channel_id=1, source_target_pairs={{0,28},{4,0},{8,4},{12,8},{16,12},{20,16},{24,20},{28,24},{1,29},{... | collective-permute-start | bytes 1196552 | tf_op jit(solution)/shard_map/ppermute | solution.py:16
  11.0 15.4 %collective-permute-start.2 = (f32[779,128]{1,0:T(8,128)S(1)}, f32[779,128]{1,0:T(8,128)S(1)}, u32[]{:S(2)}, u32[]{:S(2)}) collective-permute-start(f32[779,128]{1,0:T(8,128)S(1)} %get-tuple-element.20.refs_4_.refs_0_), channel_id=1, source_target_pairs={{0,4},{4,8},{8,12},{12,16},{16,20},{20,24},{24,28},{28,0},{1,5},{5... | collective-permute-start | bytes 1196552 | tf_op jit(solution)/shard_map/ppermute | solution.py:16
  13.5 13.4 %collective-permute-start.8 = (f32[779,128]{1,0:T(8,128)S(1)}, f32[779,128]{1,0:T(8,128)S(1)}, u32[]{:S(2)}, u32[]{:S(2)}) collective-permute-start(f32[779,128]{1,0:T(8,128)S(1)} %get-tuple-element.20.refs_4_.refs_0_), channel_id=1, source_target_pairs={{0,2},{1,3},{2,0},{3,1},{4,6},{5,7},{6,4},{7,5},{8,10},{9,11},{10,... | collective-permute-start | bytes 1196552 | tf_op jit(solution)/shard_map/ppermute | solution.py:33
  16.6 9.8 %collective-permute-start.1 = (f32[776,128]{1,0:T(8,128)S(1)}, f32[776,128]{1,0:T(8,128)S(1)}, u32[]{:S(2)}, u32[]{:S(2)}) collective-permute-start(f32[776,128]{1,0:T(8,128)S(1)} %slice.12.refs_5_.refs_2_), channel_id=1, source_target_pairs={{0,1},{1,0},{2,3},{3,2},{4,5},{5,4},{6,7},{7,6},{8,9},{9,8},{10,11... | collective-permute-start | bytes 1191944 | tf_op jit(solution)/shard_map/ppermute | solution.py:33
  26.4 11.2 %collective-permute-start.4 = (f32[779,128]{1,0:T(8,128)S(1)}, f32[779,128]{1,0:T(8,128)S(1)}, u32[]{:S(2)}, u32[]{:S(2)}) collective-permute-start(f32[779,128]{1,0:T(8,128)S(1)} %get-tuple-element.19.refs_0_), channel_id=1, source_target_pairs={{0,2},{1,3},{2,0},{3,1},{4,6},{5,7},{6,4},{7,5},{8,10},{9,11},{10,... | collective-permute-start | bytes 1196552 | tf_op jit(solution)/shard_map/ppermute | solution.py:33
  26.9 5.0 %collective-permute-start.9 = (f32[776,128]{1,0:T(8,128)S(1)}, f32[776,128]{1,0:T(8,128)S(1)}, u32[]{:S(2)}, u32[]{:S(2)}) collective-permute-start(f32[776,128]{1,0:T(8,128)S(1)} %slice.13.refs_2_.refs_4_), channel_id=1, source_target_pairs={{0,1},{1,0},{2,3},{3,2},{4,5},{5,4},{6,7},{7,6},{8,9},{9,8},{10,11... | collective-permute-start | bytes 1191944 | tf_op jit(solution)/shard_map/ppermute | solution.py:33
  28.9 9.2 %collective-permute-start.15 = (f32[778,128]{1,0:T(8,128)S(1)}, f32[778,128]{1,0:T(8,128)S(1)}, u32[]{:S(2)}, u32[]{:S(2)}) collective-permute-start(f32[778,128]{1,0:T(8,128)S(1)} %get-tuple-element.25), channel_id=1, source_target_pairs={{0,1},{1,0},{2,3},{3,2},{4,5},{5,4},{6,7},{7,6},{8,9},{9,8},{10,11... | collective-permute-start | bytes 1195016 | tf_op jit(solution)/shard_map/ppermute | solution.py:33
  33.1 14.4 %collective-permute-start.11 = (f32[778,128]{1,0:T(8,128)S(1)}, f32[778,128]{1,0:T(8,128)S(1)}, u32[]{:S(2)}, u32[]{:S(2)}) collective-permute-start(f32[778,128]{1,0:T(8,128)S(1)} %sums.8), channel_id=1, source_target_pairs={{0,5},{1,4},{2,7},{3,6},{4,9},{5,8},{6,11},{7,10},{8,13},{9,12},{1... | collective-permute-start | bytes 1195016 | tf_op jit(solution)/shard_map/ppermute | solution.py:28
  37.6 3.1 %collective-permute-start.10 = (f32[776,128]{1,0:T(8,128)S(1)}, f32[776,128]{1,0:T(8,128)S(1)}, u32[]{:S(2)}, u32[]{:S(2)}) collective-permute-start(f32[776,128]{1,0:T(8,128)S(1)} %slice.11.refs_0_.refs_2_), channel_id=1, source_target_pairs={{0,1},{1,0},{2,3},{3,2},{4,5},{5,4},{6,7},{7,6},{8,9},{9,8},{10,11... | collective-permute-start | bytes 1191944 | tf_op jit(solution)/shard_map/ppermute | solution.py:33
  37.6 9.9 %collective-permute-start.14 = (f32[778,128]{1,0:T(8,128)S(1)}, f32[778,128]{1,0:T(8,128)S(1)}, u32[]{:S(2)}, u32[]{:S(2)}) collective-permute-start(f32[778,128]{1,0:T(8,128)S(1)} %get-tuple-element.23), channel_id=1, source_target_pairs={{0,1},{1,0},{2,3},{3,2},{4,5},{5,4},{6,7},{7,6},{8,9},{9,8},{10,11... | collective-permute-start | bytes 1195016 | tf_op jit(solution)/shard_map/ppermute | solution.py:33
  38.2 11.3 %collective-permute-start.16 = (f32[778,128]{1,0:T(8,128)S(1)}, f32[778,128]{1,0:T(8,128)S(1)}, u32[]{:S(2)}, u32[]{:S(2)}) collective-permute-start(f32[778,128]{1,0:T(8,128)S(1)} %add.7), channel_id=1, source_target_pairs={{0,2},{1,3},{2,0},{3,1},{4,6},{5,7},{6,4},{7,5},{8,10},{9,11},{10,... | collective-permute-start | bytes 1195016 | tf_op jit(solution)/shard_map/ppermute | solution.py:33
  41.6 14.5 %collective-permute-start.13 = (f32[778,128]{1,0:T(8,128)S(1)}, f32[778,128]{1,0:T(8,128)S(1)}, u32[]{:S(2)}, u32[]{:S(2)}) collective-permute-start(f32[778,128]{1,0:T(8,128)S(1)} %sums.11), channel_id=1, source_target_pairs={{0,28},{4,0},{8,4},{12,8},{16,12},{20,16},{24,20},{28,24},{1,29},{... | collective-permute-start | bytes 1195016 | tf_op jit(solution)/shard_map/ppermute | solution.py:16
  47.5 8.7 %collective-permute-start.12 = (f32[778,128]{1,0:T(8,128)S(1)}, f32[778,128]{1,0:T(8,128)S(1)}, u32[]{:S(2)}, u32[]{:S(2)}) collective-permute-start(f32[778,128]{1,0:T(8,128)S(1)} %collective-permute-done.11), channel_id=1, source_target_pairs={{0,1},{1,0},{2,3},{3,2},{4,5},{5,4},{6,7},{7,6},{8,9},{9,8},{10,11... | collective-permute-start | bytes 1195016 | tf_op jit(solution)/shard_map/ppermute | solution.py:33

commit v5 on v4

--- a/solution.py
+++ b/solution.py
@@ -213,7 +213,7 @@
     strip_rows = local_rows * parts
     meta_rows = local_rows * per + -(local_rows * per) % 8
     used_rows = local_rows * per * side + meta_rows
-    payload_rows = used_rows + 3
+    payload_rows = used_rows + 7
     in_hbm = pl.BlockSpec(memory_space=pltpu.HBM)
     scalars = pl.BlockSpec(memory_space=pltpu.SMEM)
     vectors = pl.BlockSpec(memory_space=pltpu.VMEM)
@@ -238,15 +238,15 @@
         lax.axis_index("inner").reshape(1),
     )
 
-    spare = 10
-
-    def sums(groups, a_at, plan, first, width, offset=0, base=()):
+    lines = local_rows * per * side
+
+    def sums(groups, a_at, plan, first, width, offset=0, base=(), spare=0):
         held = len(groups[0])
         dims = (offset, held, local_rows, slots, side, meta_rows, a_at, len(groups), first, width)
         return pl.pallas_call(
             functools.partial(sums_kernel, dims, plan),
             out_shape=jax.ShapeDtypeStruct(
-                (local_rows * per * side + spare, side) if width == per else density.shape,
+                (lines + spare, side) if width == per else density.shape,
                 jnp.float32,
             ),
             in_specs=[vectors] * (held * len(groups) + len(base)),
@@ -262,12 +262,12 @@
             name="sums",
         )(*[payload for group in groups for payload in group], *base)
 
-    def strip_sums(groups, a_at, plan, first):
+    def strip_sums(groups, a_at, plan, first, spare):
         early = parts // 2 + 1
-        total = sums([group[:early] for group in groups], a_at, plan, first, per)
+        total = sums([group[:early] for group in groups], a_at, plan, first, per, spare=spare)
         if parts > early:
             rest = [group[early:] for group in groups]
-            total = sums(rest, a_at, plan, first, per, early, [total])
+            total = sums(rest, a_at, plan, first, per, early, [total], spare)
         return total
 
     def spread(far):
@@ -280,7 +280,7 @@
         return pl.pallas_call(
             functools.partial(partial_kernel, (parts, local_rows, slots, side, meta_rows)),
             out_shape=[
-                jax.ShapeDtypeStruct((local_rows * per * side + spare, side), jnp.float32)
+                jax.ShapeDtypeStruct((lines + 10, side), jnp.float32)
             ] * parts,
             in_specs=[vectors] * 2,
             out_specs=[vectors] * parts,
@@ -302,13 +302,13 @@
 
     far_upper = across(upper, [base])
     far_middles = spread(far_middle)
-    far_lower = across(lower, [*far_middles, below, above])
+    far_lower = across(lower, far_middles)
     all_middles = middles + far_middles
-    far_uppers = spread(far_upper)
-    below_next = strip_sums([uppers + far_uppers, all_middles], 0, ((1, per),), 0)
+    far_uppers = spread(tied(far_upper, below, above))
+    below_next = strip_sums([uppers + far_uppers, all_middles], 0, ((1, per),), 0, 22)
     to_below_next = shifted_aslant(below_next, 1)
 
-    shares = dict(enumerate(partials(below, above)))
+    shares = dict(enumerate(partials(*tied([below, above], below_next))))
     for bit in [1 << i for i in range(20) if (1 << i) < parts // 2]:
         shares = {
             distance: share + swapped(shares[distance ^ bit], bit)
@@ -317,13 +317,13 @@
         }
     far_share = across(shares[parts // 2], [below_next]) if parts > 1 else []
     far_lowers = spread(tied(far_lower, below_next)) if far_lower else []
-    above_next = strip_sums([lowers + far_lowers, all_middles], 0, ((1, per),), 2 * per)
+    above_next = strip_sums([lowers + far_lowers, all_middles], 0, ((1, per),), 2 * per, 9)
     to_above_next = shifted(above_next, -1)
     if far_lowers:
         near = len(lowers)
         groups = [far_lowers, far_middles, far_uppers]
         base = sums(groups, 1, own_plan, 0, slots, near, [base])
-        to_below_next = swapped(to_below_next, 1)
+        to_below_next = swapped(to_below_next[:lines], 1)
     middle_shares = [shares[0], *far_share]
     return pl.pallas_call(
         finish_kernel,

time: 57.5 us -> 54.2 us (0.943)
  waiting for transfers between devices: 22.6 us -> 17.6 us
  starting transfers between devices: 18.2 us -> 20 us
    ppermute x3, waiting for transfers between devices: 16.4 us -> 12 us  [shifted(): return lax.ppermute(value, 'blk', pairs)]
    ppermute x13, starting transfers between devices: 7.01 us -> 8.99 us  [swapped(): lax.ppermute(value, 'inner', [(i, i ^ distance) for i in range(count)])]
    ppermute x1, waiting for transfers between devices: 1.35 us -> 0.01 us  [shifted_aslant(): return lax.ppermute(value, ('blk', 'inner'), pairs)]
    ppermute x3, starting transfers between devices: 9.09 us -> 8.04 us  [shifted(): return lax.ppermute(value, 'blk', pairs)]
    ppermute x1, starting transfers between devices: 2.15 us -> 2.99 us  [shifted_aslant(): return lax.ppermute(value, ('blk', 'inner'), pairs)]
    ppermute x13, waiting for transfers between devices: 4.9 us -> 5.52 us  [swapped(): lax.ppermute(value, 'inner', [(i, i ^ distance) for i in range(count)])]
  transfers between devices with their start and end apart: 17 -> 17, of which waited for: 6 -> 6; matrix products, arithmetic and copies ran while one was open for 0% -> 0% of each run, Pallas kernels for 21% -> 22%
where the time goes in v5:
time: 54.2 us; the launch traced here: 54 us
  starting transfers between devices  20 us (37%)
  waiting for transfers between devices  17.6 us (32%)
  Pallas kernels  14.6 us (27%)
  local copies, waits for them, and re-layouts  1.49 us (3%)
    ppermute x3, waiting for transfers between devices, shifted(): return lax.ppermute(value, 'blk', pairs)  12 us
    pallas_call x6, Pallas kernels, sums(): pl.pallas_call(functools.partial(sums_kernel, dims, plan), out_shape=jax....  10.1 us
    ppermute x13, starting transfers between devices, swapped(): lax.ppermute(value, 'inner', [(i, i ^ distance) for i in range(count)])  8.99 us
    ppermute x3, starting transfers between devices, shifted(): return lax.ppermute(value, 'blk', pairs)  8.04 us
    ppermute x13, waiting for transfers between devices, swapped(): lax.ppermute(value, 'inner', [(i, i ^ distance) for i in range(count)])  5.52 us
    ppermute x1, starting transfers between devices, shifted_aslant(): return lax.ppermute(value, ('blk', 'inner'), pairs)  2.99 us
    pallas_call x1, Pallas kernels, partials(): pl.pallas_call(functools.partial(partial_kernel, (parts, local_rows, slot...  1.96 us
    pallas_call x1, Pallas kernels, shards(): pl.pallas_call(functools.partial(pack_kernel, (local_rows, slots, side, s...  1.41 us
  transfers between devices with their start and end apart: 17, of which 6 were waited for; matrix products, arithmetic and copies ran while one was open for 0% of the time, Pallas kernels for 22%

profile of v5, /device:TPU:0, one launch (start us, length us, event | category | flops | bytes accessed | tf_op | source)
XLA Modules:
  0.0 54.0 jit_solution(11275193379593764270)
XLA Ops:
  0.0 0.0 copy-start
  0.0 0.7 %copy-done = s32[2,9,9]{2,0,1:T(2,128)S(1)} copy-done((s32[2,9,9]{2,0,1:T(2,128)S(1)}, s32[2,9,9]{2,0,1:T(2,128)}, u32[]{:S(2)}) %copy-start) | copy-done | bytes 672
  0.7 0.7 %copy-done.1 = s32[2,9]{1,0:T(2,128)S(1)} copy-done((s32[2,9]{1,0:T(2,128)S(1)}, s32[2,9]{1,0:T(2,128)}, u32[]{:S(2)}) %copy-start.1) | copy-done | bytes 96
  1.4 1.4 %pack.1 = (f32[783,128]{1,0:T(8,128)S(1)}, f32[783,128]{1,0:T(8,128)S(1)}, f32[783,128]{1,0:T(8,128)S(1)}) custom-call(f32[2304,128]{1,0:T(8,128)} %bitcast.4, s32[9,2,9]{2,1,0:T(2,128)S(1)} %bitcast.3, s32[2,9]{1,0:T(2,128)S(1)} %copy-done.1, s32[1]{0:T(128)} %bitcast.2.inner), custom_call_target="tpu_custom_call" | custom-call | tf_op jit(solution)/shard_map/pack/pallas_call | solution.py:221
  2.8 0.5 collective-permute-start.3
  3.3 0.1 collective-permute-start.4
  3.4 0.4 collective-permute-start.5
  3.8 2.6 %collective-permute-start = (f32[783,128]{1,0:T(8,128)S(1)}, f32[783,128]{1,0:T(8,128)S(1)}, u32[]{:S(2)}, u32[]{:S(2)}) collective-permute-start(f32[783,128]{1,0:T(8,128)S(1)} %get-tuple-element.20.refs_2_.refs_3_), channel_id=1, source_target_pairs={{0,2},{1,3},{2,0},{3,1},{4,6},{5,7},{6,4},{7,5},{8,10},{9,11},{10,... | collective-permute-start | bytes 1202696 | tf_op jit(solution)/shard_map/ppermute | solution.py:33
  6.4 4.6 %collective-permute-start.8 = (f32[783,128]{1,0:T(8,128)S(1)}, f32[783,128]{1,0:T(8,128)S(1)}, u32[]{:S(2)}, u32[]{:S(2)}) collective-permute-start(f32[783,128]{1,0:T(8,128)S(1)} %get-tuple-element.21.refs_0_), channel_id=1, source_target_pairs={{0,28},{4,0},{8,4},{12,8},{16,12},{20,16},{24,20},{28,24},{1,29},{... | collective-permute-start | bytes 1202696 | tf_op jit(solution)/shard_map/ppermute | solution.py:16
  10.9 0.0 collective-permute-done.3.refs_1_
  11.0 0.0 collective-permute-start.7
  11.0 0.0 collective-permute-done.4.refs_3_.refs_4_
  11.0 0.0 collective-permute-done.5.refs_5_.refs_1_
  11.0 1.7 %sums.6.refs_6_ = f32[2,9,128,128]{3,2,1,0:T(8,128)S(1)} custom-call(f32[783,128]{1,0:T(8,128)S(1)} %get-tuple-element.21.refs_0_, f32[783,128]{1,0:T(8,128)S(1)} %collective-permute-done.3.refs_1_, f32[783,128]{1,0:T(8,128)S(1)} %get-tuple-element.20.refs_2_.refs_3_, f32[783,128]{1,0:T(8,128)S(1)} %collective-permute-done.4.refs_3_.refs_4_, ...), custom_call_target="tpu_custom_call" | custom-call | flops 1 | bytes 1 | tf_op jit(solution)/shard_map/sums/pallas_call | solution.py:246
  12.7 1.4 %collective-permute-start.6 = (f32[783,128]{1,0:T(8,128)S(1)}, f32[783,128]{1,0:T(8,128)S(1)}, u32[]{:S(2)}, u32[]{:S(2)}) collective-permute-start(f32[783,128]{1,0:T(8,128)S(1)} %get-tuple-element.23.refs_4_.refs_0_), channel_id=1, source_target_pairs={{0,2},{1,3},{2,0},{3,1},{4,6},{5,7},{6,4},{7,5},{8,10},{9,11},{10,... | collective-permute-start | bytes 1202696 | tf_op jit(solution)/shard_map/ppermute | solution.py:33
  14.1 2.4 %collective-permute-done = f32[783,128]{1,0:T(8,128)S(1)} collective-permute-done((f32[783,128]{1,0:T(8,128)S(1)}, f32[783,128]{1,0:T(8,128)S(1)}, u32[]{:S(2)}, u32[]{:S(2)}) %collective-permute-start) | collective-permute-done | bytes 400928 | tf_op jit(solution)/shard_map/ppermute | solution.py:33
  16.5 0.1 collective-permute-start.1
  16.6 1.7 %collective-permute-done.1.refs_1_.refs_3_ = f32[776,128]{1,0:T(8,128)S(1)} collective-permute-done((f32[776,128]{1,0:T(8,128)S(1)}, f32[776,128]{1,0:T(8,128)S(1)}, u32[]{:S(2)}, u32[]{:S(2)}) %collective-permute-start.1) | collective-permute-done | bytes 397344 | tf_op jit(solution)/shard_map/ppermute | solution.py:33
  18.3 2.0 %collective-permute-start.2 = (f32[783,128]{1,0:T(8,128)S(1)}, f32[783,128]{1,0:T(8,128)S(1)}, u32[]{:S(2)}, u32[]{:S(2)}) collective-permute-start(f32[783,128]{1,0:T(8,128)S(1)} %get-tuple-element.21.refs_0_), channel_id=1, source_target_pairs={{0,2},{1,3},{2,0},{3,1},{4,6},{5,7},{6,4},{7,5},{8,10},{9,11},{10,... | collective-permute-start | bytes 1202696 | tf_op jit(solution)/shard_map/ppermute | solution.py:33
  20.3 6.0 %collective-permute-done.8.above = f32[783,128]{1,0:T(8,128)S(1)} collective-permute-done((f32[783,128]{1,0:T(8,128)S(1)}, f32[783,128]{1,0:T(8,128)S(1)}, u32[]{:S(2)}, u32[]{:S(2)}) %collective-permute-start.8) | collective-permute-done | bytes 400928 | tf_op jit(solution)/shard_map/ppermute | solution.py:16
  26.4 0.0 collective-permute-done.7.below
  26.4 0.0 collective-permute-done.6
  26.4 0.1 collective-permute-start.9
  26.5 1.3 %sums.7.refs_2_ = f32[790,128]{1,0:T(8,128)S(1)} custom-call(f32[783,128]{1,0:T(8,128)S(1)} %get-tuple-element.23.refs_4_.refs_0_, f32[783,128]{1,0:T(8,128)S(1)} %collective-permute-done.5.refs_5_.refs_1_, f32[776,128]{1,0:T(8,128)S(1)} %slice.13.refs_2_.refs_4_, f32[783,128]{1,0:T(8,128)S(1)} %get-tuple-element.20.refs_2_.refs_3_, ...), custom_call_target="tpu_custom_call" | custom-call | flops 1 | bytes 1 | tf_op jit(solution)/shard_map/sums/pallas_call | solution.py:246
  27.8 0.4 collective-permute-done.9.refs_0_.refs_5_
  28.2 1.0 %sums.8 = f32[790,128]{1,0:T(8,128)S(1)} custom-call(f32[776,128]{1,0:T(8,128)S(1)} %collective-permute-done.9.refs_0_.refs_5_, f32[776,128]{1,0:T(8,128)S(1)} %collective-permute-done.1.refs_1_.refs_3_, f32[790,128]{1,0:T(8,128)S(1)} %sums.7.refs_2_), custom_call_target="tpu_custom_call" | custom-call | flops 1 | bytes 1 | tf_op jit(solution)/shard_map/sums/pallas_call | solution.py:246
  29.2 3.0 %collective-permute-start.11 = (f32[790,128]{1,0:T(8,128)S(1)}, f32[790,128]{1,0:T(8,128)S(1)}, u32[]{:S(2)}, u32[]{:S(2)}) collective-permute-start(f32[790,128]{1,0:T(8,128)S(1)} %sums.8), channel_id=1, source_target_pairs={{0,5},{1,4},{2,7},{3,6},{4,9},{5,8},{6,11},{7,10},{8,13},{9,12},{1... | collective-permute-start | bytes 1213448 | tf_op jit(solution)/shard_map/ppermute | solution.py:28
  32.1 2.0 %partials.1 = (f32[778,128]{1,0:T(8,128)S(1)}, f32[778,128]{1,0:T(8,128)S(1)}, f32[778,128]{1,0:T(8,128)S(1)}, f32[778,128]{1,0:T(8,128)S(1)}) custom-call(f32[783,128]{1,0:T(8,128)S(1)} %collective-permute-done.7.below, f32[783,128]{1,0:T(8,128)S(1)} %collective-permute-done.8.above), custom_call_target="tpu_custom_call" | custom-call | flops 1 | bytes 1 | tf_op jit(solution)/shard_map/partials/pallas_call | solution.py:280
  34.1 0.1 collective-permute-start.15
  34.2 0.0 collective-permute-done.2
  34.2 0.6 %collective-permute-start.10 = (f32[776,128]{1,0:T(8,128)S(1)}, f32[776,128]{1,0:T(8,128)S(1)}, u32[]{:S(2)}, u32[]{:S(2)}) collective-permute-start(f32[776,128]{1,0:T(8,128)S(1)} %slice.14.refs_0_.refs_2_), channel_id=1, source_target_pairs={{0,1},{1,0},{2,3},{3,2},{4,5},{5,4},{6,7},{7,6},{8,9},{9,8},{10,11... | collective-permute-start | bytes 1191944 | tf_op jit(solution)/shard_map/ppermute | solution.py:33
  34.8 0.1 collective-permute-start.14
  34.9 1.0 %collective-permute-done.15 = f32[778,128]{1,0:T(8,128)S(1)} collective-permute-done((f32[778,128]{1,0:T(8,128)S(1)}, f32[778,128]{1,0:T(8,128)S(1)}, u32[]{:S(2)}, u32[]{:S(2)}) %collective-permute-start.15) | collective-permute-done | bytes 398368 | tf_op jit(solution)/shard_map/ppermute | solution.py:33
  35.9 0.1 add.7
  36.0 0.9 %collective-permute-start.16 = (f32[778,128]{1,0:T(8,128)S(1)}, f32[778,128]{1,0:T(8,128)S(1)}, u32[]{:S(2)}, u32[]{:S(2)}) collective-permute-start(f32[778,128]{1,0:T(8,128)S(1)} %add.7), channel_id=1, source_target_pairs={{0,2},{1,3},{2,0},{3,1},{4,6},{5,7},{6,4},{7,5},{8,10},{9,11},{10,... | collective-permute-start | bytes 1195016 | tf_op jit(solution)/shard_map/ppermute | solution.py:33
  36.8 2.1 %sums.10.refs_2_ = f32[777,128]{1,0:T(8,128)S(1)} custom-call(f32[783,128]{1,0:T(8,128)S(1)} %get-tuple-element.21.refs_0_, f32[783,128]{1,0:T(8,128)S(1)} %collective-permute-done.3.refs_1_, f32[776,128]{1,0:T(8,128)S(1)} %slice.14.refs_0_.refs_2_, f32[783,128]{1,0:T(8,128)S(1)} %get-tuple-element.20.refs_2_.refs_3_, ...), custom_call_target="tpu_custom_call" | custom-call | flops 1 | bytes 1 | tf_op jit(solution)/shard_map/sums/pallas_call | solution.py:246
  39.0 0.0 collective-permute-done.10.refs_1_.refs_0_
  39.0 1.5 %sums.11 = f32[777,128]{1,0:T(8,128)S(1)} custom-call(f32[776,128]{1,0:T(8,128)S(1)} %collective-permute-done.10.refs_1_.refs_0_, f32[776,128]{1,0:T(8,128)S(1)} %collective-permute-done.1.refs_1_.refs_3_, f32[777,128]{1,0:T(8,128)S(1)} %sums.10.refs_2_), custom_call_target="tpu_custom_call" | custom-call | flops 1 | bytes 1 | tf_op jit(solution)/shard_map/sums/pallas_call | solution.py:246
  40.5 3.5 %collective-permute-start.13 = (f32[777,128]{1,0:T(8,128)S(1)}, f32[777,128]{1,0:T(8,128)S(1)}, u32[]{:S(2)}, u32[]{:S(2)}) collective-permute-start(f32[777,128]{1,0:T(8,128)S(1)} %sums.11), channel_id=1, source_target_pairs={{0,28},{4,0},{8,4},{12,8},{16,12},{20,16},{24,20},{28,24},{1,29},{... | collective-permute-start | bytes 1193480 | tf_op jit(solution)/shard_map/ppermute | solution.py:16
  44.0 0.0 collective-permute-done.11
  44.0 0.2 collective-permute-start.12
  44.2 2.5 %sums.9.base = f32[2,9,128,128]{3,2,1,0:T(8,128)S(1)} custom-call(f32[776,128]{1,0:T(8,128)S(1)} %slice.14.refs_0_.refs_2_, f32[776,128]{1,0:T(8,128)S(1)} %collective-permute-done.10.refs_1_.refs_0_, f32[776,128]{1,0:T(8,128)S(1)} %slice.16.refs_5_.refs_2_, f32[776,128]{1,0:T(8,128)S(1)} %collective-permute-done.1.refs_1_.refs_3_, ...), custom_call_target="tpu_custom_call" | custom-call | flops 1 | bytes 1 | tf_op jit(solution)/shard_map/sums/pallas_call | solution.py:246
  46.7 0.0 collective-permute-done.14
  46.7 0.1 add.6.refs_0_
  46.8 6.0 %collective-permute-done.13.upper = f32[777,128]{1,0:T(8,128)S(1)} collective-permute-done((f32[777,128]{1,0:T(8,128)S(1)}, f32[777,128]{1,0:T(8,128)S(1)}, u32[]{:S(2)}, u32[]{:S(2)}) %collective-permute-start.13) | collective-permute-done | bytes 397856 | tf_op jit(solution)/shard_map/ppermute | solution.py:16
  52.8 0.0 collective-permute-done.16.refs_1_
  52.8 0.0 collective-permute-done.12.lower
  52.8 1.2 %finish.1 = f32[2,9,128,128]{3,2,1,0:T(8,128)} custom-call(f32[2,9,128,128]{3,2,1,0:T(8,128)S(1)} %sums.9.base, f32[768,128]{1,0:T(8,128)S(1)} %collective-permute-done.12.lower, f32[777,128]{1,0:T(8,128)S(1)} %collective-permute-done.13.upper, f32[778,128]{1,0:T(8,128)S(1)} %add.6.refs_0_, f32[778,128]{1,0:T(8,128)S(1)} %collective-permute-done.16.refs_1_), custom_call_target="tpu_custom_call" | custom-call | flops 1 | bytes 1 | tf_op jit(solution)/shard_map/finish/pallas_call | solution.py:328
  (5 shorter events, 0.1 us)
Async XLA Ops:
  0.0 0.7 %copy-start = (s32[2,9,9]{2,0,1:T(2,128)S(1)}, s32[2,9,9]{2,0,1:T(2,128)}, u32[]{:S(2)}) copy-start(s32[2,9,9]{2,0,1:T(2,128)} %param.5) | copy-start | bytes 1948
  0.7 0.7 %copy-start.1 = (s32[2,9]{1,0:T(2,128)S(1)}, s32[2,9]{1,0:T(2,128)}, u32[]{:S(2)}) copy-start(s32[2,9]{1,0:T(2,128)} %cols.1) | copy-start | bytes 220
  2.8 8.2 %collective-permute-start.3 = (f32[783,128]{1,0:T(8,128)S(1)}, f32[783,128]{1,0:T(8,128)S(1)}, u32[]{:S(2)}, u32[]{:S(2)}) collective-permute-start(f32[783,128]{1,0:T(8,128)S(1)} %get-tuple-element.21.refs_0_), channel_id=1, source_target_pairs={{0,1},{1,0},{2,3},{3,2},{4,5},{5,4},{6,7},{7,6},{8,9},{9,8},{10,11... | collective-permute-start | bytes 1202696 | tf_op jit(solution)/shard_map/ppermute | solution.py:33
  3.3 7.6 %collective-permute-start.4 = (f32[783,128]{1,0:T(8,128)S(1)}, f32[783,128]{1,0:T(8,128)S(1)}, u32[]{:S(2)}, u32[]{:S(2)}) collective-permute-start(f32[783,128]{1,0:T(8,128)S(1)} %get-tuple-element.20.refs_2_.refs_3_), channel_id=1, source_target_pairs={{0,1},{1,0},{2,3},{3,2},{4,5},{5,4},{6,7},{7,6},{8,9},{9,8},{10,11... | collective-permute-start | bytes 1202696 | tf_op jit(solution)/shard_map/ppermute | solution.py:33
  3.4 7.6 %collective-permute-start.5 = (f32[783,128]{1,0:T(8,128)S(1)}, f32[783,128]{1,0:T(8,128)S(1)}, u32[]{:S(2)}, u32[]{:S(2)}) collective-permute-start(f32[783,128]{1,0:T(8,128)S(1)} %get-tuple-element.23.refs_4_.refs_0_), channel_id=1, source_target_pairs={{0,1},{1,0},{2,3},{3,2},{4,5},{5,4},{6,7},{7,6},{8,9},{9,8},{10,11... | collective-permute-start | bytes 1202696 | tf_op jit(solution)/shard_map/ppermute | solution.py:33
  3.8 12.6 %collective-permute-start = (f32[783,128]{1,0:T(8,128)S(1)}, f32[783,128]{1,0:T(8,128)S(1)}, u32[]{:S(2)}, u32[]{:S(2)}) collective-permute-start(f32[783,128]{1,0:T(8,128)S(1)} %get-tuple-element.20.refs_2_.refs_3_), channel_id=1, source_target_pairs={{0,2},{1,3},{2,0},{3,1},{4,6},{5,7},{6,4},{7,5},{8,10},{9,11},{10,... | collective-permute-start | bytes 1202696 | tf_op jit(solution)/shard_map/ppermute | solution.py:33
  6.4 20.0 %collective-permute-start.8 = (f32[783,128]{1,0:T(8,128)S(1)}, f32[783,128]{1,0:T(8,128)S(1)}, u32[]{:S(2)}, u32[]{:S(2)}) collective-permute-start(f32[783,128]{1,0:T(8,128)S(1)} %get-tuple-element.21.refs_0_), channel_id=1, source_target_pairs={{0,28},{4,0},{8,4},{12,8},{16,12},{20,16},{24,20},{28,24},{1,29},{... | collective-permute-start | bytes 1202696 | tf_op jit(solution)/shard_map/ppermute | solution.py:16
  11.0 15.4 %collective-permute-start.7 = (f32[783,128]{1,0:T(8,128)S(1)}, f32[783,128]{1,0:T(8,128)S(1)}, u32[]{:S(2)}, u32[]{:S(2)}) collective-permute-start(f32[783,128]{1,0:T(8,128)S(1)} %get-tuple-element.23.refs_4_.refs_0_), channel_id=1, source_target_pairs={{0,4},{4,8},{8,12},{12,16},{16,20},{20,24},{24,28},{28,0},{1,5},{5... | collective-permute-start | bytes 1202696 | tf_op jit(solution)/shard_map/ppermute | solution.py:16
  12.7 13.7 %collective-permute-start.6 = (f32[783,128]{1,0:T(8,128)S(1)}, f32[783,128]{1,0:T(8,128)S(1)}, u32[]{:S(2)}, u32[]{:S(2)}) collective-permute-start(f32[783,128]{1,0:T(8,128)S(1)} %get-tuple-element.23.refs_4_.refs_0_), channel_id=1, source_target_pairs={{0,2},{1,3},{2,0},{3,1},{4,6},{5,7},{6,4},{7,5},{8,10},{9,11},{10,... | collective-permute-start | bytes 1202696 | tf_op jit(solution)/shard_map/ppermute | solution.py:33
  16.5 1.8 %collective-permute-start.1 = (f32[776,128]{1,0:T(8,128)S(1)}, f32[776,128]{1,0:T(8,128)S(1)}, u32[]{:S(2)}, u32[]{:S(2)}) collective-permute-start(f32[776,128]{1,0:T(8,128)S(1)} %slice.16.refs_5_.refs_2_), channel_id=1, source_target_pairs={{0,1},{1,0},{2,3},{3,2},{4,5},{5,4},{6,7},{7,6},{8,9},{9,8},{10,11... | collective-permute-start | bytes 1191944 | tf_op jit(solution)/shard_map/ppermute | solution.py:33
  18.3 15.9 %collective-permute-start.2 = (f32[783,128]{1,0:T(8,128)S(1)}, f32[783,128]{1,0:T(8,128)S(1)}, u32[]{:S(2)}, u32[]{:S(2)}) collective-permute-start(f32[783,128]{1,0:T(8,128)S(1)} %get-tuple-element.21.refs_0_), channel_id=1, source_target_pairs={{0,2},{1,3},{2,0},{3,1},{4,6},{5,7},{6,4},{7,5},{8,10},{9,11},{10,... | collective-permute-start | bytes 1202696 | tf_op jit(solution)/shard_map/ppermute | solution.py:33
  26.4 1.8 %collective-permute-start.9 = (f32[776,128]{1,0:T(8,128)S(1)}, f32[776,128]{1,0:T(8,128)S(1)}, u32[]{:S(2)}, u32[]{:S(2)}) collective-permute-start(f32[776,128]{1,0:T(8,128)S(1)} %slice.13.refs_2_.refs_4_), channel_id=1, source_target_pairs={{0,1},{1,0},{2,3},{3,2},{4,5},{5,4},{6,7},{7,6},{8,9},{9,8},{10,11... | collective-permute-start | bytes 1191944 | tf_op jit(solution)/shard_map/ppermute | solution.py:33
  29.2 14.8 %collective-permute-start.11 = (f32[790,128]{1,0:T(8,128)S(1)}, f32[790,128]{1,0:T(8,128)S(1)}, u32[]{:S(2)}, u32[]{:S(2)}) collective-permute-start(f32[790,128]{1,0:T(8,128)S(1)} %sums.8), channel_id=1, source_target_pairs={{0,5},{1,4},{2,7},{3,6},{4,9},{5,8},{6,11},{7,10},{8,13},{9,12},{1... | collective-permute-start | bytes 1213448 | tf_op jit(solution)/shard_map/ppermute | solution.py:28
  34.1 1.8 %collective-permute-start.15 = (f32[778,128]{1,0:T(8,128)S(1)}, f32[778,128]{1,0:T(8,128)S(1)}, u32[]{:S(2)}, u32[]{:S(2)}) collective-permute-start(f32[778,128]{1,0:T(8,128)S(1)} %get-tuple-element.31), channel_id=1, source_target_pairs={{0,1},{1,0},{2,3},{3,2},{4,5},{5,4},{6,7},{7,6},{8,9},{9,8},{10,11... | collective-permute-start | bytes 1195016 | tf_op jit(solution)/shard_map/ppermute | solution.py:33
  34.2 4.7 %collective-permute-start.10 = (f32[776,128]{1,0:T(8,128)S(1)}, f32[776,128]{1,0:T(8,128)S(1)}, u32[]{:S(2)}, u32[]{:S(2)}) collective-permute-start(f32[776,128]{1,0:T(8,128)S(1)} %slice.14.refs_0_.refs_2_), channel_id=1, source_target_pairs={{0,1},{1,0},{2,3},{3,2},{4,5},{5,4},{6,7},{7,6},{8,9},{9,8},{10,11... | collective-permute-start | bytes 1191944 | tf_op jit(solution)/shard_map/ppermute | solution.py:33
  34.8 11.9 %collective-permute-start.14 = (f32[778,128]{1,0:T(8,128)S(1)}, f32[778,128]{1,0:T(8,128)S(1)}, u32[]{:S(2)}, u32[]{:S(2)}) collective-permute-start(f32[778,128]{1,0:T(8,128)S(1)} %get-tuple-element.29), channel_id=1, source_target_pairs={{0,1},{1,0},{2,3},{3,2},{4,5},{5,4},{6,7},{7,6},{8,9},{9,8},{10,11... | collective-permute-start | bytes 1195016 | tf_op jit(solution)/shard_map/ppermute | solution.py:33
  36.0 16.8 %collective-permute-start.16 = (f32[778,128]{1,0:T(8,128)S(1)}, f32[778,128]{1,0:T(8,128)S(1)}, u32[]{:S(2)}, u32[]{:S(2)}) collective-permute-start(f32[778,128]{1,0:T(8,128)S(1)} %add.7), channel_id=1, source_target_pairs={{0,2},{1,3},{2,0},{3,1},{4,6},{5,7},{6,4},{7,5},{8,10},{9,11},{10,... | collective-permute-start | bytes 1195016 | tf_op jit(solution)/shard_map/ppermute | solution.py:33
  40.5 12.3 %collective-permute-start.13 = (f32[777,128]{1,0:T(8,128)S(1)}, f32[777,128]{1,0:T(8,128)S(1)}, u32[]{:S(2)}, u32[]{:S(2)}) collective-permute-start(f32[777,128]{1,0:T(8,128)S(1)} %sums.11), channel_id=1, source_target_pairs={{0,28},{4,0},{8,4},{12,8},{16,12},{20,16},{24,20},{28,24},{1,29},{... | collective-permute-start | bytes 1193480 | tf_op jit(solution)/shard_map/ppermute | solution.py:16
  44.0 8.8 %collective-permute-start.12 = (f32[768,128]{1,0:T(8,128)S(1)}, f32[768,128]{1,0:T(8,128)S(1)}, u32[]{:S(2)}, u32[]{:S(2)}) collective-permute-start(f32[768,128]{1,0:T(8,128)S(1)} %slice.17), channel_id=1, source_target_pairs={{0,1},{1,0},{2,3},{3,2},{4,5},{5,4},{6,7},{7,6},{8,9},{9,8},{10,11... | collective-permute-start | bytes 1179656 | tf_op jit(solution)/shard_map/ppermute | solution.py:33

commit v6 on v5

--- a/solution.py
+++ b/solution.py
@@ -52,17 +52,11 @@
     return lax.div(value, size), lax.rem(value, size)
 
 
-def pack_kernel(dims, density, targets, cols, inner, *refs):
+def pack_kernel(dims, density, codes, inner, *refs):
     local_rows, slots, side, strip_rows, meta_rows = dims
     per = slots // 3
     data = local_rows * per * side
-    outs, (targets_v, cols_s, sems, meta_sems) = refs[:3], refs[3:]
-    arrivals = [
-        pltpu.make_async_copy(targets, targets_v, meta_sems.at[0]),
-        pltpu.make_async_copy(cols, cols_s, meta_sems.at[1]),
-    ]
-    for arrival in arrivals:
-        arrival.start()
+    outs, sems = refs[:3], refs[3]
     copies = []
     for group in (0, 2, 1):
         for row in range(local_rows):
@@ -72,19 +66,18 @@
             copies[-1].start()
     for group in (0, 2, 1):
         outs[group][data : data + meta_rows, :] = jnp.zeros((meta_rows, side), jnp.float32)
-    for arrival in arrivals:
-        arrival.wait()
+    lanes = lax.broadcasted_iota(jnp.int32, (local_rows, slots), 1)
+    owner, place = parted(parted(codes[slots], strip_rows)[1], local_rows)
+    dests = ((owner ^ inner[0]) * local_rows + place).astype(jnp.float32)
     for group in (0, 2, 1):
-        for row in range(local_rows):
-            for slot in range(per):
-                in_strip = parted(cols_s[row, group * per + slot], strip_rows)[1]
-                owner, line = parted(in_strip, local_rows)
-                code = (owner ^ inner[0]) * local_rows + line
+        for slot in range(per):
+            chosen = codes[group * per + slot].astype(jnp.float32)
+            mine = jnp.where(lanes == group * per + slot, dests, 0.0)
+            dest = jnp.sum(mine, axis=1, keepdims=True)
+            for row in range(local_rows):
                 at = data + row * per + slot
-                chosen = targets_v[group * per + slot, row : row + 1, :]
-                outs[group][at : at + 1, :slots] = chosen.astype(jnp.float32)
-                code = jnp.full((1, 1), code, jnp.int32).astype(jnp.float32)
-                outs[group][at : at + 1, slots : slots + 1] = code
+                outs[group][at : at + 1, :slots] = chosen[row : row + 1]
+                outs[group][at : at + 1, slots : slots + 1] = dest[row : row + 1]
     for copy in copies:
         copy.wait()
 
@@ -218,23 +211,20 @@
     scalars = pl.BlockSpec(memory_space=pltpu.SMEM)
     vectors = pl.BlockSpec(memory_space=pltpu.VMEM)
 
+    codes = jnp.concatenate([jnp.transpose(targets, (1, 0, 2)), block_cols[None]], axis=0)
     lower, middle, upper = pl.pallas_call(
         functools.partial(pack_kernel, (local_rows, slots, side, strip_rows, meta_rows)),
         out_shape=[jax.ShapeDtypeStruct((payload_rows, side), jnp.float32)] * 3,
-        in_specs=[in_hbm, in_hbm, in_hbm, scalars],
+        in_specs=[in_hbm, vectors, scalars],
         out_specs=[vectors] * 3,
         scratch_shapes=[
-            pltpu.VMEM((slots, local_rows, slots), jnp.int32),
-            pltpu.SMEM((local_rows, slots), jnp.int32),
             pltpu.SemaphoreType.DMA((3, local_rows)),
-            pltpu.SemaphoreType.DMA((2,)),
         ],
         compiler_params=pltpu.CompilerParams(vmem_limit_bytes=52 << 20),
         name="pack",
     )(
         density.reshape(-1, side),
-        jnp.transpose(targets, (1, 0, 2)),
-        block_cols,
+        codes,
         lax.axis_index("inner").reshape(1),
     )
 

time: 54.2 us -> 54 us (level)
  local copies, waits for them, and re-layouts: 1.49 us -> 0.11 us
  other arithmetic: 0.11 us -> 0.83 us
    unnamed x4 -> x0, local copies, waits for them, and re-layouts: 1.38 us -> none
    ppermute x13, waiting for transfers between devices: 5.52 us -> 4.55 us  [swapped(): lax.ppermute(value, 'inner', [(i, i ^ distance) for i in range(count)])]
    ppermute x3, waiting for transfers between devices: 12 us -> 12.8 us  [shifted(): return lax.ppermute(value, 'blk', pairs)]
    concatenate x0 -> x1, other arithmetic: none -> 0.72 us  [shards(): jnp.concatenate([jnp.transpose(targets, (1, 0, 2)), block_cols[None]], ax...]
where the time goes in v6:
time: 54 us; the launch traced here: 53.5 us
  starting transfers between devices  20.1 us (37%)
  waiting for transfers between devices  17.8 us (33%)
  Pallas kernels  14.5 us (27%)
  other arithmetic  0.83 us (2%)
    ppermute x3, waiting for transfers between devices, shifted(): return lax.ppermute(value, 'blk', pairs)  12.8 us
    pallas_call x6, Pallas kernels, sums(): pl.pallas_call(functools.partial(sums_kernel, dims, plan), out_shape=jax....  9.99 us
    ppermute x13, starting transfers between devices, swapped(): lax.ppermute(value, 'inner', [(i, i ^ distance) for i in range(count)])  8.67 us
    ppermute x3, starting transfers between devices, shifted(): return lax.ppermute(value, 'blk', pairs)  8.37 us
    ppermute x13, waiting for transfers between devices, swapped(): lax.ppermute(value, 'inner', [(i, i ^ distance) for i in range(count)])  4.55 us
    ppermute x1, starting transfers between devices, shifted_aslant(): return lax.ppermute(value, ('blk', 'inner'), pairs)  3.1 us
    pallas_call x1, Pallas kernels, partials(): pl.pallas_call(functools.partial(partial_kernel, (parts, local_rows, slot...  1.95 us
    pallas_call x1, Pallas kernels, shards(): pl.pallas_call(functools.partial(pack_kernel, (local_rows, slots, side, s...  1.39 us
  transfers between devices with their start and end apart: 17, of which 6 were waited for; matrix products, arithmetic and copies ran while one was open for 0% of the time, Pallas kernels for 22%

profile of v6, /device:TPU:0, one launch (start us, length us, event | category | flops | bytes accessed | tf_op | source)
XLA Modules:
  0.0 53.5 jit_solution(15980233722120373874)
XLA Ops:
  0.0 0.7 %pad_add_fusion.codes = s32[10,2,9]{2,1,0:T(2,128)S(1)} fusion(s32[1,2,9]{2,1,0:T(2,128)} %bitcast.6, s32[9,2,9]{2,1,0:T(2,128)} %bitcast.5), kind=kLoop, calls=%fused_computation | loop fusion | flops 180 | bytes 1440 | tf_op jit(solution)/shard_map/concatenate | solution.py:214
  0.7 1.4 %pack.1 = (f32[783,128]{1,0:T(8,128)S(1)}, f32[783,128]{1,0:T(8,128)S(1)}, f32[783,128]{1,0:T(8,128)S(1)}) custom-call(f32[2304,128]{1,0:T(8,128)} %bitcast.4, s32[10,2,9]{2,1,0:T(2,128)S(1)} %pad_add_fusion.codes, s32[1]{0:T(128)} %bitcast.3.inner), custom_call_target="tpu_custom_call" | custom-call | tf_op jit(solution)/shard_map/pack/pallas_call | solution.py:215
  2.1 0.5 collective-permute-start.3
  2.6 0.1 collective-permute-start.4
  2.7 0.4 collective-permute-start.5
  3.2 2.6 %collective-permute-start = (f32[783,128]{1,0:T(8,128)S(1)}, f32[783,128]{1,0:T(8,128)S(1)}, u32[]{:S(2)}, u32[]{:S(2)}) collective-permute-start(f32[783,128]{1,0:T(8,128)S(1)} %get-tuple-element.20.refs_2_.refs_3_), channel_id=1, source_target_pairs={{0,2},{1,3},{2,0},{3,1},{4,6},{5,7},{6,4},{7,5},{8,10},{9,11},{10,... | collective-permute-start | bytes 1202696 | tf_op jit(solution)/shard_map/ppermute | solution.py:33
  5.7 4.6 %collective-permute-start.8 = (f32[783,128]{1,0:T(8,128)S(1)}, f32[783,128]{1,0:T(8,128)S(1)}, u32[]{:S(2)}, u32[]{:S(2)}) collective-permute-start(f32[783,128]{1,0:T(8,128)S(1)} %get-tuple-element.21.refs_0_), channel_id=1, source_target_pairs={{0,28},{4,0},{8,4},{12,8},{16,12},{20,16},{24,20},{28,24},{1,29},{... | collective-permute-start | bytes 1202696 | tf_op jit(solution)/shard_map/ppermute | solution.py:16
  10.3 0.0 collective-permute-done.3.refs_1_
  10.3 0.0 collective-permute-start.7
  10.3 0.0 collective-permute-done.4.refs_3_.refs_4_
  10.3 0.0 collective-permute-done.5.refs_5_.refs_1_
  10.3 2.9 %sums.6.refs_6_ = f32[2,9,128,128]{3,2,1,0:T(8,128)S(1)} custom-call(f32[783,128]{1,0:T(8,128)S(1)} %get-tuple-element.21.refs_0_, f32[783,128]{1,0:T(8,128)S(1)} %collective-permute-done.3.refs_1_, f32[783,128]{1,0:T(8,128)S(1)} %get-tuple-element.20.refs_2_.refs_3_, f32[783,128]{1,0:T(8,128)S(1)} %collective-permute-done.4.refs_3_.refs_4_, ...), custom_call_target="tpu_custom_call" | custom-call | flops 1 | bytes 1 | tf_op jit(solution)/shard_map/sums/pallas_call | solution.py:236
  13.2 0.6 %collective-permute-start.6 = (f32[783,128]{1,0:T(8,128)S(1)}, f32[783,128]{1,0:T(8,128)S(1)}, u32[]{:S(2)}, u32[]{:S(2)}) collective-permute-start(f32[783,128]{1,0:T(8,128)S(1)} %get-tuple-element.23.refs_4_.refs_0_), channel_id=1, source_target_pairs={{0,2},{1,3},{2,0},{3,1},{4,6},{5,7},{6,4},{7,5},{8,10},{9,11},{10,... | collective-permute-start | bytes 1202696 | tf_op jit(solution)/shard_map/ppermute | solution.py:33
  13.8 1.8 %collective-permute-done = f32[783,128]{1,0:T(8,128)S(1)} collective-permute-done((f32[783,128]{1,0:T(8,128)S(1)}, f32[783,128]{1,0:T(8,128)S(1)}, u32[]{:S(2)}, u32[]{:S(2)}) %collective-permute-start) | collective-permute-done | bytes 400928 | tf_op jit(solution)/shard_map/ppermute | solution.py:33
  15.6 0.1 collective-permute-start.1
  15.7 1.7 %collective-permute-done.1.refs_1_.refs_3_ = f32[776,128]{1,0:T(8,128)S(1)} collective-permute-done((f32[776,128]{1,0:T(8,128)S(1)}, f32[776,128]{1,0:T(8,128)S(1)}, u32[]{:S(2)}, u32[]{:S(2)}) %collective-permute-start.1) | collective-permute-done | bytes 397344 | tf_op jit(solution)/shard_map/ppermute | solution.py:33
  17.4 2.2 %collective-permute-start.2 = (f32[783,128]{1,0:T(8,128)S(1)}, f32[783,128]{1,0:T(8,128)S(1)}, u32[]{:S(2)}, u32[]{:S(2)}) collective-permute-start(f32[783,128]{1,0:T(8,128)S(1)} %get-tuple-element.21.refs_0_), channel_id=1, source_target_pairs={{0,2},{1,3},{2,0},{3,1},{4,6},{5,7},{6,4},{7,5},{8,10},{9,11},{10,... | collective-permute-start | bytes 1202696 | tf_op jit(solution)/shard_map/ppermute | solution.py:33
  19.6 6.0 %collective-permute-done.8.above = f32[783,128]{1,0:T(8,128)S(1)} collective-permute-done((f32[783,128]{1,0:T(8,128)S(1)}, f32[783,128]{1,0:T(8,128)S(1)}, u32[]{:S(2)}, u32[]{:S(2)}) %collective-permute-start.8) | collective-permute-done | bytes 400928 | tf_op jit(solution)/shard_map/ppermute | solution.py:16
  25.7 0.0 collective-permute-done.7.below
  25.7 0.0 collective-permute-done.6
  25.7 0.1 collective-permute-start.9
  25.8 1.9 %sums.7.refs_2_ = f32[790,128]{1,0:T(8,128)S(1)} custom-call(f32[783,128]{1,0:T(8,128)S(1)} %get-tuple-element.23.refs_4_.refs_0_, f32[783,128]{1,0:T(8,128)S(1)} %collective-permute-done.5.refs_5_.refs_1_, f32[776,128]{1,0:T(8,128)S(1)} %slice.13.refs_2_.refs_4_, f32[783,128]{1,0:T(8,128)S(1)} %get-tuple-element.20.refs_2_.refs_3_, ...), custom_call_target="tpu_custom_call" | custom-call | flops 1 | bytes 1 | tf_op jit(solution)/shard_map/sums/pallas_call | solution.py:236
  27.7 0.0 collective-permute-done.9.refs_0_.refs_5_
  27.7 0.7 %sums.8 = f32[790,128]{1,0:T(8,128)S(1)} custom-call(f32[776,128]{1,0:T(8,128)S(1)} %collective-permute-done.9.refs_0_.refs_5_, f32[776,128]{1,0:T(8,128)S(1)} %collective-permute-done.1.refs_1_.refs_3_, f32[790,128]{1,0:T(8,128)S(1)} %sums.7.refs_2_), custom_call_target="tpu_custom_call" | custom-call | flops 1 | bytes 1 | tf_op jit(solution)/shard_map/sums/pallas_call | solution.py:236
  28.4 3.1 %collective-permute-start.11 = (f32[790,128]{1,0:T(8,128)S(1)}, f32[790,128]{1,0:T(8,128)S(1)}, u32[]{:S(2)}, u32[]{:S(2)}) collective-permute-start(f32[790,128]{1,0:T(8,128)S(1)} %sums.8), channel_id=1, source_target_pairs={{0,5},{1,4},{2,7},{3,6},{4,9},{5,8},{6,11},{7,10},{8,13},{9,12},{1... | collective-permute-start | bytes 1213448 | tf_op jit(solution)/shard_map/ppermute | solution.py:28
  31.5 2.0 %partials.1 = (f32[778,128]{1,0:T(8,128)S(1)}, f32[778,128]{1,0:T(8,128)S(1)}, f32[778,128]{1,0:T(8,128)S(1)}, f32[778,128]{1,0:T(8,128)S(1)}) custom-call(f32[783,128]{1,0:T(8,128)S(1)} %collective-permute-done.7.below, f32[783,128]{1,0:T(8,128)S(1)} %collective-permute-done.8.above), custom_call_target="tpu_custom_call" | custom-call | flops 1 | bytes 1 | tf_op jit(solution)/shard_map/partials/pallas_call | solution.py:270
  33.4 0.1 collective-permute-start.15
  33.5 0.0 collective-permute-done.2
  33.6 0.6 %collective-permute-start.10 = (f32[776,128]{1,0:T(8,128)S(1)}, f32[776,128]{1,0:T(8,128)S(1)}, u32[]{:S(2)}, u32[]{:S(2)}) collective-permute-start(f32[776,128]{1,0:T(8,128)S(1)} %slice.14.refs_0_.refs_2_), channel_id=1, source_target_pairs={{0,1},{1,0},{2,3},{3,2},{4,5},{5,4},{6,7},{7,6},{8,9},{9,8},{10,11... | collective-permute-start | bytes 1191944 | tf_op jit(solution)/shard_map/ppermute | solution.py:33
  34.1 0.1 collective-permute-start.14
  34.2 1.0 %collective-permute-done.15 = f32[778,128]{1,0:T(8,128)S(1)} collective-permute-done((f32[778,128]{1,0:T(8,128)S(1)}, f32[778,128]{1,0:T(8,128)S(1)}, u32[]{:S(2)}, u32[]{:S(2)}) %collective-permute-start.15) | collective-permute-done | bytes 398368 | tf_op jit(solution)/shard_map/ppermute | solution.py:33
  35.2 0.1 add.7
  35.3 0.8 %collective-permute-start.16 = (f32[778,128]{1,0:T(8,128)S(1)}, f32[778,128]{1,0:T(8,128)S(1)}, u32[]{:S(2)}, u32[]{:S(2)}) collective-permute-start(f32[778,128]{1,0:T(8,128)S(1)} %add.7), channel_id=1, source_target_pairs={{0,2},{1,3},{2,0},{3,1},{4,6},{5,7},{6,4},{7,5},{8,10},{9,11},{10,... | collective-permute-start | bytes 1195016 | tf_op jit(solution)/shard_map/ppermute | solution.py:33
  36.1 1.6 %sums.10.refs_2_ = f32[777,128]{1,0:T(8,128)S(1)} custom-call(f32[783,128]{1,0:T(8,128)S(1)} %get-tuple-element.21.refs_0_, f32[783,128]{1,0:T(8,128)S(1)} %collective-permute-done.3.refs_1_, f32[776,128]{1,0:T(8,128)S(1)} %slice.14.refs_0_.refs_2_, f32[783,128]{1,0:T(8,128)S(1)} %get-tuple-element.20.refs_2_.refs_3_, ...), custom_call_target="tpu_custom_call" | custom-call | flops 1 | bytes 1 | tf_op jit(solution)/shard_map/sums/pallas_call | solution.py:236
  37.7 0.0 collective-permute-done.10.refs_1_.refs_0_
  37.7 1.2 %sums.11 = f32[777,128]{1,0:T(8,128)S(1)} custom-call(f32[776,128]{1,0:T(8,128)S(1)} %collective-permute-done.10.refs_1_.refs_0_, f32[776,128]{1,0:T(8,128)S(1)} %collective-permute-done.1.refs_1_.refs_3_, f32[777,128]{1,0:T(8,128)S(1)} %sums.10.refs_2_), custom_call_target="tpu_custom_call" | custom-call | flops 1 | bytes 1 | tf_op jit(solution)/shard_map/sums/pallas_call | solution.py:236
  39.0 3.8 %collective-permute-start.13 = (f32[777,128]{1,0:T(8,128)S(1)}, f32[777,128]{1,0:T(8,128)S(1)}, u32[]{:S(2)}, u32[]{:S(2)}) collective-permute-start(f32[777,128]{1,0:T(8,128)S(1)} %sums.11), channel_id=1, source_target_pairs={{0,28},{4,0},{8,4},{12,8},{16,12},{20,16},{24,20},{28,24},{1,29},{... | collective-permute-start | bytes 1193480 | tf_op jit(solution)/shard_map/ppermute | solution.py:16
  42.8 0.4 collective-permute-done.11
  43.2 0.6 %collective-permute-start.12 = (f32[768,128]{1,0:T(8,128)S(1)}, f32[768,128]{1,0:T(8,128)S(1)}, u32[]{:S(2)}, u32[]{:S(2)}) collective-permute-start(f32[768,128]{1,0:T(8,128)S(1)} %slice.17), channel_id=1, source_target_pairs={{0,1},{1,0},{2,3},{3,2},{4,5},{5,4},{6,7},{7,6},{8,9},{9,8},{10,11... | collective-permute-start | bytes 1179656 | tf_op jit(solution)/shard_map/ppermute | solution.py:33
  43.8 1.7 %sums.9.base = f32[2,9,128,128]{3,2,1,0:T(8,128)S(1)} custom-call(f32[776,128]{1,0:T(8,128)S(1)} %slice.14.refs_0_.refs_2_, f32[776,128]{1,0:T(8,128)S(1)} %collective-permute-done.10.refs_1_.refs_0_, f32[776,128]{1,0:T(8,128)S(1)} %slice.16.refs_5_.refs_2_, f32[776,128]{1,0:T(8,128)S(1)} %collective-permute-done.1.refs_1_.refs_3_, ...), custom_call_target="tpu_custom_call" | custom-call | flops 1 | bytes 1 | tf_op jit(solution)/shard_map/sums/pallas_call | solution.py:236
  45.5 0.0 collective-permute-done.14
  45.5 0.1 add.6.refs_0_
  45.6 6.8 %collective-permute-done.13.upper = f32[777,128]{1,0:T(8,128)S(1)} collective-permute-done((f32[777,128]{1,0:T(8,128)S(1)}, f32[777,128]{1,0:T(8,128)S(1)}, u32[]{:S(2)}, u32[]{:S(2)}) %collective-permute-start.13) | collective-permute-done | bytes 397856 | tf_op jit(solution)/shard_map/ppermute | solution.py:16
  52.4 0.0 collective-permute-done.16.refs_1_
  52.4 0.0 collective-permute-done.12.lower
  52.4 1.2 %finish.1 = f32[2,9,128,128]{3,2,1,0:T(8,128)} custom-call(f32[2,9,128,128]{3,2,1,0:T(8,128)S(1)} %sums.9.base, f32[768,128]{1,0:T(8,128)S(1)} %collective-permute-done.12.lower, f32[777,128]{1,0:T(8,128)S(1)} %collective-permute-done.13.upper, f32[778,128]{1,0:T(8,128)S(1)} %add.6.refs_0_, f32[778,128]{1,0:T(8,128)S(1)} %collective-permute-done.16.refs_1_), custom_call_target="tpu_custom_call" | custom-call | flops 1 | bytes 1 | tf_op jit(solution)/shard_map/finish/pallas_call | solution.py:318
  (4 shorter events, 0.1 us)
Async XLA Ops:
  2.1 8.2 %collective-permute-start.3 = (f32[783,128]{1,0:T(8,128)S(1)}, f32[783,128]{1,0:T(8,128)S(1)}, u32[]{:S(2)}, u32[]{:S(2)}) collective-permute-start(f32[783,128]{1,0:T(8,128)S(1)} %get-tuple-element.21.refs_0_), channel_id=1, source_target_pairs={{0,1},{1,0},{2,3},{3,2},{4,5},{5,4},{6,7},{7,6},{8,9},{9,8},{10,11... | collective-permute-start | bytes 1202696 | tf_op jit(solution)/shard_map/ppermute | solution.py:33
  2.6 7.6 %collective-permute-start.4 = (f32[783,128]{1,0:T(8,128)S(1)}, f32[783,128]{1,0:T(8,128)S(1)}, u32[]{:S(2)}, u32[]{:S(2)}) collective-permute-start(f32[783,128]{1,0:T(8,128)S(1)} %get-tuple-element.20.refs_2_.refs_3_), channel_id=1, source_target_pairs={{0,1},{1,0},{2,3},{3,2},{4,5},{5,4},{6,7},{7,6},{8,9},{9,8},{10,11... | collective-permute-start | bytes 1202696 | tf_op jit(solution)/shard_map/ppermute | solution.py:33
  2.7 7.6 %collective-permute-start.5 = (f32[783,128]{1,0:T(8,128)S(1)}, f32[783,128]{1,0:T(8,128)S(1)}, u32[]{:S(2)}, u32[]{:S(2)}) collective-permute-start(f32[783,128]{1,0:T(8,128)S(1)} %get-tuple-element.23.refs_4_.refs_0_), channel_id=1, source_target_pairs={{0,1},{1,0},{2,3},{3,2},{4,5},{5,4},{6,7},{7,6},{8,9},{9,8},{10,11... | collective-permute-start | bytes 1202696 | tf_op jit(solution)/shard_map/ppermute | solution.py:33
  3.2 12.4 %collective-permute-start = (f32[783,128]{1,0:T(8,128)S(1)}, f32[783,128]{1,0:T(8,128)S(1)}, u32[]{:S(2)}, u32[]{:S(2)}) collective-permute-start(f32[783,128]{1,0:T(8,128)S(1)} %get-tuple-element.20.refs_2_.refs_3_), channel_id=1, source_target_pairs={{0,2},{1,3},{2,0},{3,1},{4,6},{5,7},{6,4},{7,5},{8,10},{9,11},{10,... | collective-permute-start | bytes 1202696 | tf_op jit(solution)/shard_map/ppermute | solution.py:33
  5.7 20.0 %collective-permute-start.8 = (f32[783,128]{1,0:T(8,128)S(1)}, f32[783,128]{1,0:T(8,128)S(1)}, u32[]{:S(2)}, u32[]{:S(2)}) collective-permute-start(f32[783,128]{1,0:T(8,128)S(1)} %get-tuple-element.21.refs_0_), channel_id=1, source_target_pairs={{0,28},{4,0},{8,4},{12,8},{16,12},{20,16},{24,20},{28,24},{1,29},{... | collective-permute-start | bytes 1202696 | tf_op jit(solution)/shard_map/ppermute | solution.py:16
  10.3 15.4 %collective-permute-start.7 = (f32[783,128]{1,0:T(8,128)S(1)}, f32[783,128]{1,0:T(8,128)S(1)}, u32[]{:S(2)}, u32[]{:S(2)}) collective-permute-start(f32[783,128]{1,0:T(8,128)S(1)} %get-tuple-element.23.refs_4_.refs_0_), channel_id=1, source_target_pairs={{0,4},{4,8},{8,12},{12,16},{16,20},{20,24},{24,28},{28,0},{1,5},{5... | collective-permute-start | bytes 1202696 | tf_op jit(solution)/shard_map/ppermute | solution.py:16
  13.2 12.5 %collective-permute-start.6 = (f32[783,128]{1,0:T(8,128)S(1)}, f32[783,128]{1,0:T(8,128)S(1)}, u32[]{:S(2)}, u32[]{:S(2)}) collective-permute-start(f32[783,128]{1,0:T(8,128)S(1)} %get-tuple-element.23.refs_4_.refs_0_), channel_id=1, source_target_pairs={{0,2},{1,3},{2,0},{3,1},{4,6},{5,7},{6,4},{7,5},{8,10},{9,11},{10,... | collective-permute-start | bytes 1202696 | tf_op jit(solution)/shard_map/ppermute | solution.py:33
  15.6 1.8 %collective-permute-start.1 = (f32[776,128]{1,0:T(8,128)S(1)}, f32[776,128]{1,0:T(8,128)S(1)}, u32[]{:S(2)}, u32[]{:S(2)}) collective-permute-start(f32[776,128]{1,0:T(8,128)S(1)} %slice.16.refs_5_.refs_2_), channel_id=1, source_target_pairs={{0,1},{1,0},{2,3},{3,2},{4,5},{5,4},{6,7},{7,6},{8,9},{9,8},{10,11... | collective-permute-start | bytes 1191944 | tf_op jit(solution)/shard_map/ppermute | solution.py:33
  17.4 16.1 %collective-permute-start.2 = (f32[783,128]{1,0:T(8,128)S(1)}, f32[783,128]{1,0:T(8,128)S(1)}, u32[]{:S(2)}, u32[]{:S(2)}) collective-permute-start(f32[783,128]{1,0:T(8,128)S(1)} %get-tuple-element.21.refs_0_), channel_id=1, source_target_pairs={{0,2},{1,3},{2,0},{3,1},{4,6},{5,7},{6,4},{7,5},{8,10},{9,11},{10,... | collective-permute-start | bytes 1202696 | tf_op jit(solution)/shard_map/ppermute | solution.py:33
  25.7 1.9 %collective-permute-start.9 = (f32[776,128]{1,0:T(8,128)S(1)}, f32[776,128]{1,0:T(8,128)S(1)}, u32[]{:S(2)}, u32[]{:S(2)}) collective-permute-start(f32[776,128]{1,0:T(8,128)S(1)} %slice.13.refs_2_.refs_4_), channel_id=1, source_target_pairs={{0,1},{1,0},{2,3},{3,2},{4,5},{5,4},{6,7},{7,6},{8,9},{9,8},{10,11... | collective-permute-start | bytes 1191944 | tf_op jit(solution)/shard_map/ppermute | solution.py:33
  28.4 14.8 %collective-permute-start.11 = (f32[790,128]{1,0:T(8,128)S(1)}, f32[790,128]{1,0:T(8,128)S(1)}, u32[]{:S(2)}, u32[]{:S(2)}) collective-permute-start(f32[790,128]{1,0:T(8,128)S(1)} %sums.8), channel_id=1, source_target_pairs={{0,5},{1,4},{2,7},{3,6},{4,9},{5,8},{6,11},{7,10},{8,13},{9,12},{1... | collective-permute-start | bytes 1213448 | tf_op jit(solution)/shard_map/ppermute | solution.py:28
  33.4 1.8 %collective-permute-start.15 = (f32[778,128]{1,0:T(8,128)S(1)}, f32[778,128]{1,0:T(8,128)S(1)}, u32[]{:S(2)}, u32[]{:S(2)}) collective-permute-start(f32[778,128]{1,0:T(8,128)S(1)} %get-tuple-element.31), channel_id=1, source_target_pairs={{0,1},{1,0},{2,3},{3,2},{4,5},{5,4},{6,7},{7,6},{8,9},{9,8},{10,11... | collective-permute-start | bytes 1195016 | tf_op jit(solution)/shard_map/ppermute | solution.py:33
  33.6 4.1 %collective-permute-start.10 = (f32[776,128]{1,0:T(8,128)S(1)}, f32[776,128]{1,0:T(8,128)S(1)}, u32[]{:S(2)}, u32[]{:S(2)}) collective-permute-start(f32[776,128]{1,0:T(8,128)S(1)} %slice.14.refs_0_.refs_2_), channel_id=1, source_target_pairs={{0,1},{1,0},{2,3},{3,2},{4,5},{5,4},{6,7},{7,6},{8,9},{9,8},{10,11... | collective-permute-start | bytes 1191944 | tf_op jit(solution)/shard_map/ppermute | solution.py:33
  34.1 11.4 %collective-permute-start.14 = (f32[778,128]{1,0:T(8,128)S(1)}, f32[778,128]{1,0:T(8,128)S(1)}, u32[]{:S(2)}, u32[]{:S(2)}) collective-permute-start(f32[778,128]{1,0:T(8,128)S(1)} %get-tuple-element.29), channel_id=1, source_target_pairs={{0,1},{1,0},{2,3},{3,2},{4,5},{5,4},{6,7},{7,6},{8,9},{9,8},{10,11... | collective-permute-start | bytes 1195016 | tf_op jit(solution)/shard_map/ppermute | solution.py:33
  35.3 17.1 %collective-permute-start.16 = (f32[778,128]{1,0:T(8,128)S(1)}, f32[778,128]{1,0:T(8,128)S(1)}, u32[]{:S(2)}, u32[]{:S(2)}) collective-permute-start(f32[778,128]{1,0:T(8,128)S(1)} %add.7), channel_id=1, source_target_pairs={{0,2},{1,3},{2,0},{3,1},{4,6},{5,7},{6,4},{7,5},{8,10},{9,11},{10,... | collective-permute-start | bytes 1195016 | tf_op jit(solution)/shard_map/ppermute | solution.py:33
  39.0 13.4 %collective-permute-start.13 = (f32[777,128]{1,0:T(8,128)S(1)}, f32[777,128]{1,0:T(8,128)S(1)}, u32[]{:S(2)}, u32[]{:S(2)}) collective-permute-start(f32[777,128]{1,0:T(8,128)S(1)} %sums.11), channel_id=1, source_target_pairs={{0,28},{4,0},{8,4},{12,8},{16,12},{20,16},{24,20},{28,24},{1,29},{... | collective-permute-start | bytes 1193480 | tf_op jit(solution)/shard_map/ppermute | solution.py:16
  43.2 9.2 %collective-permute-start.12 = (f32[768,128]{1,0:T(8,128)S(1)}, f32[768,128]{1,0:T(8,128)S(1)}, u32[]{:S(2)}, u32[]{:S(2)}) collective-permute-start(f32[768,128]{1,0:T(8,128)S(1)} %slice.17), channel_id=1, source_target_pairs={{0,1},{1,0},{2,3},{3,2},{4,5},{5,4},{6,7},{7,6},{8,9},{9,8},{10,11... | collective-permute-start | bytes 1179656 | tf_op jit(solution)/shard_map/ppermute | solution.py:33

commit v7 on v6

--- a/solution.py
+++ b/solution.py
@@ -180,20 +180,21 @@
                 out[lines, :] = base[0][lines, :] + acc[row, t] if base else acc[row, t]
 
 
-def finish_kernel(base, lower, upper, *refs):
-    middles, (out, result, sems) = refs[:-3], refs[-3:]
+def finish_kernel(first, base, *refs):
+    groups, (out, result, sems) = refs[:-3], refs[-3:]
     local_rows, slots, side, _ = base.shape
     per = slots // 3
+    last = first + per * len(groups)
     copies = []
     for row in range(local_rows):
-        for slot in range(per):
-            start = (row * per + slot) * side
-            lines = slice(start, start + side)
-            result[row, slot] = base[row, slot] - lower[lines, :]
-            total = sum(middle[lines, :] for middle in middles)
-            result[row, per + slot] = base[row, per + slot] - total
-            result[row, 2 * per + slot] = base[row, 2 * per + slot] - upper[lines, :]
-        copies.append(pltpu.make_async_copy(result.at[row], out.at[row], sems.at[row]))
+        for index, group in enumerate(groups):
+            for slot in range(per):
+                start = (row * per + slot) * side
+                total = sum(one[start : start + side, :] for one in group)
+                at = first + index * per + slot
+                result[row, at - first] = base[row, at] - total
+        dest = out.at[row, pl.ds(first, last - first)]
+        copies.append(pltpu.make_async_copy(result.at[row], dest, sems.at[row]))
         copies[-1].start()
     for copy in copies:
         copy.wait()
@@ -305,7 +306,7 @@
             for distance, share in shares.items()
             if not distance & bit
         }
-    far_share = across(shares[parts // 2], [below_next]) if parts > 1 else []
+    far_share = across(shares[parts // 2], [below_next, shares[0]]) if parts > 1 else []
     far_lowers = spread(tied(far_lower, below_next)) if far_lower else []
     above_next = strip_sums([lowers + far_lowers, all_middles], 0, ((1, per),), 2 * per, 9)
     to_above_next = shifted(above_next, -1)
@@ -315,19 +316,32 @@
         base = sums(groups, 1, own_plan, 0, slots, near, [base])
         to_below_next = swapped(to_below_next[:lines], 1)
     middle_shares = [shares[0], *far_share]
-    return pl.pallas_call(
-        finish_kernel,
-        out_shape=jax.ShapeDtypeStruct(density.shape, jnp.float32),
-        in_specs=[vectors] * (3 + len(middle_shares)),
-        out_specs=in_hbm,
-        scratch_shapes=[
-            pltpu.VMEM(density.shape, jnp.float32),
-            pltpu.SemaphoreType.DMA((local_rows,)),
-        ],
-        compiler_params=pltpu.CompilerParams(vmem_limit_bytes=16 << 20),
-        cost_estimate=pl.CostEstimate(flops=1, bytes_accessed=1, transcendentals=0),
-        name="finish",
-    )(base, to_below_next, to_above_next, *middle_shares)
+    def finish(first, groups, result=()):
+        counts = [len(group) for group in groups]
+        flat = [one for group in groups for one in group]
+
+        def kernel(base, *refs):
+            ends = [sum(counts[: i + 1]) for i in range(len(counts))]
+            grouped = [refs[end - count : end] for end, count in zip(ends, counts)]
+            finish_kernel(first, base, *grouped, *refs[-3:])
+
+        return pl.pallas_call(
+            kernel,
+            out_shape=jax.ShapeDtypeStruct(density.shape, jnp.float32),
+            in_specs=[vectors] * (1 + len(flat)) + [in_hbm] * len(result),
+            out_specs=in_hbm,
+            scratch_shapes=[
+                pltpu.VMEM((local_rows, per * len(groups), side, side), jnp.float32),
+                pltpu.SemaphoreType.DMA((local_rows,)),
+            ],
+            input_output_aliases={1 + len(flat): 0} if result else {},
+            compiler_params=pltpu.CompilerParams(vmem_limit_bytes=16 << 20),
+            cost_estimate=pl.CostEstimate(flops=1, bytes_accessed=1, transcendentals=0),
+            name="finish",
+        )(base, *flat, *result)
+
+    purified = finish(0, [[to_below_next], middle_shares])
+    return finish(2 * per, [[to_above_next]], [purified])
 
 
 def solution(mesh):

time: 54 us -> 53.4 us (0.989)
  starting transfers between devices: 20.1 us -> 18.5 us
  waiting for transfers between devices: 17.8 us -> 19.1 us
    ppermute x13, waiting for transfers between devices: 4.55 us -> 7.88 us  [swapped(): lax.ppermute(value, 'inner', [(i, i ^ distance) for i in range(count)])]
    ppermute x3, waiting for transfers between devices: 12.8 us -> 10.2 us  [shifted(): return lax.ppermute(value, 'blk', pairs)]
    ppermute x13, starting transfers between devices: 8.67 us -> 6.99 us  [swapped(): lax.ppermute(value, 'inner', [(i, i ^ distance) for i in range(count)])]
    ppermute x3, starting transfers between devices: 8.37 us -> 9.2 us  [shifted(): return lax.ppermute(value, 'blk', pairs)]
    ppermute x1, starting transfers between devices: 3.1 us -> 2.31 us  [shifted_aslant(): return lax.ppermute(value, ('blk', 'inner'), pairs)]
    ppermute x1, waiting for transfers between devices: 0.43 us -> 1.05 us  [shifted_aslant(): return lax.ppermute(value, ('blk', 'inner'), pairs)]
    pallas_call x1 -> x2, Pallas kernels: 1.16 us -> 1.74 us  [finish(): pl.pallas_call(kernel, out_shape=jax.ShapeDtypeStruct(density.shape, jnp....]
  transfers between devices with their start and end apart: 17 -> 17, of which waited for: 6 -> 8; matrix products, arithmetic and copies ran while one was open for 0% -> 0% of each run, Pallas kernels for 22% -> 23%
where the time goes in v7:
time: 53.4 us
  waiting for transfers between devices  19.1 us (36%)
  starting transfers between devices  18.5 us (35%)
  Pallas kernels  14.7 us (28%)
  other arithmetic  0.83 us (2%)
    ppermute x3, waiting for transfers between devices, shifted(): return lax.ppermute(value, 'blk', pairs)  10.2 us
    pallas_call x6, Pallas kernels, sums(): pl.pallas_call(functools.partial(sums_kernel, dims, plan), out_shape=jax....  9.63 us
    ppermute x3, starting transfers between devices, shifted(): return lax.ppermute(value, 'blk', pairs)  9.2 us
    ppermute x13, waiting for transfers between devices, swapped(): lax.ppermute(value, 'inner', [(i, i ^ distance) for i in range(count)])  7.88 us
    ppermute x13, starting transfers between devices, swapped(): lax.ppermute(value, 'inner', [(i, i ^ distance) for i in range(count)])  6.99 us
    ppermute x1, starting transfers between devices, shifted_aslant(): return lax.ppermute(value, ('blk', 'inner'), pairs)  2.31 us
    pallas_call x1, Pallas kernels, partials(): pl.pallas_call(functools.partial(partial_kernel, (parts, local_rows, slot...  1.94 us
    pallas_call x2, Pallas kernels, finish(): pl.pallas_call(kernel, out_shape=jax.ShapeDtypeStruct(density.shape, jnp....  1.74 us
  transfers between devices with their start and end apart: 17, of which 8 were waited for; matrix products, arithmetic and copies ran while one was open for 0% of the time, Pallas kernels for 23%

profile of v7, /device:TPU:0, one launch (start us, length us, event | category | flops | bytes accessed | tf_op | source)
XLA Modules:
  0.0 53.4 jit_solution(478187148177015797)
XLA Ops:
  0.0 0.7 %pad_add_fusion.codes = s32[10,2,9]{2,1,0:T(2,128)S(1)} fusion(s32[1,2,9]{2,1,0:T(2,128)} %bitcast.6, s32[9,2,9]{2,1,0:T(2,128)} %bitcast.5), kind=kLoop, calls=%fused_computation | loop fusion | flops 180 | bytes 1440 | tf_op jit(solution)/shard_map/concatenate | solution.py:215
  0.7 1.4 %pack.1 = (f32[783,128]{1,0:T(8,128)S(1)}, f32[783,128]{1,0:T(8,128)S(1)}, f32[783,128]{1,0:T(8,128)S(1)}) custom-call(f32[2304,128]{1,0:T(8,128)} %bitcast.4, s32[10,2,9]{2,1,0:T(2,128)S(1)} %pad_add_fusion.codes, s32[1]{0:T(128)} %bitcast.3.inner), custom_call_target="tpu_custom_call" | custom-call | tf_op jit(solution)/shard_map/pack/pallas_call | solution.py:216
  2.1 0.5 collective-permute-start.3
  2.6 0.1 collective-permute-start.4
  2.7 0.4 collective-permute-start.5
  3.2 2.6 %collective-permute-start = (f32[783,128]{1,0:T(8,128)S(1)}, f32[783,128]{1,0:T(8,128)S(1)}, u32[]{:S(2)}, u32[]{:S(2)}) collective-permute-start(f32[783,128]{1,0:T(8,128)S(1)} %get-tuple-element.20.refs_2_.refs_3_), channel_id=1, source_target_pairs={{0,2},{1,3},{2,0},{3,1},{4,6},{5,7},{6,4},{7,5},{8,10},{9,11},{10,... | collective-permute-start | bytes 1202696 | tf_op jit(solution)/shard_map/ppermute | solution.py:33
  5.7 4.6 %collective-permute-start.8 = (f32[783,128]{1,0:T(8,128)S(1)}, f32[783,128]{1,0:T(8,128)S(1)}, u32[]{:S(2)}, u32[]{:S(2)}) collective-permute-start(f32[783,128]{1,0:T(8,128)S(1)} %get-tuple-element.21.refs_0_), channel_id=1, source_target_pairs={{0,28},{4,0},{8,4},{12,8},{16,12},{20,16},{24,20},{28,24},{1,29},{... | collective-permute-start | bytes 1202696 | tf_op jit(solution)/shard_map/ppermute | solution.py:16
  10.3 0.0 collective-permute-done.3.refs_1_
  10.3 0.0 collective-permute-start.7
  10.3 0.0 collective-permute-done.4.refs_3_.refs_4_
  10.3 0.0 collective-permute-done.5.refs_5_.refs_1_
  10.3 2.1 %sums.6.refs_6_ = f32[2,9,128,128]{3,2,1,0:T(8,128)S(1)} custom-call(f32[783,128]{1,0:T(8,128)S(1)} %get-tuple-element.21.refs_0_, f32[783,128]{1,0:T(8,128)S(1)} %collective-permute-done.3.refs_1_, f32[783,128]{1,0:T(8,128)S(1)} %get-tuple-element.20.refs_2_.refs_3_, f32[783,128]{1,0:T(8,128)S(1)} %collective-permute-done.4.refs_3_.refs_4_, ...), custom_call_target="tpu_custom_call" | custom-call | flops 1 | bytes 1 | tf_op jit(solution)/shard_map/sums/pallas_call | solution.py:237
  12.4 0.2 collective-permute-start.6
  12.6 3.3 %collective-permute-done = f32[783,128]{1,0:T(8,128)S(1)} collective-permute-done((f32[783,128]{1,0:T(8,128)S(1)}, f32[783,128]{1,0:T(8,128)S(1)}, u32[]{:S(2)}, u32[]{:S(2)}) %collective-permute-start) | collective-permute-done | bytes 400928 | tf_op jit(solution)/shard_map/ppermute | solution.py:33
  15.9 0.1 collective-permute-start.1
  16.0 1.7 %collective-permute-done.1.refs_1_.refs_3_ = f32[776,128]{1,0:T(8,128)S(1)} collective-permute-done((f32[776,128]{1,0:T(8,128)S(1)}, f32[776,128]{1,0:T(8,128)S(1)}, u32[]{:S(2)}, u32[]{:S(2)}) %collective-permute-start.1) | collective-permute-done | bytes 397344 | tf_op jit(solution)/shard_map/ppermute | solution.py:33
  17.7 1.9 %collective-permute-start.2 = (f32[783,128]{1,0:T(8,128)S(1)}, f32[783,128]{1,0:T(8,128)S(1)}, u32[]{:S(2)}, u32[]{:S(2)}) collective-permute-start(f32[783,128]{1,0:T(8,128)S(1)} %get-tuple-element.21.refs_0_), channel_id=1, source_target_pairs={{0,2},{1,3},{2,0},{3,1},{4,6},{5,7},{6,4},{7,5},{8,10},{9,11},{10,... | collective-permute-start | bytes 1202696 | tf_op jit(solution)/shard_map/ppermute | solution.py:33
  19.6 6.0 %collective-permute-done.8.above = f32[783,128]{1,0:T(8,128)S(1)} collective-permute-done((f32[783,128]{1,0:T(8,128)S(1)}, f32[783,128]{1,0:T(8,128)S(1)}, u32[]{:S(2)}, u32[]{:S(2)}) %collective-permute-start.8) | collective-permute-done | bytes 400928 | tf_op jit(solution)/shard_map/ppermute | solution.py:16
  25.7 0.0 collective-permute-done.7.below
  25.7 0.0 collective-permute-done.6
  25.7 0.1 collective-permute-start.9
  25.8 2.6 %sums.7.refs_2_ = f32[790,128]{1,0:T(8,128)S(1)} custom-call(f32[783,128]{1,0:T(8,128)S(1)} %get-tuple-element.23.refs_4_.refs_0_, f32[783,128]{1,0:T(8,128)S(1)} %collective-permute-done.5.refs_5_.refs_1_, f32[776,128]{1,0:T(8,128)S(1)} %slice.13.refs_2_.refs_4_, f32[783,128]{1,0:T(8,128)S(1)} %get-tuple-element.20.refs_2_.refs_3_, ...), custom_call_target="tpu_custom_call" | custom-call | flops 1 | bytes 1 | tf_op jit(solution)/shard_map/sums/pallas_call | solution.py:237
  28.5 0.0 collective-permute-done.9.refs_0_.refs_5_
  28.5 1.0 %sums.8 = f32[790,128]{1,0:T(8,128)S(1)} custom-call(f32[776,128]{1,0:T(8,128)S(1)} %collective-permute-done.9.refs_0_.refs_5_, f32[776,128]{1,0:T(8,128)S(1)} %collective-permute-done.1.refs_1_.refs_3_, f32[790,128]{1,0:T(8,128)S(1)} %sums.7.refs_2_), custom_call_target="tpu_custom_call" | custom-call | flops 1 | bytes 1 | tf_op jit(solution)/shard_map/sums/pallas_call | solution.py:237
  29.4 2.3 %collective-permute-start.12 = (f32[790,128]{1,0:T(8,128)S(1)}, f32[790,128]{1,0:T(8,128)S(1)}, u32[]{:S(2)}, u32[]{:S(2)}) collective-permute-start(f32[790,128]{1,0:T(8,128)S(1)} %sums.8), channel_id=1, source_target_pairs={{0,5},{1,4},{2,7},{3,6},{4,9},{5,8},{6,11},{7,10},{8,13},{9,12},{1... | collective-permute-start | bytes 1213448 | tf_op jit(solution)/shard_map/ppermute | solution.py:28
  31.7 1.9 %partials.1 = (f32[778,128]{1,0:T(8,128)S(1)}, f32[778,128]{1,0:T(8,128)S(1)}, f32[778,128]{1,0:T(8,128)S(1)}, f32[778,128]{1,0:T(8,128)S(1)}) custom-call(f32[783,128]{1,0:T(8,128)S(1)} %collective-permute-done.7.below, f32[783,128]{1,0:T(8,128)S(1)} %collective-permute-done.8.above), custom_call_target="tpu_custom_call" | custom-call | flops 1 | bytes 1 | tf_op jit(solution)/shard_map/partials/pallas_call | solution.py:271
  33.7 0.1 collective-permute-start.14
  33.8 0.5 collective-permute-start.15
  34.3 0.0 collective-permute-done.2
  34.3 0.1 collective-permute-start.10
  34.4 1.0 %collective-permute-done.14 = f32[778,128]{1,0:T(8,128)S(1)} collective-permute-done((f32[778,128]{1,0:T(8,128)S(1)}, f32[778,128]{1,0:T(8,128)S(1)}, u32[]{:S(2)}, u32[]{:S(2)}) %collective-permute-start.14) | collective-permute-done | bytes 398368 | tf_op jit(solution)/shard_map/ppermute | solution.py:33
  35.5 0.1 add.6.refs_1_
  35.5 0.5 collective-permute-done.15
  36.1 0.1 add.7
  36.1 0.3 collective-permute-start.16
  36.4 0.8 %sums.10.refs_2_ = f32[777,128]{1,0:T(8,128)S(1)} custom-call(f32[783,128]{1,0:T(8,128)S(1)} %get-tuple-element.21.refs_0_, f32[783,128]{1,0:T(8,128)S(1)} %collective-permute-done.3.refs_1_, f32[776,128]{1,0:T(8,128)S(1)} %slice.14.refs_0_.refs_2_, f32[783,128]{1,0:T(8,128)S(1)} %get-tuple-element.20.refs_2_.refs_3_, ...), custom_call_target="tpu_custom_call" | custom-call | flops 1 | bytes 1 | tf_op jit(solution)/shard_map/sums/pallas_call | solution.py:237
  37.2 0.0 collective-permute-done.10.refs_1_.refs_0_
  37.2 1.0 %sums.11 = f32[777,128]{1,0:T(8,128)S(1)} custom-call(f32[776,128]{1,0:T(8,128)S(1)} %collective-permute-done.10.refs_1_.refs_0_, f32[776,128]{1,0:T(8,128)S(1)} %collective-permute-done.1.refs_1_.refs_3_, f32[777,128]{1,0:T(8,128)S(1)} %sums.10.refs_2_), custom_call_target="tpu_custom_call" | custom-call | flops 1 | bytes 1 | tf_op jit(solution)/shard_map/sums/pallas_call | solution.py:237
  38.2 4.6 %collective-permute-start.11 = (f32[777,128]{1,0:T(8,128)S(1)}, f32[777,128]{1,0:T(8,128)S(1)}, u32[]{:S(2)}, u32[]{:S(2)}) collective-permute-start(f32[777,128]{1,0:T(8,128)S(1)} %sums.11), channel_id=1, source_target_pairs={{0,28},{4,0},{8,4},{12,8},{16,12},{20,16},{24,20},{28,24},{1,29},{... | collective-permute-start | bytes 1193480 | tf_op jit(solution)/shard_map/ppermute | solution.py:16
  42.9 1.0 %collective-permute-done.12 = f32[790,128]{1,0:T(8,128)S(1)} collective-permute-done((f32[790,128]{1,0:T(8,128)S(1)}, f32[790,128]{1,0:T(8,128)S(1)}, u32[]{:S(2)}, u32[]{:S(2)}) %collective-permute-start.12) | collective-permute-done | bytes 404512 | tf_op jit(solution)/shard_map/ppermute | solution.py:28
  43.9 0.1 collective-permute-start.13
  44.1 2.1 %sums.9.base = f32[2,9,128,128]{3,2,1,0:T(8,128)S(1)} custom-call(f32[776,128]{1,0:T(8,128)S(1)} %slice.14.refs_0_.refs_2_, f32[776,128]{1,0:T(8,128)S(1)} %collective-permute-done.10.refs_1_.refs_0_, f32[776,128]{1,0:T(8,128)S(1)} %slice.16.refs_5_.refs_2_, f32[776,128]{1,0:T(8,128)S(1)} %collective-permute-done.1.refs_1_.refs_3_, ...), custom_call_target="tpu_custom_call" | custom-call | flops 1 | bytes 1 | tf_op jit(solution)/shard_map/sums/pallas_call | solution.py:237
  46.2 1.3 %collective-permute-done.16.refs_2_ = f32[778,128]{1,0:T(8,128)S(1)} collective-permute-done((f32[778,128]{1,0:T(8,128)S(1)}, f32[778,128]{1,0:T(8,128)S(1)}, u32[]{:S(2)}, u32[]{:S(2)}) %collective-permute-start.16) | collective-permute-done | bytes 398368 | tf_op jit(solution)/shard_map/ppermute | solution.py:33
  47.5 0.0 collective-permute-done.13.refs_0_
  47.5 1.0 %finish.2.refs_1_ = f32[2,9,128,128]{3,2,1,0:T(8,128)} custom-call(f32[2,9,128,128]{3,2,1,0:T(8,128)S(1)} %sums.9.base, f32[768,128]{1,0:T(8,128)S(1)} %collective-permute-done.13.refs_0_, f32[778,128]{1,0:T(8,128)S(1)} %add.6.refs_1_, f32[778,128]{1,0:T(8,128)S(1)} %collective-permute-done.16.refs_2_), custom_call_target="tpu_custom_call" | custom-call | flops 1 | bytes 1 | tf_op jit(solution)/shard_map/finish/pallas_call | solution.py:328
  48.5 4.2 %collective-permute-done.11.refs_0_ = f32[777,128]{1,0:T(8,128)S(1)} collective-permute-done((f32[777,128]{1,0:T(8,128)S(1)}, f32[777,128]{1,0:T(8,128)S(1)}, u32[]{:S(2)}, u32[]{:S(2)}) %collective-permute-start.11) | collective-permute-done | bytes 397856 | tf_op jit(solution)/shard_map/ppermute | solution.py:16
  52.6 0.8 %finish.3 = f32[2,9,128,128]{3,2,1,0:T(8,128)} custom-call(f32[2,9,128,128]{3,2,1,0:T(8,128)S(1)} %sums.9.base, f32[777,128]{1,0:T(8,128)S(1)} %collective-permute-done.11.refs_0_, f32[2,9,128,128]{3,2,1,0:T(8,128)} %finish.2.refs_1_), custom_call_target="tpu_custom_call", output_to_operand_aliasing={{}: (2, {})} | custom-call | flops 1 | bytes 1 | tf_op jit(solution)/shard_map/finish/pallas_call | solution.py:328
  (4 shorter events, 0.1 us)
Async XLA Ops:
  2.1 8.2 %collective-permute-start.3 = (f32[783,128]{1,0:T(8,128)S(1)}, f32[783,128]{1,0:T(8,128)S(1)}, u32[]{:S(2)}, u32[]{:S(2)}) collective-permute-start(f32[783,128]{1,0:T(8,128)S(1)} %get-tuple-element.21.refs_0_), channel_id=1, source_target_pairs={{0,1},{1,0},{2,3},{3,2},{4,5},{5,4},{6,7},{7,6},{8,9},{9,8},{10,11... | collective-permute-start | bytes 1202696 | tf_op jit(solution)/shard_map/ppermute | solution.py:33
  2.6 7.6 %collective-permute-start.4 = (f32[783,128]{1,0:T(8,128)S(1)}, f32[783,128]{1,0:T(8,128)S(1)}, u32[]{:S(2)}, u32[]{:S(2)}) collective-permute-start(f32[783,128]{1,0:T(8,128)S(1)} %get-tuple-element.20.refs_2_.refs_3_), channel_id=1, source_target_pairs={{0,1},{1,0},{2,3},{3,2},{4,5},{5,4},{6,7},{7,6},{8,9},{9,8},{10,11... | collective-permute-start | bytes 1202696 | tf_op jit(solution)/shard_map/ppermute | solution.py:33
  2.7 7.6 %collective-permute-start.5 = (f32[783,128]{1,0:T(8,128)S(1)}, f32[783,128]{1,0:T(8,128)S(1)}, u32[]{:S(2)}, u32[]{:S(2)}) collective-permute-start(f32[783,128]{1,0:T(8,128)S(1)} %get-tuple-element.23.refs_4_.refs_0_), channel_id=1, source_target_pairs={{0,1},{1,0},{2,3},{3,2},{4,5},{5,4},{6,7},{7,6},{8,9},{9,8},{10,11... | collective-permute-start | bytes 1202696 | tf_op jit(solution)/shard_map/ppermute | solution.py:33
  3.2 12.7 %collective-permute-start = (f32[783,128]{1,0:T(8,128)S(1)}, f32[783,128]{1,0:T(8,128)S(1)}, u32[]{:S(2)}, u32[]{:S(2)}) collective-permute-start(f32[783,128]{1,0:T(8,128)S(1)} %get-tuple-element.20.refs_2_.refs_3_), channel_id=1, source_target_pairs={{0,2},{1,3},{2,0},{3,1},{4,6},{5,7},{6,4},{7,5},{8,10},{9,11},{10,... | collective-permute-start | bytes 1202696 | tf_op jit(solution)/shard_map/ppermute | solution.py:33
  5.7 20.0 %collective-permute-start.8 = (f32[783,128]{1,0:T(8,128)S(1)}, f32[783,128]{1,0:T(8,128)S(1)}, u32[]{:S(2)}, u32[]{:S(2)}) collective-permute-start(f32[783,128]{1,0:T(8,128)S(1)} %get-tuple-element.21.refs_0_), channel_id=1, source_target_pairs={{0,28},{4,0},{8,4},{12,8},{16,12},{20,16},{24,20},{28,24},{1,29},{... | collective-permute-start | bytes 1202696 | tf_op jit(solution)/shard_map/ppermute | solution.py:16
  10.3 15.4 %collective-permute-start.7 = (f32[783,128]{1,0:T(8,128)S(1)}, f32[783,128]{1,0:T(8,128)S(1)}, u32[]{:S(2)}, u32[]{:S(2)}) collective-permute-start(f32[783,128]{1,0:T(8,128)S(1)} %get-tuple-element.23.refs_4_.refs_0_), channel_id=1, source_target_pairs={{0,4},{4,8},{8,12},{12,16},{16,20},{20,24},{24,28},{28,0},{1,5},{5... | collective-permute-start | bytes 1202696 | tf_op jit(solution)/shard_map/ppermute | solution.py:16
  12.4 13.3 %collective-permute-start.6 = (f32[783,128]{1,0:T(8,128)S(1)}, f32[783,128]{1,0:T(8,128)S(1)}, u32[]{:S(2)}, u32[]{:S(2)}) collective-permute-start(f32[783,128]{1,0:T(8,128)S(1)} %get-tuple-element.23.refs_4_.refs_0_), channel_id=1, source_target_pairs={{0,2},{1,3},{2,0},{3,1},{4,6},{5,7},{6,4},{7,5},{8,10},{9,11},{10,... | collective-permute-start | bytes 1202696 | tf_op jit(solution)/shard_map/ppermute | solution.py:33
  15.9 1.8 %collective-permute-start.1 = (f32[776,128]{1,0:T(8,128)S(1)}, f32[776,128]{1,0:T(8,128)S(1)}, u32[]{:S(2)}, u32[]{:S(2)}) collective-permute-start(f32[776,128]{1,0:T(8,128)S(1)} %slice.16.refs_5_.refs_2_), channel_id=1, source_target_pairs={{0,1},{1,0},{2,3},{3,2},{4,5},{5,4},{6,7},{7,6},{8,9},{9,8},{10,11... | collective-permute-start | bytes 1191944 | tf_op jit(solution)/shard_map/ppermute | solution.py:33
  17.7 16.6 %collective-permute-start.2 = (f32[783,128]{1,0:T(8,128)S(1)}, f32[783,128]{1,0:T(8,128)S(1)}, u32[]{:S(2)}, u32[]{:S(2)}) collective-permute-start(f32[783,128]{1,0:T(8,128)S(1)} %get-tuple-element.21.refs_0_), channel_id=1, source_target_pairs={{0,2},{1,3},{2,0},{3,1},{4,6},{5,7},{6,4},{7,5},{8,10},{9,11},{10,... | collective-permute-start | bytes 1202696 | tf_op jit(solution)/shard_map/ppermute | solution.py:33
  25.7 2.7 %collective-permute-start.9 = (f32[776,128]{1,0:T(8,128)S(1)}, f32[776,128]{1,0:T(8,128)S(1)}, u32[]{:S(2)}, u32[]{:S(2)}) collective-permute-start(f32[776,128]{1,0:T(8,128)S(1)} %slice.13.refs_2_.refs_4_), channel_id=1, source_target_pairs={{0,1},{1,0},{2,3},{3,2},{4,5},{5,4},{6,7},{7,6},{8,9},{9,8},{10,11... | collective-permute-start | bytes 1191944 | tf_op jit(solution)/shard_map/ppermute | solution.py:33
  29.4 14.5 %collective-permute-start.12 = (f32[790,128]{1,0:T(8,128)S(1)}, f32[790,128]{1,0:T(8,128)S(1)}, u32[]{:S(2)}, u32[]{:S(2)}) collective-permute-start(f32[790,128]{1,0:T(8,128)S(1)} %sums.8), channel_id=1, source_target_pairs={{0,5},{1,4},{2,7},{3,6},{4,9},{5,8},{6,11},{7,10},{8,13},{9,12},{1... | collective-permute-start | bytes 1213448 | tf_op jit(solution)/shard_map/ppermute | solution.py:28
  33.7 1.8 %collective-permute-start.14 = (f32[778,128]{1,0:T(8,128)S(1)}, f32[778,128]{1,0:T(8,128)S(1)}, u32[]{:S(2)}, u32[]{:S(2)}) collective-permute-start(f32[778,128]{1,0:T(8,128)S(1)} %get-tuple-element.29), channel_id=1, source_target_pairs={{0,1},{1,0},{2,3},{3,2},{4,5},{5,4},{6,7},{7,6},{8,9},{9,8},{10,11... | collective-permute-start | bytes 1195016 | tf_op jit(solution)/shard_map/ppermute | solution.py:33
  33.8 2.3 %collective-permute-start.15 = (f32[778,128]{1,0:T(8,128)S(1)}, f32[778,128]{1,0:T(8,128)S(1)}, u32[]{:S(2)}, u32[]{:S(2)}) collective-permute-start(f32[778,128]{1,0:T(8,128)S(1)} %get-tuple-element.31), channel_id=1, source_target_pairs={{0,1},{1,0},{2,3},{3,2},{4,5},{5,4},{6,7},{7,6},{8,9},{9,8},{10,11... | collective-permute-start | bytes 1195016 | tf_op jit(solution)/shard_map/ppermute | solution.py:33
  34.3 2.9 %collective-permute-start.10 = (f32[776,128]{1,0:T(8,128)S(1)}, f32[776,128]{1,0:T(8,128)S(1)}, u32[]{:S(2)}, u32[]{:S(2)}) collective-permute-start(f32[776,128]{1,0:T(8,128)S(1)} %slice.14.refs_0_.refs_2_), channel_id=1, source_target_pairs={{0,1},{1,0},{2,3},{3,2},{4,5},{5,4},{6,7},{7,6},{8,9},{9,8},{10,11... | collective-permute-start | bytes 1191944 | tf_op jit(solution)/shard_map/ppermute | solution.py:33
  36.1 11.4 %collective-permute-start.16 = (f32[778,128]{1,0:T(8,128)S(1)}, f32[778,128]{1,0:T(8,128)S(1)}, u32[]{:S(2)}, u32[]{:S(2)}) collective-permute-start(f32[778,128]{1,0:T(8,128)S(1)} %add.7), channel_id=1, source_target_pairs={{0,2},{1,3},{2,0},{3,1},{4,6},{5,7},{6,4},{7,5},{8,10},{9,11},{10,... | collective-permute-start | bytes 1195016 | tf_op jit(solution)/shard_map/ppermute | solution.py:33
  38.2 14.4 %collective-permute-start.11 = (f32[777,128]{1,0:T(8,128)S(1)}, f32[777,128]{1,0:T(8,128)S(1)}, u32[]{:S(2)}, u32[]{:S(2)}) collective-permute-start(f32[777,128]{1,0:T(8,128)S(1)} %sums.11), channel_id=1, source_target_pairs={{0,28},{4,0},{8,4},{12,8},{16,12},{20,16},{24,20},{28,24},{1,29},{... | collective-permute-start | bytes 1193480 | tf_op jit(solution)/shard_map/ppermute | solution.py:16
  43.9 3.6 %collective-permute-start.13 = (f32[768,128]{1,0:T(8,128)S(1)}, f32[768,128]{1,0:T(8,128)S(1)}, u32[]{:S(2)}, u32[]{:S(2)}) collective-permute-start(f32[768,128]{1,0:T(8,128)S(1)} %slice.17), channel_id=1, source_target_pairs={{0,1},{1,0},{2,3},{3,2},{4,5},{5,4},{6,7},{7,6},{8,9},{9,8},{10,11... | collective-permute-start | bytes 1179656 | tf_op jit(solution)/shard_map/ppermute | solution.py:33

commit v8 on v7

--- a/solution.py
+++ b/solution.py
@@ -255,11 +255,11 @@
 
     def strip_sums(groups, a_at, plan, first, spare):
         early = parts // 2 + 1
-        total = sums([group[:early] for group in groups], a_at, plan, first, per, spare=spare)
+        begun = total = sums([group[:early] for group in groups], a_at, plan, first, per, spare=spare)
         if parts > early:
             rest = [group[early:] for group in groups]
             total = sums(rest, a_at, plan, first, per, early, [total], spare)
-        return total
+        return total, begun
 
     def spread(far):
         return [one for value in far for one in halves(value[:used_rows])]
@@ -296,7 +296,7 @@
     far_lower = across(lower, far_middles)
     all_middles = middles + far_middles
     far_uppers = spread(tied(far_upper, below, above))
-    below_next = strip_sums([uppers + far_uppers, all_middles], 0, ((1, per),), 0, 22)
+    below_next, _ = strip_sums([uppers + far_uppers, all_middles], 0, ((1, per),), 0, 22)
     to_below_next = shifted_aslant(below_next, 1)
 
     shares = dict(enumerate(partials(*tied([below, above], below_next))))
@@ -306,9 +306,9 @@
             for distance, share in shares.items()
             if not distance & bit
         }
-    far_share = across(shares[parts // 2], [below_next, shares[0]]) if parts > 1 else []
     far_lowers = spread(tied(far_lower, below_next)) if far_lower else []
-    above_next = strip_sums([lowers + far_lowers, all_middles], 0, ((1, per),), 2 * per, 9)
+    above_next, begun = strip_sums([lowers + far_lowers, all_middles], 0, ((1, per),), 2 * per, 9)
+    far_share = across(shares[parts // 2], [begun, shares[0]]) if parts > 1 else []
     to_above_next = shifted(above_next, -1)
     if far_lowers:
         near = len(lowers)

time: 53.4 us -> 53.3 us (level)
  waiting for transfers between devices: 19.1 us -> 16.2 us
  starting transfers between devices: 18.5 us -> 20.8 us
    ppermute x13, starting transfers between devices: 6.99 us -> 8.46 us  [swapped(): lax.ppermute(value, 'inner', [(i, i ^ distance) for i in range(count)])]
    ppermute x3, waiting for transfers between devices: 10.2 us -> 8.8 us  [shifted(): return lax.ppermute(value, 'blk', pairs)]
    ppermute x1, waiting for transfers between devices: 1.05 us -> 0.05 us  [shifted_aslant(): return lax.ppermute(value, ('blk', 'inner'), pairs)]
    ppermute x1, starting transfers between devices: 2.31 us -> 3.26 us  [shifted_aslant(): return lax.ppermute(value, ('blk', 'inner'), pairs)]
    ppermute x13, waiting for transfers between devices: 7.88 us -> 7.32 us  [swapped(): lax.ppermute(value, 'inner', [(i, i ^ distance) for i in range(count)])]
  transfers between devices with their start and end apart: 17 -> 17, of which waited for: 8 -> 6; matrix products, arithmetic and copies ran while one was open for 0% -> 0% of each run, Pallas kernels for 23% -> 24%
where the time goes in v8:
time: 53.3 us; the launch traced here: 52.9 us
  starting transfers between devices  20.8 us (39%)
  waiting for transfers between devices  16.2 us (30%)
  Pallas kernels  14.8 us (28%)
  other arithmetic  0.83 us (2%)
    pallas_call x6, Pallas kernels, sums(): pl.pallas_call(functools.partial(sums_kernel, dims, plan), out_shape=jax....  9.73 us
    ppermute x3, starting transfers between devices, shifted(): return lax.ppermute(value, 'blk', pairs)  9.11 us
    ppermute x3, waiting for transfers between devices, shifted(): return lax.ppermute(value, 'blk', pairs)  8.8 us
    ppermute x13, starting transfers between devices, swapped(): lax.ppermute(value, 'inner', [(i, i ^ distance) for i in range(count)])  8.46 us
    ppermute x13, waiting for transfers between devices, swapped(): lax.ppermute(value, 'inner', [(i, i ^ distance) for i in range(count)])  7.32 us
    ppermute x1, starting transfers between devices, shifted_aslant(): return lax.ppermute(value, ('blk', 'inner'), pairs)  3.26 us
    pallas_call x1, Pallas kernels, partials(): pl.pallas_call(functools.partial(partial_kernel, (parts, local_rows, slot...  1.95 us
    pallas_call x2, Pallas kernels, finish(): pl.pallas_call(kernel, out_shape=jax.ShapeDtypeStruct(density.shape, jnp....  1.74 us
  transfers between devices with their start and end apart: 17, of which 6 were waited for; matrix products, arithmetic and copies ran while one was open for 0% of the time, Pallas kernels for 24%

profile of v8, /device:TPU:0, one launch (start us, length us, event | category | flops | bytes accessed | tf_op | source)
XLA Modules:
  0.0 52.9 jit_solution(424555798810120225)
XLA Ops:
  0.0 0.7 %pad_add_fusion.codes = s32[10,2,9]{2,1,0:T(2,128)S(1)} fusion(s32[1,2,9]{2,1,0:T(2,128)} %bitcast.6, s32[9,2,9]{2,1,0:T(2,128)} %bitcast.5), kind=kLoop, calls=%fused_computation | loop fusion | flops 180 | bytes 1440 | tf_op jit(solution)/shard_map/concatenate | solution.py:215
  0.7 1.4 %pack.1 = (f32[783,128]{1,0:T(8,128)S(1)}, f32[783,128]{1,0:T(8,128)S(1)}, f32[783,128]{1,0:T(8,128)S(1)}) custom-call(f32[2304,128]{1,0:T(8,128)} %bitcast.4, s32[10,2,9]{2,1,0:T(2,128)S(1)} %pad_add_fusion.codes, s32[1]{0:T(128)} %bitcast.3.inner), custom_call_target="tpu_custom_call" | custom-call | tf_op jit(solution)/shard_map/pack/pallas_call | solution.py:216
  2.1 0.5 collective-permute-start.3
  2.6 0.1 collective-permute-start.4
  2.7 0.4 collective-permute-start.5
  3.2 2.6 %collective-permute-start = (f32[783,128]{1,0:T(8,128)S(1)}, f32[783,128]{1,0:T(8,128)S(1)}, u32[]{:S(2)}, u32[]{:S(2)}) collective-permute-start(f32[783,128]{1,0:T(8,128)S(1)} %get-tuple-element.20.refs_2_.refs_3_), channel_id=1, source_target_pairs={{0,2},{1,3},{2,0},{3,1},{4,6},{5,7},{6,4},{7,5},{8,10},{9,11},{10,... | collective-permute-start | bytes 1202696 | tf_op jit(solution)/shard_map/ppermute | solution.py:33
  5.7 4.6 %collective-permute-start.8 = (f32[783,128]{1,0:T(8,128)S(1)}, f32[783,128]{1,0:T(8,128)S(1)}, u32[]{:S(2)}, u32[]{:S(2)}) collective-permute-start(f32[783,128]{1,0:T(8,128)S(1)} %get-tuple-element.21.refs_0_), channel_id=1, source_target_pairs={{0,28},{4,0},{8,4},{12,8},{16,12},{20,16},{24,20},{28,24},{1,29},{... | collective-permute-start | bytes 1202696 | tf_op jit(solution)/shard_map/ppermute | solution.py:16
  10.3 0.0 collective-permute-done.3.refs_1_
  10.3 0.0 collective-permute-start.7
  10.3 0.0 collective-permute-done.4.refs_3_.refs_4_
  10.3 0.0 collective-permute-done.5.refs_5_.refs_1_
  10.3 2.9 %sums.6.refs_6_ = f32[2,9,128,128]{3,2,1,0:T(8,128)S(1)} custom-call(f32[783,128]{1,0:T(8,128)S(1)} %get-tuple-element.21.refs_0_, f32[783,128]{1,0:T(8,128)S(1)} %collective-permute-done.3.refs_1_, f32[783,128]{1,0:T(8,128)S(1)} %get-tuple-element.20.refs_2_.refs_3_, f32[783,128]{1,0:T(8,128)S(1)} %collective-permute-done.4.refs_3_.refs_4_, ...), custom_call_target="tpu_custom_call" | custom-call | flops 1 | bytes 1 | tf_op jit(solution)/shard_map/sums/pallas_call | solution.py:237
  13.2 0.2 collective-permute-start.6
  13.4 2.5 %collective-permute-done = f32[783,128]{1,0:T(8,128)S(1)} collective-permute-done((f32[783,128]{1,0:T(8,128)S(1)}, f32[783,128]{1,0:T(8,128)S(1)}, u32[]{:S(2)}, u32[]{:S(2)}) %collective-permute-start) | collective-permute-done | bytes 400928 | tf_op jit(solution)/shard_map/ppermute | solution.py:33
  15.9 0.1 collective-permute-start.1
  16.0 1.7 %collective-permute-done.1.refs_1_.refs_3_ = f32[776,128]{1,0:T(8,128)S(1)} collective-permute-done((f32[776,128]{1,0:T(8,128)S(1)}, f32[776,128]{1,0:T(8,128)S(1)}, u32[]{:S(2)}, u32[]{:S(2)}) %collective-permute-start.1) | collective-permute-done | bytes 397344 | tf_op jit(solution)/shard_map/ppermute | solution.py:33
  17.7 1.9 %collective-permute-start.2 = (f32[783,128]{1,0:T(8,128)S(1)}, f32[783,128]{1,0:T(8,128)S(1)}, u32[]{:S(2)}, u32[]{:S(2)}) collective-permute-start(f32[783,128]{1,0:T(8,128)S(1)} %get-tuple-element.21.refs_0_), channel_id=1, source_target_pairs={{0,2},{1,3},{2,0},{3,1},{4,6},{5,7},{6,4},{7,5},{8,10},{9,11},{10,... | collective-permute-start | bytes 1202696 | tf_op jit(solution)/shard_map/ppermute | solution.py:33
  19.6 6.0 %collective-permute-done.8.above = f32[783,128]{1,0:T(8,128)S(1)} collective-permute-done((f32[783,128]{1,0:T(8,128)S(1)}, f32[783,128]{1,0:T(8,128)S(1)}, u32[]{:S(2)}, u32[]{:S(2)}) %collective-permute-start.8) | collective-permute-done | bytes 400928 | tf_op jit(solution)/shard_map/ppermute | solution.py:16
  25.7 0.0 collective-permute-done.7.below
  25.7 0.0 collective-permute-done.6
  25.7 0.1 collective-permute-start.9
  25.8 1.6 %sums.7.refs_2_ = f32[790,128]{1,0:T(8,128)S(1)} custom-call(f32[783,128]{1,0:T(8,128)S(1)} %get-tuple-element.23.refs_4_.refs_0_, f32[783,128]{1,0:T(8,128)S(1)} %collective-permute-done.5.refs_5_.refs_1_, f32[776,128]{1,0:T(8,128)S(1)} %slice.13.refs_2_.refs_4_, f32[783,128]{1,0:T(8,128)S(1)} %get-tuple-element.20.refs_2_.refs_3_, ...), custom_call_target="tpu_custom_call" | custom-call | flops 1 | bytes 1 | tf_op jit(solution)/shard_map/sums/pallas_call | solution.py:237
  27.4 0.1 collective-permute-done.9.refs_0_.refs_5_
  27.5 1.0 %sums.8 = f32[790,128]{1,0:T(8,128)S(1)} custom-call(f32[776,128]{1,0:T(8,128)S(1)} %collective-permute-done.9.refs_0_.refs_5_, f32[776,128]{1,0:T(8,128)S(1)} %collective-permute-done.1.refs_1_.refs_3_, f32[790,128]{1,0:T(8,128)S(1)} %sums.7.refs_2_), custom_call_target="tpu_custom_call" | custom-call | flops 1 | bytes 1 | tf_op jit(solution)/shard_map/sums/pallas_call | solution.py:237
  28.5 3.3 %collective-permute-start.12 = (f32[790,128]{1,0:T(8,128)S(1)}, f32[790,128]{1,0:T(8,128)S(1)}, u32[]{:S(2)}, u32[]{:S(2)}) collective-permute-start(f32[790,128]{1,0:T(8,128)S(1)} %sums.8), channel_id=1, source_target_pairs={{0,5},{1,4},{2,7},{3,6},{4,9},{5,8},{6,11},{7,10},{8,13},{9,12},{1... | collective-permute-start | bytes 1213448 | tf_op jit(solution)/shard_map/ppermute | solution.py:28
  31.7 2.0 %partials.1 = (f32[778,128]{1,0:T(8,128)S(1)}, f32[778,128]{1,0:T(8,128)S(1)}, f32[778,128]{1,0:T(8,128)S(1)}, f32[778,128]{1,0:T(8,128)S(1)}) custom-call(f32[783,128]{1,0:T(8,128)S(1)} %collective-permute-done.7.below, f32[783,128]{1,0:T(8,128)S(1)} %collective-permute-done.8.above), custom_call_target="tpu_custom_call" | custom-call | flops 1 | bytes 1 | tf_op jit(solution)/shard_map/partials/pallas_call | solution.py:271
  33.7 0.1 collective-permute-start.14
  33.8 0.5 collective-permute-start.15
  34.3 0.0 collective-permute-done.2
  34.3 0.1 collective-permute-start.10
  34.5 1.9 %sums.10.refs_2_ = f32[777,128]{1,0:T(8,128)S(1)} custom-call(f32[783,128]{1,0:T(8,128)S(1)} %get-tuple-element.21.refs_0_, f32[783,128]{1,0:T(8,128)S(1)} %collective-permute-done.3.refs_1_, f32[776,128]{1,0:T(8,128)S(1)} %slice.14.refs_0_.refs_2_, f32[783,128]{1,0:T(8,128)S(1)} %get-tuple-element.20.refs_2_.refs_3_, ...), custom_call_target="tpu_custom_call" | custom-call | flops 1 | bytes 1 | tf_op jit(solution)/shard_map/sums/pallas_call | solution.py:237
  36.3 0.0 collective-permute-done.14
  36.3 0.1 add.6.refs_1_
  36.4 0.0 collective-permute-done.15
  36.4 0.1 add.7
  36.5 0.9 %collective-permute-start.16 = (f32[778,128]{1,0:T(8,128)S(1)}, f32[778,128]{1,0:T(8,128)S(1)}, u32[]{:S(2)}, u32[]{:S(2)}) collective-permute-start(f32[778,128]{1,0:T(8,128)S(1)} %add.7), channel_id=1, source_target_pairs={{0,2},{1,3},{2,0},{3,1},{4,6},{5,7},{6,4},{7,5},{8,10},{9,11},{10,... | collective-permute-start | bytes 1195016 | tf_op jit(solution)/shard_map/ppermute | solution.py:33
  37.3 0.0 collective-permute-done.10.refs_1_.refs_0_
  37.3 0.7 %sums.11 = f32[777,128]{1,0:T(8,128)S(1)} custom-call(f32[776,128]{1,0:T(8,128)S(1)} %collective-permute-done.10.refs_1_.refs_0_, f32[776,128]{1,0:T(8,128)S(1)} %collective-permute-done.1.refs_1_.refs_3_, f32[777,128]{1,0:T(8,128)S(1)} %sums.10.refs_2_), custom_call_target="tpu_custom_call" | custom-call | flops 1 | bytes 1 | tf_op jit(solution)/shard_map/sums/pallas_call | solution.py:237
  38.0 4.5 %collective-permute-start.11 = (f32[777,128]{1,0:T(8,128)S(1)}, f32[777,128]{1,0:T(8,128)S(1)}, u32[]{:S(2)}, u32[]{:S(2)}) collective-permute-start(f32[777,128]{1,0:T(8,128)S(1)} %sums.11), channel_id=1, source_target_pairs={{0,28},{4,0},{8,4},{12,8},{16,12},{20,16},{24,20},{28,24},{1,29},{... | collective-permute-start | bytes 1193480 | tf_op jit(solution)/shard_map/ppermute | solution.py:16
  42.6 0.0 collective-permute-done.12
  42.7 1.0 %collective-permute-start.13 = (f32[768,128]{1,0:T(8,128)S(1)}, f32[768,128]{1,0:T(8,128)S(1)}, u32[]{:S(2)}, u32[]{:S(2)}) collective-permute-start(f32[768,128]{1,0:T(8,128)S(1)} %slice.17), channel_id=1, source_target_pairs={{0,1},{1,0},{2,3},{3,2},{4,5},{5,4},{6,7},{7,6},{8,9},{9,8},{10,11... | collective-permute-start | bytes 1179656 | tf_op jit(solution)/shard_map/ppermute | solution.py:33
  43.7 1.7 %sums.9.base = f32[2,9,128,128]{3,2,1,0:T(8,128)S(1)} custom-call(f32[776,128]{1,0:T(8,128)S(1)} %slice.14.refs_0_.refs_2_, f32[776,128]{1,0:T(8,128)S(1)} %collective-permute-done.10.refs_1_.refs_0_, f32[776,128]{1,0:T(8,128)S(1)} %slice.16.refs_5_.refs_2_, f32[776,128]{1,0:T(8,128)S(1)} %collective-permute-done.1.refs_1_.refs_3_, ...), custom_call_target="tpu_custom_call" | custom-call | flops 1 | bytes 1 | tf_op jit(solution)/shard_map/sums/pallas_call | solution.py:237
  45.4 3.0 %collective-permute-done.16.refs_2_ = f32[778,128]{1,0:T(8,128)S(1)} collective-permute-done((f32[778,128]{1,0:T(8,128)S(1)}, f32[778,128]{1,0:T(8,128)S(1)}, u32[]{:S(2)}, u32[]{:S(2)}) %collective-permute-start.16) | collective-permute-done | bytes 398368 | tf_op jit(solution)/shard_map/ppermute | solution.py:33
  48.4 0.0 collective-permute-done.13.refs_0_
  48.4 1.0 %finish.2.refs_1_ = f32[2,9,128,128]{3,2,1,0:T(8,128)} custom-call(f32[2,9,128,128]{3,2,1,0:T(8,128)S(1)} %sums.9.base, f32[768,128]{1,0:T(8,128)S(1)} %collective-permute-done.13.refs_0_, f32[778,128]{1,0:T(8,128)S(1)} %add.6.refs_1_, f32[778,128]{1,0:T(8,128)S(1)} %collective-permute-done.16.refs_2_), custom_call_target="tpu_custom_call" | custom-call | flops 1 | bytes 1 | tf_op jit(solution)/shard_map/finish/pallas_call | solution.py:328
  49.4 2.7 %collective-permute-done.11.refs_0_ = f32[777,128]{1,0:T(8,128)S(1)} collective-permute-done((f32[777,128]{1,0:T(8,128)S(1)}, f32[777,128]{1,0:T(8,128)S(1)}, u32[]{:S(2)}, u32[]{:S(2)}) %collective-permute-start.11) | collective-permute-done | bytes 397856 | tf_op jit(solution)/shard_map/ppermute | solution.py:16
  52.1 0.8 %finish.3 = f32[2,9,128,128]{3,2,1,0:T(8,128)} custom-call(f32[2,9,128,128]{3,2,1,0:T(8,128)S(1)} %sums.9.base, f32[777,128]{1,0:T(8,128)S(1)} %collective-permute-done.11.refs_0_, f32[2,9,128,128]{3,2,1,0:T(8,128)} %finish.2.refs_1_), custom_call_target="tpu_custom_call", output_to_operand_aliasing={{}: (2, {})} | custom-call | flops 1 | bytes 1 | tf_op jit(solution)/shard_map/finish/pallas_call | solution.py:328
  (4 shorter events, 0.1 us)
Async XLA Ops:
  2.1 8.2 %collective-permute-start.3 = (f32[783,128]{1,0:T(8,128)S(1)}, f32[783,128]{1,0:T(8,128)S(1)}, u32[]{:S(2)}, u32[]{:S(2)}) collective-permute-start(f32[783,128]{1,0:T(8,128)S(1)} %get-tuple-element.21.refs_0_), channel_id=1, source_target_pairs={{0,1},{1,0},{2,3},{3,2},{4,5},{5,4},{6,7},{7,6},{8,9},{9,8},{10,11... | collective-permute-start | bytes 1202696 | tf_op jit(solution)/shard_map/ppermute | solution.py:33
  2.6 7.6 %collective-permute-start.4 = (f32[783,128]{1,0:T(8,128)S(1)}, f32[783,128]{1,0:T(8,128)S(1)}, u32[]{:S(2)}, u32[]{:S(2)}) collective-permute-start(f32[783,128]{1,0:T(8,128)S(1)} %get-tuple-element.20.refs_2_.refs_3_), channel_id=1, source_target_pairs={{0,1},{1,0},{2,3},{3,2},{4,5},{5,4},{6,7},{7,6},{8,9},{9,8},{10,11... | collective-permute-start | bytes 1202696 | tf_op jit(solution)/shard_map/ppermute | solution.py:33
  2.7 7.6 %collective-permute-start.5 = (f32[783,128]{1,0:T(8,128)S(1)}, f32[783,128]{1,0:T(8,128)S(1)}, u32[]{:S(2)}, u32[]{:S(2)}) collective-permute-start(f32[783,128]{1,0:T(8,128)S(1)} %get-tuple-element.23.refs_4_.refs_0_), channel_id=1, source_target_pairs={{0,1},{1,0},{2,3},{3,2},{4,5},{5,4},{6,7},{7,6},{8,9},{9,8},{10,11... | collective-permute-start | bytes 1202696 | tf_op jit(solution)/shard_map/ppermute | solution.py:33
  3.2 12.7 %collective-permute-start = (f32[783,128]{1,0:T(8,128)S(1)}, f32[783,128]{1,0:T(8,128)S(1)}, u32[]{:S(2)}, u32[]{:S(2)}) collective-permute-start(f32[783,128]{1,0:T(8,128)S(1)} %get-tuple-element.20.refs_2_.refs_3_), channel_id=1, source_target_pairs={{0,2},{1,3},{2,0},{3,1},{4,6},{5,7},{6,4},{7,5},{8,10},{9,11},{10,... | collective-permute-start | bytes 1202696 | tf_op jit(solution)/shard_map/ppermute | solution.py:33
  5.7 20.0 %collective-permute-start.8 = (f32[783,128]{1,0:T(8,128)S(1)}, f32[783,128]{1,0:T(8,128)S(1)}, u32[]{:S(2)}, u32[]{:S(2)}) collective-permute-start(f32[783,128]{1,0:T(8,128)S(1)} %get-tuple-element.21.refs_0_), channel_id=1, source_target_pairs={{0,28},{4,0},{8,4},{12,8},{16,12},{20,16},{24,20},{28,24},{1,29},{... | collective-permute-start | bytes 1202696 | tf_op jit(solution)/shard_map/ppermute | solution.py:16
  10.3 15.4 %collective-permute-start.7 = (f32[783,128]{1,0:T(8,128)S(1)}, f32[783,128]{1,0:T(8,128)S(1)}, u32[]{:S(2)}, u32[]{:S(2)}) collective-permute-start(f32[783,128]{1,0:T(8,128)S(1)} %get-tuple-element.23.refs_4_.refs_0_), channel_id=1, source_target_pairs={{0,4},{4,8},{8,12},{12,16},{16,20},{20,24},{24,28},{28,0},{1,5},{5... | collective-permute-start | bytes 1202696 | tf_op jit(solution)/shard_map/ppermute | solution.py:16
  13.2 12.5 %collective-permute-start.6 = (f32[783,128]{1,0:T(8,128)S(1)}, f32[783,128]{1,0:T(8,128)S(1)}, u32[]{:S(2)}, u32[]{:S(2)}) collective-permute-start(f32[783,128]{1,0:T(8,128)S(1)} %get-tuple-element.23.refs_4_.refs_0_), channel_id=1, source_target_pairs={{0,2},{1,3},{2,0},{3,1},{4,6},{5,7},{6,4},{7,5},{8,10},{9,11},{10,... | collective-permute-start | bytes 1202696 | tf_op jit(solution)/shard_map/ppermute | solution.py:33
  15.9 1.8 %collective-permute-start.1 = (f32[776,128]{1,0:T(8,128)S(1)}, f32[776,128]{1,0:T(8,128)S(1)}, u32[]{:S(2)}, u32[]{:S(2)}) collective-permute-start(f32[776,128]{1,0:T(8,128)S(1)} %slice.16.refs_5_.refs_2_), channel_id=1, source_target_pairs={{0,1},{1,0},{2,3},{3,2},{4,5},{5,4},{6,7},{7,6},{8,9},{9,8},{10,11... | collective-permute-start | bytes 1191944 | tf_op jit(solution)/shard_map/ppermute | solution.py:33
  17.7 16.6 %collective-permute-start.2 = (f32[783,128]{1,0:T(8,128)S(1)}, f32[783,128]{1,0:T(8,128)S(1)}, u32[]{:S(2)}, u32[]{:S(2)}) collective-permute-start(f32[783,128]{1,0:T(8,128)S(1)} %get-tuple-element.21.refs_0_), channel_id=1, source_target_pairs={{0,2},{1,3},{2,0},{3,1},{4,6},{5,7},{6,4},{7,5},{8,10},{9,11},{10,... | collective-permute-start | bytes 1202696 | tf_op jit(solution)/shard_map/ppermute | solution.py:33
  25.7 1.8 %collective-permute-start.9 = (f32[776,128]{1,0:T(8,128)S(1)}, f32[776,128]{1,0:T(8,128)S(1)}, u32[]{:S(2)}, u32[]{:S(2)}) collective-permute-start(f32[776,128]{1,0:T(8,128)S(1)} %slice.13.refs_2_.refs_4_), channel_id=1, source_target_pairs={{0,1},{1,0},{2,3},{3,2},{4,5},{5,4},{6,7},{7,6},{8,9},{9,8},{10,11... | collective-permute-start | bytes 1191944 | tf_op jit(solution)/shard_map/ppermute | solution.py:33
  28.5 14.2 %collective-permute-start.12 = (f32[790,128]{1,0:T(8,128)S(1)}, f32[790,128]{1,0:T(8,128)S(1)}, u32[]{:S(2)}, u32[]{:S(2)}) collective-permute-start(f32[790,128]{1,0:T(8,128)S(1)} %sums.8), channel_id=1, source_target_pairs={{0,5},{1,4},{2,7},{3,6},{4,9},{5,8},{6,11},{7,10},{8,13},{9,12},{1... | collective-permute-start | bytes 1213448 | tf_op jit(solution)/shard_map/ppermute | solution.py:28
  33.7 2.6 %collective-permute-start.14 = (f32[778,128]{1,0:T(8,128)S(1)}, f32[778,128]{1,0:T(8,128)S(1)}, u32[]{:S(2)}, u32[]{:S(2)}) collective-permute-start(f32[778,128]{1,0:T(8,128)S(1)} %get-tuple-element.29), channel_id=1, source_target_pairs={{0,1},{1,0},{2,3},{3,2},{4,5},{5,4},{6,7},{7,6},{8,9},{9,8},{10,11... | collective-permute-start | bytes 1195016 | tf_op jit(solution)/shard_map/ppermute | solution.py:33
  33.8 2.6 %collective-permute-start.15 = (f32[778,128]{1,0:T(8,128)S(1)}, f32[778,128]{1,0:T(8,128)S(1)}, u32[]{:S(2)}, u32[]{:S(2)}) collective-permute-start(f32[778,128]{1,0:T(8,128)S(1)} %get-tuple-element.31), channel_id=1, source_target_pairs={{0,1},{1,0},{2,3},{3,2},{4,5},{5,4},{6,7},{7,6},{8,9},{9,8},{10,11... | collective-permute-start | bytes 1195016 | tf_op jit(solution)/shard_map/ppermute | solution.py:33
  34.3 3.0 %collective-permute-start.10 = (f32[776,128]{1,0:T(8,128)S(1)}, f32[776,128]{1,0:T(8,128)S(1)}, u32[]{:S(2)}, u32[]{:S(2)}) collective-permute-start(f32[776,128]{1,0:T(8,128)S(1)} %slice.14.refs_0_.refs_2_), channel_id=1, source_target_pairs={{0,1},{1,0},{2,3},{3,2},{4,5},{5,4},{6,7},{7,6},{8,9},{9,8},{10,11... | collective-permute-start | bytes 1191944 | tf_op jit(solution)/shard_map/ppermute | solution.py:33
  36.5 11.9 %collective-permute-start.16 = (f32[778,128]{1,0:T(8,128)S(1)}, f32[778,128]{1,0:T(8,128)S(1)}, u32[]{:S(2)}, u32[]{:S(2)}) collective-permute-start(f32[778,128]{1,0:T(8,128)S(1)} %add.7), channel_id=1, source_target_pairs={{0,2},{1,3},{2,0},{3,1},{4,6},{5,7},{6,4},{7,5},{8,10},{9,11},{10,... | collective-permute-start | bytes 1195016 | tf_op jit(solution)/shard_map/ppermute | solution.py:33
  38.0 14.1 %collective-permute-start.11 = (f32[777,128]{1,0:T(8,128)S(1)}, f32[777,128]{1,0:T(8,128)S(1)}, u32[]{:S(2)}, u32[]{:S(2)}) collective-permute-start(f32[777,128]{1,0:T(8,128)S(1)} %sums.11), channel_id=1, source_target_pairs={{0,28},{4,0},{8,4},{12,8},{16,12},{20,16},{24,20},{28,24},{1,29},{... | collective-permute-start | bytes 1193480 | tf_op jit(solution)/shard_map/ppermute | solution.py:16
  42.7 5.7 %collective-permute-start.13 = (f32[768,128]{1,0:T(8,128)S(1)}, f32[768,128]{1,0:T(8,128)S(1)}, u32[]{:S(2)}, u32[]{:S(2)}) collective-permute-start(f32[768,128]{1,0:T(8,128)S(1)} %slice.17), channel_id=1, source_target_pairs={{0,1},{1,0},{2,3},{3,2},{4,5},{5,4},{6,7},{7,6},{8,9},{9,8},{10,11... | collective-permute-start | bytes 1179656 | tf_op jit(solution)/shard_map/ppermute | solution.py:33

commit v9 on v8

--- a/solution.py
+++ b/solution.py
@@ -314,7 +314,7 @@
         near = len(lowers)
         groups = [far_lowers, far_middles, far_uppers]
         base = sums(groups, 1, own_plan, 0, slots, near, [base])
-        to_below_next = swapped(to_below_next[:lines], 1)
+        to_below_next = swapped(tied([to_below_next], base)[0][:lines], 1)
     middle_shares = [shares[0], *far_share]
     def finish(first, groups, result=()):
         counts = [len(group) for group in groups]

time: 53.3 us -> 53.4 us (level)
  starting transfers between devices: 20.8 us -> 20 us
  waiting for transfers between devices: 16.2 us -> 16.8 us
    ppermute x1, starting transfers between devices: 3.26 us -> 2.3 us  [shifted_aslant(): return lax.ppermute(value, ('blk', 'inner'), pairs)]
    ppermute x3, waiting for transfers between devices: 8.8 us -> 9.39 us  [shifted(): return lax.ppermute(value, 'blk', pairs)]
  transfers between devices with their start and end apart: 17 -> 17, of which waited for: 6 -> 5; matrix products, arithmetic and copies ran while one was open for 0% -> 0% of each run, Pallas kernels for 24% -> 25%
where the time goes in v9:
time: 53.4 us; the launch traced here: 53.2 us
  starting transfers between devices  20 us (37%)
  waiting for transfers between devices  16.8 us (31%)
  Pallas kernels  15.3 us (29%)
  other arithmetic  0.82 us (2%)
    pallas_call x6, Pallas kernels, sums(): pl.pallas_call(functools.partial(sums_kernel, dims, plan), out_shape=jax....  10.2 us
    ppermute x3, waiting for transfers between devices, shifted(): return lax.ppermute(value, 'blk', pairs)  9.39 us
    ppermute x3, starting transfers between devices, shifted(): return lax.ppermute(value, 'blk', pairs)  9.14 us
    ppermute x13, starting transfers between devices, swapped(): lax.ppermute(value, 'inner', [(i, i ^ distance) for i in range(count)])  8.58 us
    ppermute x13, waiting for transfers between devices, swapped(): lax.ppermute(value, 'inner', [(i, i ^ distance) for i in range(count)])  7.4 us
    ppermute x1, starting transfers between devices, shifted_aslant(): return lax.ppermute(value, ('blk', 'inner'), pairs)  2.3 us
    pallas_call x1, Pallas kernels, partials(): pl.pallas_call(functools.partial(partial_kernel, (parts, local_rows, slot...  1.95 us
    pallas_call x2, Pallas kernels, finish(): pl.pallas_call(kernel, out_shape=jax.ShapeDtypeStruct(density.shape, jnp....  1.74 us
  transfers between devices with their start and end apart: 17, of which 5 were waited for; matrix products, arithmetic and copies ran while one was open for 0% of the time, Pallas kernels for 25%

profile of v9, /device:TPU:0, one launch (start us, length us, event | category | flops | bytes accessed | tf_op | source)
XLA Modules:
  0.0 53.2 jit_solution(15554341602030950406)
XLA Ops:
  0.0 0.7 %pad_add_fusion.codes = s32[10,2,9]{2,1,0:T(2,128)S(1)} fusion(s32[1,2,9]{2,1,0:T(2,128)} %bitcast.6, s32[9,2,9]{2,1,0:T(2,128)} %bitcast.5), kind=kLoop, calls=%fused_computation | loop fusion | flops 180 | bytes 1440 | tf_op jit(solution)/shard_map/concatenate | solution.py:215
  0.7 1.4 %pack.1 = (f32[783,128]{1,0:T(8,128)S(1)}, f32[783,128]{1,0:T(8,128)S(1)}, f32[783,128]{1,0:T(8,128)S(1)}) custom-call(f32[2304,128]{1,0:T(8,128)} %bitcast.4, s32[10,2,9]{2,1,0:T(2,128)S(1)} %pad_add_fusion.codes, s32[1]{0:T(128)} %bitcast.3.inner), custom_call_target="tpu_custom_call" | custom-call | tf_op jit(solution)/shard_map/pack/pallas_call | solution.py:216
  2.1 0.5 collective-permute-start.3
  2.6 0.1 collective-permute-start.4
  2.7 0.4 collective-permute-start.5
  3.2 2.6 %collective-permute-start = (f32[783,128]{1,0:T(8,128)S(1)}, f32[783,128]{1,0:T(8,128)S(1)}, u32[]{:S(2)}, u32[]{:S(2)}) collective-permute-start(f32[783,128]{1,0:T(8,128)S(1)} %get-tuple-element.21.refs_2_.refs_3_), channel_id=1, source_target_pairs={{0,2},{1,3},{2,0},{3,1},{4,6},{5,7},{6,4},{7,5},{8,10},{9,11},{10,... | collective-permute-start | bytes 1202696 | tf_op jit(solution)/shard_map/ppermute | solution.py:33
  5.7 4.6 %collective-permute-start.8 = (f32[783,128]{1,0:T(8,128)S(1)}, f32[783,128]{1,0:T(8,128)S(1)}, u32[]{:S(2)}, u32[]{:S(2)}) collective-permute-start(f32[783,128]{1,0:T(8,128)S(1)} %get-tuple-element.22.refs_0_), channel_id=1, source_target_pairs={{0,28},{4,0},{8,4},{12,8},{16,12},{20,16},{24,20},{28,24},{1,29},{... | collective-permute-start | bytes 1202696 | tf_op jit(solution)/shard_map/ppermute | solution.py:16
  10.3 0.0 collective-permute-done.3.refs_1_
  10.3 0.0 collective-permute-start.7
  10.3 0.0 collective-permute-done.4.refs_3_.refs_4_
  10.3 0.0 collective-permute-done.5.refs_5_.refs_1_
  10.3 1.7 %sums.6.refs_6_ = f32[2,9,128,128]{3,2,1,0:T(8,128)S(1)} custom-call(f32[783,128]{1,0:T(8,128)S(1)} %get-tuple-element.22.refs_0_, f32[783,128]{1,0:T(8,128)S(1)} %collective-permute-done.3.refs_1_, f32[783,128]{1,0:T(8,128)S(1)} %get-tuple-element.21.refs_2_.refs_3_, f32[783,128]{1,0:T(8,128)S(1)} %collective-permute-done.4.refs_3_.refs_4_, ...), custom_call_target="tpu_custom_call" | custom-call | flops 1 | bytes 1 | tf_op jit(solution)/shard_map/sums/pallas_call | solution.py:237
  12.0 1.4 %collective-permute-start.6 = (f32[783,128]{1,0:T(8,128)S(1)}, f32[783,128]{1,0:T(8,128)S(1)}, u32[]{:S(2)}, u32[]{:S(2)}) collective-permute-start(f32[783,128]{1,0:T(8,128)S(1)} %get-tuple-element.24.refs_4_.refs_0_), channel_id=1, source_target_pairs={{0,2},{1,3},{2,0},{3,1},{4,6},{5,7},{6,4},{7,5},{8,10},{9,11},{10,... | collective-permute-start | bytes 1202696 | tf_op jit(solution)/shard_map/ppermute | solution.py:33
  13.4 2.4 %collective-permute-done = f32[783,128]{1,0:T(8,128)S(1)} collective-permute-done((f32[783,128]{1,0:T(8,128)S(1)}, f32[783,128]{1,0:T(8,128)S(1)}, u32[]{:S(2)}, u32[]{:S(2)}) %collective-permute-start) | collective-permute-done | bytes 400928 | tf_op jit(solution)/shard_map/ppermute | solution.py:33
  15.8 0.1 collective-permute-start.1
  15.9 1.7 %collective-permute-done.1.refs_1_.refs_3_ = f32[776,128]{1,0:T(8,128)S(1)} collective-permute-done((f32[776,128]{1,0:T(8,128)S(1)}, f32[776,128]{1,0:T(8,128)S(1)}, u32[]{:S(2)}, u32[]{:S(2)}) %collective-permute-start.1) | collective-permute-done | bytes 397344 | tf_op jit(solution)/shard_map/ppermute | solution.py:33
  17.6 2.0 %collective-permute-start.2 = (f32[783,128]{1,0:T(8,128)S(1)}, f32[783,128]{1,0:T(8,128)S(1)}, u32[]{:S(2)}, u32[]{:S(2)}) collective-permute-start(f32[783,128]{1,0:T(8,128)S(1)} %get-tuple-element.22.refs_0_), channel_id=1, source_target_pairs={{0,2},{1,3},{2,0},{3,1},{4,6},{5,7},{6,4},{7,5},{8,10},{9,11},{10,... | collective-permute-start | bytes 1202696 | tf_op jit(solution)/shard_map/ppermute | solution.py:33
  19.6 6.0 %collective-permute-done.8.above = f32[783,128]{1,0:T(8,128)S(1)} collective-permute-done((f32[783,128]{1,0:T(8,128)S(1)}, f32[783,128]{1,0:T(8,128)S(1)}, u32[]{:S(2)}, u32[]{:S(2)}) %collective-permute-start.8) | collective-permute-done | bytes 400928 | tf_op jit(solution)/shard_map/ppermute | solution.py:16
  25.7 0.0 collective-permute-done.7.below
  25.7 0.0 collective-permute-done.6
  25.7 0.1 collective-permute-start.9
  25.8 2.4 %sums.7.refs_2_ = f32[790,128]{1,0:T(8,128)S(1)} custom-call(f32[783,128]{1,0:T(8,128)S(1)} %get-tuple-element.24.refs_4_.refs_0_, f32[783,128]{1,0:T(8,128)S(1)} %collective-permute-done.5.refs_5_.refs_1_, f32[776,128]{1,0:T(8,128)S(1)} %slice.13.refs_2_.refs_4_, f32[783,128]{1,0:T(8,128)S(1)} %get-tuple-element.21.refs_2_.refs_3_, ...), custom_call_target="tpu_custom_call" | custom-call | flops 1 | bytes 1 | tf_op jit(solution)/shard_map/sums/pallas_call | solution.py:237
  28.2 0.0 collective-permute-done.9.refs_0_.refs_5_
  28.2 1.2 %sums.8 = f32[790,128]{1,0:T(8,128)S(1)} custom-call(f32[776,128]{1,0:T(8,128)S(1)} %collective-permute-done.9.refs_0_.refs_5_, f32[776,128]{1,0:T(8,128)S(1)} %collective-permute-done.1.refs_1_.refs_3_, f32[790,128]{1,0:T(8,128)S(1)} %sums.7.refs_2_), custom_call_target="tpu_custom_call" | custom-call | flops 1 | bytes 1 | tf_op jit(solution)/shard_map/sums/pallas_call | solution.py:237
  29.4 2.3 %collective-permute-start.12 = (f32[790,128]{1,0:T(8,128)S(1)}, f32[790,128]{1,0:T(8,128)S(1)}, u32[]{:S(2)}, u32[]{:S(2)}) collective-permute-start(f32[790,128]{1,0:T(8,128)S(1)} %sums.8), channel_id=1, source_target_pairs={{0,5},{1,4},{2,7},{3,6},{4,9},{5,8},{6,11},{7,10},{8,13},{9,12},{1... | collective-permute-start | bytes 1213448 | tf_op jit(solution)/shard_map/ppermute | solution.py:28
  31.7 2.0 %partials.1 = (f32[778,128]{1,0:T(8,128)S(1)}, f32[778,128]{1,0:T(8,128)S(1)}, f32[778,128]{1,0:T(8,128)S(1)}, f32[778,128]{1,0:T(8,128)S(1)}) custom-call(f32[783,128]{1,0:T(8,128)S(1)} %collective-permute-done.7.below, f32[783,128]{1,0:T(8,128)S(1)} %collective-permute-done.8.above), custom_call_target="tpu_custom_call" | custom-call | flops 1 | bytes 1 | tf_op jit(solution)/shard_map/partials/pallas_call | solution.py:271
  33.7 0.1 collective-permute-start.14
  33.8 0.5 collective-permute-start.15
  34.3 0.0 collective-permute-done.2
  34.3 0.1 collective-permute-start.10
  34.5 1.9 %sums.10.refs_2_ = f32[777,128]{1,0:T(8,128)S(1)} custom-call(f32[783,128]{1,0:T(8,128)S(1)} %get-tuple-element.22.refs_0_, f32[783,128]{1,0:T(8,128)S(1)} %collective-permute-done.3.refs_1_, f32[776,128]{1,0:T(8,128)S(1)} %slice.14.refs_0_.refs_2_, f32[783,128]{1,0:T(8,128)S(1)} %get-tuple-element.21.refs_2_.refs_3_, ...), custom_call_target="tpu_custom_call" | custom-call | flops 1 | bytes 1 | tf_op jit(solution)/shard_map/sums/pallas_call | solution.py:237
  36.3 0.0 collective-permute-done.14
  36.4 0.0 collective-permute-done.15
  36.4 0.1 add.7
  36.4 0.6 %collective-permute-start.16 = (f32[778,128]{1,0:T(8,128)S(1)}, f32[778,128]{1,0:T(8,128)S(1)}, u32[]{:S(2)}, u32[]{:S(2)}) collective-permute-start(f32[778,128]{1,0:T(8,128)S(1)} %add.7), channel_id=1, source_target_pairs={{0,2},{1,3},{2,0},{3,1},{4,6},{5,7},{6,4},{7,5},{8,10},{9,11},{10,... | collective-permute-start | bytes 1195016 | tf_op jit(solution)/shard_map/ppermute | solution.py:33
  37.0 0.0 collective-permute-done.10.refs_1_.refs_0_
  37.0 1.0 %sums.11 = f32[777,128]{1,0:T(8,128)S(1)} custom-call(f32[776,128]{1,0:T(8,128)S(1)} %collective-permute-done.10.refs_1_.refs_0_, f32[776,128]{1,0:T(8,128)S(1)} %collective-permute-done.1.refs_1_.refs_3_, f32[777,128]{1,0:T(8,128)S(1)} %sums.10.refs_2_), custom_call_target="tpu_custom_call" | custom-call | flops 1 | bytes 1 | tf_op jit(solution)/shard_map/sums/pallas_call | solution.py:237
  38.0 4.6 %collective-permute-start.11 = (f32[777,128]{1,0:T(8,128)S(1)}, f32[777,128]{1,0:T(8,128)S(1)}, u32[]{:S(2)}, u32[]{:S(2)}) collective-permute-start(f32[777,128]{1,0:T(8,128)S(1)} %sums.11), channel_id=1, source_target_pairs={{0,28},{4,0},{8,4},{12,8},{16,12},{20,16},{24,20},{28,24},{1,29},{... | collective-permute-start | bytes 1193480 | tf_op jit(solution)/shard_map/ppermute | solution.py:16
  42.6 2.1 %sums.9.base = f32[2,9,128,128]{3,2,1,0:T(8,128)S(1)} custom-call(f32[776,128]{1,0:T(8,128)S(1)} %slice.14.refs_0_.refs_2_, f32[776,128]{1,0:T(8,128)S(1)} %collective-permute-done.10.refs_1_.refs_0_, f32[776,128]{1,0:T(8,128)S(1)} %slice.16.refs_5_.refs_2_, f32[776,128]{1,0:T(8,128)S(1)} %collective-permute-done.1.refs_1_.refs_3_, ...), custom_call_target="tpu_custom_call" | custom-call | flops 1 | bytes 1 | tf_op jit(solution)/shard_map/sums/pallas_call | solution.py:237
  44.7 0.0 collective-permute-done.12
  44.8 0.1 collective-permute-start.13
  44.8 3.3 %collective-permute-done.16.refs_2_ = f32[778,128]{1,0:T(8,128)S(1)} collective-permute-done((f32[778,128]{1,0:T(8,128)S(1)}, f32[778,128]{1,0:T(8,128)S(1)}, u32[]{:S(2)}, u32[]{:S(2)}) %collective-permute-start.16) | collective-permute-done | bytes 398368 | tf_op jit(solution)/shard_map/ppermute | solution.py:33
  48.1 0.0 collective-permute-done.13.refs_0_
  48.2 1.0 %finish.2.refs_1_ = f32[2,9,128,128]{3,2,1,0:T(8,128)} custom-call(f32[2,9,128,128]{3,2,1,0:T(8,128)S(1)} %sums.9.base, f32[768,128]{1,0:T(8,128)S(1)} %collective-permute-done.13.refs_0_, f32[778,128]{1,0:T(8,128)S(1)} %add.6.refs_1_, f32[778,128]{1,0:T(8,128)S(1)} %collective-permute-done.16.refs_2_), custom_call_target="tpu_custom_call" | custom-call | flops 1 | bytes 1 | tf_op jit(solution)/shard_map/finish/pallas_call | solution.py:328
  49.1 3.3 %collective-permute-done.11.refs_0_ = f32[777,128]{1,0:T(8,128)S(1)} collective-permute-done((f32[777,128]{1,0:T(8,128)S(1)}, f32[777,128]{1,0:T(8,128)S(1)}, u32[]{:S(2)}, u32[]{:S(2)}) %collective-permute-start.11) | collective-permute-done | bytes 397856 | tf_op jit(solution)/shard_map/ppermute | solution.py:16
  52.5 0.8 %finish.3 = f32[2,9,128,128]{3,2,1,0:T(8,128)} custom-call(f32[2,9,128,128]{3,2,1,0:T(8,128)S(1)} %sums.9.base, f32[777,128]{1,0:T(8,128)S(1)} %collective-permute-done.11.refs_0_, f32[2,9,128,128]{3,2,1,0:T(8,128)} %finish.2.refs_1_), custom_call_target="tpu_custom_call", output_to_operand_aliasing={{}: (2, {})} | custom-call | flops 1 | bytes 1 | tf_op jit(solution)/shard_map/finish/pallas_call | solution.py:328
  (5 shorter events, 0.2 us)
Async XLA Ops:
  2.1 8.2 %collective-permute-start.3 = (f32[783,128]{1,0:T(8,128)S(1)}, f32[783,128]{1,0:T(8,128)S(1)}, u32[]{:S(2)}, u32[]{:S(2)}) collective-permute-start(f32[783,128]{1,0:T(8,128)S(1)} %get-tuple-element.22.refs_0_), channel_id=1, source_target_pairs={{0,1},{1,0},{2,3},{3,2},{4,5},{5,4},{6,7},{7,6},{8,9},{9,8},{10,11... | collective-permute-start | bytes 1202696 | tf_op jit(solution)/shard_map/ppermute | solution.py:33
  2.6 7.6 %collective-permute-start.4 = (f32[783,128]{1,0:T(8,128)S(1)}, f32[783,128]{1,0:T(8,128)S(1)}, u32[]{:S(2)}, u32[]{:S(2)}) collective-permute-start(f32[783,128]{1,0:T(8,128)S(1)} %get-tuple-element.21.refs_2_.refs_3_), channel_id=1, source_target_pairs={{0,1},{1,0},{2,3},{3,2},{4,5},{5,4},{6,7},{7,6},{8,9},{9,8},{10,11... | collective-permute-start | bytes 1202696 | tf_op jit(solution)/shard_map/ppermute | solution.py:33
  2.7 7.6 %collective-permute-start.5 = (f32[783,128]{1,0:T(8,128)S(1)}, f32[783,128]{1,0:T(8,128)S(1)}, u32[]{:S(2)}, u32[]{:S(2)}) collective-permute-start(f32[783,128]{1,0:T(8,128)S(1)} %get-tuple-element.24.refs_4_.refs_0_), channel_id=1, source_target_pairs={{0,1},{1,0},{2,3},{3,2},{4,5},{5,4},{6,7},{7,6},{8,9},{9,8},{10,11... | collective-permute-start | bytes 1202696 | tf_op jit(solution)/shard_map/ppermute | solution.py:33
  3.2 12.6 %collective-permute-start = (f32[783,128]{1,0:T(8,128)S(1)}, f32[783,128]{1,0:T(8,128)S(1)}, u32[]{:S(2)}, u32[]{:S(2)}) collective-permute-start(f32[783,128]{1,0:T(8,128)S(1)} %get-tuple-element.21.refs_2_.refs_3_), channel_id=1, source_target_pairs={{0,2},{1,3},{2,0},{3,1},{4,6},{5,7},{6,4},{7,5},{8,10},{9,11},{10,... | collective-permute-start | bytes 1202696 | tf_op jit(solution)/shard_map/ppermute | solution.py:33
  5.7 20.0 %collective-permute-start.8 = (f32[783,128]{1,0:T(8,128)S(1)}, f32[783,128]{1,0:T(8,128)S(1)}, u32[]{:S(2)}, u32[]{:S(2)}) collective-permute-start(f32[783,128]{1,0:T(8,128)S(1)} %get-tuple-element.22.refs_0_), channel_id=1, source_target_pairs={{0,28},{4,0},{8,4},{12,8},{16,12},{20,16},{24,20},{28,24},{1,29},{... | collective-permute-start | bytes 1202696 | tf_op jit(solution)/shard_map/ppermute | solution.py:16
  10.3 15.4 %collective-permute-start.7 = (f32[783,128]{1,0:T(8,128)S(1)}, f32[783,128]{1,0:T(8,128)S(1)}, u32[]{:S(2)}, u32[]{:S(2)}) collective-permute-start(f32[783,128]{1,0:T(8,128)S(1)} %get-tuple-element.24.refs_4_.refs_0_), channel_id=1, source_target_pairs={{0,4},{4,8},{8,12},{12,16},{16,20},{20,24},{24,28},{28,0},{1,5},{5... | collective-permute-start | bytes 1202696 | tf_op jit(solution)/shard_map/ppermute | solution.py:16
  12.0 13.7 %collective-permute-start.6 = (f32[783,128]{1,0:T(8,128)S(1)}, f32[783,128]{1,0:T(8,128)S(1)}, u32[]{:S(2)}, u32[]{:S(2)}) collective-permute-start(f32[783,128]{1,0:T(8,128)S(1)} %get-tuple-element.24.refs_4_.refs_0_), channel_id=1, source_target_pairs={{0,2},{1,3},{2,0},{3,1},{4,6},{5,7},{6,4},{7,5},{8,10},{9,11},{10,... | collective-permute-start | bytes 1202696 | tf_op jit(solution)/shard_map/ppermute | solution.py:33
  15.8 1.8 %collective-permute-start.1 = (f32[776,128]{1,0:T(8,128)S(1)}, f32[776,128]{1,0:T(8,128)S(1)}, u32[]{:S(2)}, u32[]{:S(2)}) collective-permute-start(f32[776,128]{1,0:T(8,128)S(1)} %slice.16.refs_5_.refs_2_), channel_id=1, source_target_pairs={{0,1},{1,0},{2,3},{3,2},{4,5},{5,4},{6,7},{7,6},{8,9},{9,8},{10,11... | collective-permute-start | bytes 1191944 | tf_op jit(solution)/shard_map/ppermute | solution.py:33
  17.6 16.7 %collective-permute-start.2 = (f32[783,128]{1,0:T(8,128)S(1)}, f32[783,128]{1,0:T(8,128)S(1)}, u32[]{:S(2)}, u32[]{:S(2)}) collective-permute-start(f32[783,128]{1,0:T(8,128)S(1)} %get-tuple-element.22.refs_0_), channel_id=1, source_target_pairs={{0,2},{1,3},{2,0},{3,1},{4,6},{5,7},{6,4},{7,5},{8,10},{9,11},{10,... | collective-permute-start | bytes 1202696 | tf_op jit(solution)/shard_map/ppermute | solution.py:33
  25.7 2.5 %collective-permute-start.9 = (f32[776,128]{1,0:T(8,128)S(1)}, f32[776,128]{1,0:T(8,128)S(1)}, u32[]{:S(2)}, u32[]{:S(2)}) collective-permute-start(f32[776,128]{1,0:T(8,128)S(1)} %slice.13.refs_2_.refs_4_), channel_id=1, source_target_pairs={{0,1},{1,0},{2,3},{3,2},{4,5},{5,4},{6,7},{7,6},{8,9},{9,8},{10,11... | collective-permute-start | bytes 1191944 | tf_op jit(solution)/shard_map/ppermute | solution.py:33
  29.4 15.3 %collective-permute-start.12 = (f32[790,128]{1,0:T(8,128)S(1)}, f32[790,128]{1,0:T(8,128)S(1)}, u32[]{:S(2)}, u32[]{:S(2)}) collective-permute-start(f32[790,128]{1,0:T(8,128)S(1)} %sums.8), channel_id=1, source_target_pairs={{0,5},{1,4},{2,7},{3,6},{4,9},{5,8},{6,11},{7,10},{8,13},{9,12},{1... | collective-permute-start | bytes 1213448 | tf_op jit(solution)/shard_map/ppermute | solution.py:28
  33.7 2.6 %collective-permute-start.14 = (f32[778,128]{1,0:T(8,128)S(1)}, f32[778,128]{1,0:T(8,128)S(1)}, u32[]{:S(2)}, u32[]{:S(2)}) collective-permute-start(f32[778,128]{1,0:T(8,128)S(1)} %get-tuple-element.31), channel_id=1, source_target_pairs={{0,1},{1,0},{2,3},{3,2},{4,5},{5,4},{6,7},{7,6},{8,9},{9,8},{10,11... | collective-permute-start | bytes 1195016 | tf_op jit(solution)/shard_map/ppermute | solution.py:33
  33.8 2.6 %collective-permute-start.15 = (f32[778,128]{1,0:T(8,128)S(1)}, f32[778,128]{1,0:T(8,128)S(1)}, u32[]{:S(2)}, u32[]{:S(2)}) collective-permute-start(f32[778,128]{1,0:T(8,128)S(1)} %get-tuple-element.33), channel_id=1, source_target_pairs={{0,1},{1,0},{2,3},{3,2},{4,5},{5,4},{6,7},{7,6},{8,9},{9,8},{10,11... | collective-permute-start | bytes 1195016 | tf_op jit(solution)/shard_map/ppermute | solution.py:33
  34.3 2.7 %collective-permute-start.10 = (f32[776,128]{1,0:T(8,128)S(1)}, f32[776,128]{1,0:T(8,128)S(1)}, u32[]{:S(2)}, u32[]{:S(2)}) collective-permute-start(f32[776,128]{1,0:T(8,128)S(1)} %slice.14.refs_0_.refs_2_), channel_id=1, source_target_pairs={{0,1},{1,0},{2,3},{3,2},{4,5},{5,4},{6,7},{7,6},{8,9},{9,8},{10,11... | collective-permute-start | bytes 1191944 | tf_op jit(solution)/shard_map/ppermute | solution.py:33
  36.4 11.7 %collective-permute-start.16 = (f32[778,128]{1,0:T(8,128)S(1)}, f32[778,128]{1,0:T(8,128)S(1)}, u32[]{:S(2)}, u32[]{:S(2)}) collective-permute-start(f32[778,128]{1,0:T(8,128)S(1)} %add.7), channel_id=1, source_target_pairs={{0,2},{1,3},{2,0},{3,1},{4,6},{5,7},{6,4},{7,5},{8,10},{9,11},{10,... | collective-permute-start | bytes 1195016 | tf_op jit(solution)/shard_map/ppermute | solution.py:33
  38.0 14.5 %collective-permute-start.11 = (f32[777,128]{1,0:T(8,128)S(1)}, f32[777,128]{1,0:T(8,128)S(1)}, u32[]{:S(2)}, u32[]{:S(2)}) collective-permute-start(f32[777,128]{1,0:T(8,128)S(1)} %sums.11), channel_id=1, source_target_pairs={{0,28},{4,0},{8,4},{12,8},{16,12},{20,16},{24,20},{28,24},{1,29},{... | collective-permute-start | bytes 1193480 | tf_op jit(solution)/shard_map/ppermute | solution.py:16
  44.8 3.4 %collective-permute-start.13 = (f32[768,128]{1,0:T(8,128)S(1)}, f32[768,128]{1,0:T(8,128)S(1)}, u32[]{:S(2)}, u32[]{:S(2)}) collective-permute-start(f32[768,128]{1,0:T(8,128)S(1)} %slice.15), channel_id=1, source_target_pairs={{0,1},{1,0},{2,3},{3,2},{4,5},{5,4},{6,7},{7,6},{8,9},{9,8},{10,11... | collective-permute-start | bytes 1179656 | tf_op jit(solution)/shard_map/ppermute | solution.py:33

commit v10 on v9

--- a/solution.py
+++ b/solution.py
@@ -184,7 +184,6 @@
     groups, (out, result, sems) = refs[:-3], refs[-3:]
     local_rows, slots, side, _ = base.shape
     per = slots // 3
-    last = first + per * len(groups)
     copies = []
     for row in range(local_rows):
         for index, group in enumerate(groups):
@@ -193,9 +192,9 @@
                 total = sum(one[start : start + side, :] for one in group)
                 at = first + index * per + slot
                 result[row, at - first] = base[row, at] - total
-        dest = out.at[row, pl.ds(first, last - first)]
-        copies.append(pltpu.make_async_copy(result.at[row], dest, sems.at[row]))
-        copies[-1].start()
+                sem = sems.at[row, at - first]
+                copies.append(pltpu.make_async_copy(result.at[row, at - first], out.at[row, at], sem))
+                copies[-1].start()
     for copy in copies:
         copy.wait()
 
@@ -332,7 +331,7 @@
             out_specs=in_hbm,
             scratch_shapes=[
                 pltpu.VMEM((local_rows, per * len(groups), side, side), jnp.float32),
-                pltpu.SemaphoreType.DMA((local_rows,)),
+                pltpu.SemaphoreType.DMA((local_rows, per * len(groups))),
             ],
             input_output_aliases={1 + len(flat): 0} if result else {},
             compiler_params=pltpu.CompilerParams(vmem_limit_bytes=16 << 20),

time: 53.4 us -> 53.1 us (level)
  Pallas kernels: 15.3 us -> 14.2 us
  starting transfers between devices: 20 us -> 20.6 us
    pallas_call x6, Pallas kernels: 10.2 us -> 9.13 us  [sums(): pl.pallas_call(functools.partial(sums_kernel, dims, plan), out_shape=jax....]
    ppermute x13, starting transfers between devices: 8.58 us -> 9.62 us  [swapped(): lax.ppermute(value, 'inner', [(i, i ^ distance) for i in range(count)])]
    ppermute x1, starting transfers between devices: 2.3 us -> 1.52 us  [shifted_aslant(): return lax.ppermute(value, ('blk', 'inner'), pairs)]
    ppermute x13, waiting for transfers between devices: 7.4 us -> 8.11 us  [swapped(): lax.ppermute(value, 'inner', [(i, i ^ distance) for i in range(count)])]
    ppermute x3, waiting for transfers between devices: 9.39 us -> 8.71 us  [shifted(): return lax.ppermute(value, 'blk', pairs)]
  transfers between devices with their start and end apart: 17 -> 17, of which waited for: 5 -> 5; matrix products, arithmetic and copies ran while one was open for 0% -> 0% of each run, Pallas kernels for 25% -> 23%
where the time goes in v10:
time: 53.1 us; the launch traced here: 52.7 us
  starting transfers between devices  20.6 us (39%)
  waiting for transfers between devices  16.8 us (32%)
  Pallas kernels  14.2 us (27%)
  other arithmetic  0.82 us (2%)
    ppermute x13, starting transfers between devices, swapped(): lax.ppermute(value, 'inner', [(i, i ^ distance) for i in range(count)])  9.62 us
    ppermute x3, starting transfers between devices, shifted(): return lax.ppermute(value, 'blk', pairs)  9.44 us
    pallas_call x6, Pallas kernels, sums(): pl.pallas_call(functools.partial(sums_kernel, dims, plan), out_shape=jax....  9.13 us
    ppermute x3, waiting for transfers between devices, shifted(): return lax.ppermute(value, 'blk', pairs)  8.71 us
    ppermute x13, waiting for transfers between devices, swapped(): lax.ppermute(value, 'inner', [(i, i ^ distance) for i in range(count)])  8.11 us
    pallas_call x1, Pallas kernels, partials(): pl.pallas_call(functools.partial(partial_kernel, (parts, local_rows, slot...  1.94 us
    pallas_call x2, Pallas kernels, finish(): pl.pallas_call(kernel, out_shape=jax.ShapeDtypeStruct(density.shape, jnp....  1.77 us
    ppermute x1, starting transfers between devices, shifted_aslant(): return lax.ppermute(value, ('blk', 'inner'), pairs)  1.52 us
  transfers between devices with their start and end apart: 17, of which 5 were waited for; matrix products, arithmetic and copies ran while one was open for 0% of the time, Pallas kernels for 23%

profile of v10, /device:TPU:0, one launch (start us, length us, event | category | flops | bytes accessed | tf_op | source)
XLA Modules:
  0.0 52.7 jit_solution(5826086630591194832)
XLA Ops:
  0.0 0.7 %pad_add_fusion.codes = s32[10,2,9]{2,1,0:T(2,128)S(1)} fusion(s32[1,2,9]{2,1,0:T(2,128)} %bitcast.6, s32[9,2,9]{2,1,0:T(2,128)} %bitcast.5), kind=kLoop, calls=%fused_computation | loop fusion | flops 180 | bytes 1440 | tf_op jit(solution)/shard_map/concatenate | solution.py:214
  0.7 1.4 %pack.1 = (f32[783,128]{1,0:T(8,128)S(1)}, f32[783,128]{1,0:T(8,128)S(1)}, f32[783,128]{1,0:T(8,128)S(1)}) custom-call(f32[2304,128]{1,0:T(8,128)} %bitcast.4, s32[10,2,9]{2,1,0:T(2,128)S(1)} %pad_add_fusion.codes, s32[1]{0:T(128)} %bitcast.3.inner), custom_call_target="tpu_custom_call" | custom-call | tf_op jit(solution)/shard_map/pack/pallas_call | solution.py:215
  2.1 0.5 collective-permute-start.3
  2.6 0.1 collective-permute-start.4
  2.7 0.4 collective-permute-start.5
  3.2 2.6 %collective-permute-start = (f32[783,128]{1,0:T(8,128)S(1)}, f32[783,128]{1,0:T(8,128)S(1)}, u32[]{:S(2)}, u32[]{:S(2)}) collective-permute-start(f32[783,128]{1,0:T(8,128)S(1)} %get-tuple-element.21.refs_2_.refs_3_), channel_id=1, source_target_pairs={{0,2},{1,3},{2,0},{3,1},{4,6},{5,7},{6,4},{7,5},{8,10},{9,11},{10,... | collective-permute-start | bytes 1202696 | tf_op jit(solution)/shard_map/ppermute | solution.py:33
  5.7 4.6 %collective-permute-start.8 = (f32[783,128]{1,0:T(8,128)S(1)}, f32[783,128]{1,0:T(8,128)S(1)}, u32[]{:S(2)}, u32[]{:S(2)}) collective-permute-start(f32[783,128]{1,0:T(8,128)S(1)} %get-tuple-element.22.refs_0_), channel_id=1, source_target_pairs={{0,28},{4,0},{8,4},{12,8},{16,12},{20,16},{24,20},{28,24},{1,29},{... | collective-permute-start | bytes 1202696 | tf_op jit(solution)/shard_map/ppermute | solution.py:16
  10.3 0.0 collective-permute-done.3.refs_1_
  10.3 0.0 collective-permute-start.7
  10.3 0.0 collective-permute-done.4.refs_3_.refs_4_
  10.3 0.0 collective-permute-done.5.refs_5_.refs_1_
  10.3 1.7 %sums.6.refs_6_ = f32[2,9,128,128]{3,2,1,0:T(8,128)S(1)} custom-call(f32[783,128]{1,0:T(8,128)S(1)} %get-tuple-element.22.refs_0_, f32[783,128]{1,0:T(8,128)S(1)} %collective-permute-done.3.refs_1_, f32[783,128]{1,0:T(8,128)S(1)} %get-tuple-element.21.refs_2_.refs_3_, f32[783,128]{1,0:T(8,128)S(1)} %collective-permute-done.4.refs_3_.refs_4_, ...), custom_call_target="tpu_custom_call" | custom-call | flops 1 | bytes 1 | tf_op jit(solution)/shard_map/sums/pallas_call | solution.py:236
  12.0 0.6 %collective-permute-start.6 = (f32[783,128]{1,0:T(8,128)S(1)}, f32[783,128]{1,0:T(8,128)S(1)}, u32[]{:S(2)}, u32[]{:S(2)}) collective-permute-start(f32[783,128]{1,0:T(8,128)S(1)} %get-tuple-element.24.refs_4_.refs_0_), channel_id=1, source_target_pairs={{0,2},{1,3},{2,0},{3,1},{4,6},{5,7},{6,4},{7,5},{8,10},{9,11},{10,... | collective-permute-start | bytes 1202696 | tf_op jit(solution)/shard_map/ppermute | solution.py:33
  12.6 3.0 %collective-permute-done = f32[783,128]{1,0:T(8,128)S(1)} collective-permute-done((f32[783,128]{1,0:T(8,128)S(1)}, f32[783,128]{1,0:T(8,128)S(1)}, u32[]{:S(2)}, u32[]{:S(2)}) %collective-permute-start) | collective-permute-done | bytes 400928 | tf_op jit(solution)/shard_map/ppermute | solution.py:33
  15.6 0.1 collective-permute-start.1
  15.7 1.7 %collective-permute-done.1.refs_1_.refs_3_ = f32[776,128]{1,0:T(8,128)S(1)} collective-permute-done((f32[776,128]{1,0:T(8,128)S(1)}, f32[776,128]{1,0:T(8,128)S(1)}, u32[]{:S(2)}, u32[]{:S(2)}) %collective-permute-start.1) | collective-permute-done | bytes 397344 | tf_op jit(solution)/shard_map/ppermute | solution.py:33
  17.4 2.2 %collective-permute-start.2 = (f32[783,128]{1,0:T(8,128)S(1)}, f32[783,128]{1,0:T(8,128)S(1)}, u32[]{:S(2)}, u32[]{:S(2)}) collective-permute-start(f32[783,128]{1,0:T(8,128)S(1)} %get-tuple-element.22.refs_0_), channel_id=1, source_target_pairs={{0,2},{1,3},{2,0},{3,1},{4,6},{5,7},{6,4},{7,5},{8,10},{9,11},{10,... | collective-permute-start | bytes 1202696 | tf_op jit(solution)/shard_map/ppermute | solution.py:33
  19.6 6.0 %collective-permute-done.8.above = f32[783,128]{1,0:T(8,128)S(1)} collective-permute-done((f32[783,128]{1,0:T(8,128)S(1)}, f32[783,128]{1,0:T(8,128)S(1)}, u32[]{:S(2)}, u32[]{:S(2)}) %collective-permute-start.8) | collective-permute-done | bytes 400928 | tf_op jit(solution)/shard_map/ppermute | solution.py:16
  25.7 0.0 collective-permute-done.7.below
  25.7 0.0 collective-permute-done.6
  25.7 0.1 collective-permute-start.9
  25.8 2.1 %sums.7.refs_2_ = f32[790,128]{1,0:T(8,128)S(1)} custom-call(f32[783,128]{1,0:T(8,128)S(1)} %get-tuple-element.24.refs_4_.refs_0_, f32[783,128]{1,0:T(8,128)S(1)} %collective-permute-done.5.refs_5_.refs_1_, f32[776,128]{1,0:T(8,128)S(1)} %slice.13.refs_2_.refs_4_, f32[783,128]{1,0:T(8,128)S(1)} %get-tuple-element.21.refs_2_.refs_3_, ...), custom_call_target="tpu_custom_call" | custom-call | flops 1 | bytes 1 | tf_op jit(solution)/shard_map/sums/pallas_call | solution.py:236
  27.9 0.0 collective-permute-done.9.refs_0_.refs_5_
  27.9 1.0 %sums.8 = f32[790,128]{1,0:T(8,128)S(1)} custom-call(f32[776,128]{1,0:T(8,128)S(1)} %collective-permute-done.9.refs_0_.refs_5_, f32[776,128]{1,0:T(8,128)S(1)} %collective-permute-done.1.refs_1_.refs_3_, f32[790,128]{1,0:T(8,128)S(1)} %sums.7.refs_2_), custom_call_target="tpu_custom_call" | custom-call | flops 1 | bytes 1 | tf_op jit(solution)/shard_map/sums/pallas_call | solution.py:236
  28.9 1.5 %collective-permute-start.12 = (f32[790,128]{1,0:T(8,128)S(1)}, f32[790,128]{1,0:T(8,128)S(1)}, u32[]{:S(2)}, u32[]{:S(2)}) collective-permute-start(f32[790,128]{1,0:T(8,128)S(1)} %sums.8), channel_id=1, source_target_pairs={{0,5},{1,4},{2,7},{3,6},{4,9},{5,8},{6,11},{7,10},{8,13},{9,12},{1... | collective-permute-start | bytes 1213448 | tf_op jit(solution)/shard_map/ppermute | solution.py:28
  30.4 1.9 %partials.1 = (f32[778,128]{1,0:T(8,128)S(1)}, f32[778,128]{1,0:T(8,128)S(1)}, f32[778,128]{1,0:T(8,128)S(1)}, f32[778,128]{1,0:T(8,128)S(1)}) custom-call(f32[783,128]{1,0:T(8,128)S(1)} %collective-permute-done.7.below, f32[783,128]{1,0:T(8,128)S(1)} %collective-permute-done.8.above), custom_call_target="tpu_custom_call" | custom-call | flops 1 | bytes 1 | tf_op jit(solution)/shard_map/partials/pallas_call | solution.py:270
  32.4 2.0 %collective-permute-start.14 = (f32[778,128]{1,0:T(8,128)S(1)}, f32[778,128]{1,0:T(8,128)S(1)}, u32[]{:S(2)}, u32[]{:S(2)}) collective-permute-start(f32[778,128]{1,0:T(8,128)S(1)} %get-tuple-element.31), channel_id=1, source_target_pairs={{0,1},{1,0},{2,3},{3,2},{4,5},{5,4},{6,7},{7,6},{8,9},{9,8},{10,11... | collective-permute-start | bytes 1195016 | tf_op jit(solution)/shard_map/ppermute | solution.py:33
  34.3 0.1 collective-permute-start.15
  34.4 0.0 collective-permute-done.2
  34.5 0.5 collective-permute-start.10
  34.9 1.9 %sums.10.refs_2_ = f32[777,128]{1,0:T(8,128)S(1)} custom-call(f32[783,128]{1,0:T(8,128)S(1)} %get-tuple-element.22.refs_0_, f32[783,128]{1,0:T(8,128)S(1)} %collective-permute-done.3.refs_1_, f32[776,128]{1,0:T(8,128)S(1)} %slice.14.refs_0_.refs_2_, f32[783,128]{1,0:T(8,128)S(1)} %get-tuple-element.21.refs_2_.refs_3_, ...), custom_call_target="tpu_custom_call" | custom-call | flops 1 | bytes 1 | tf_op jit(solution)/shard_map/sums/pallas_call | solution.py:236
  36.8 0.0 collective-permute-done.14
  36.9 0.0 collective-permute-done.15
  36.9 0.1 add.7
  36.9 0.3 collective-permute-start.16
  37.3 0.0 collective-permute-done.10.refs_1_.refs_0_
  37.3 1.2 %sums.11 = f32[777,128]{1,0:T(8,128)S(1)} custom-call(f32[776,128]{1,0:T(8,128)S(1)} %collective-permute-done.10.refs_1_.refs_0_, f32[776,128]{1,0:T(8,128)S(1)} %collective-permute-done.1.refs_1_.refs_3_, f32[777,128]{1,0:T(8,128)S(1)} %sums.10.refs_2_), custom_call_target="tpu_custom_call" | custom-call | flops 1 | bytes 1 | tf_op jit(solution)/shard_map/sums/pallas_call | solution.py:236
  38.5 4.9 %collective-permute-start.11 = (f32[777,128]{1,0:T(8,128)S(1)}, f32[777,128]{1,0:T(8,128)S(1)}, u32[]{:S(2)}, u32[]{:S(2)}) collective-permute-start(f32[777,128]{1,0:T(8,128)S(1)} %sums.11), channel_id=1, source_target_pairs={{0,28},{4,0},{8,4},{12,8},{16,12},{20,16},{24,20},{28,24},{1,29},{... | collective-permute-start | bytes 1193480 | tf_op jit(solution)/shard_map/ppermute | solution.py:16
  43.4 1.3 %sums.9.base = f32[2,9,128,128]{3,2,1,0:T(8,128)S(1)} custom-call(f32[776,128]{1,0:T(8,128)S(1)} %slice.14.refs_0_.refs_2_, f32[776,128]{1,0:T(8,128)S(1)} %collective-permute-done.10.refs_1_.refs_0_, f32[776,128]{1,0:T(8,128)S(1)} %slice.16.refs_5_.refs_2_, f32[776,128]{1,0:T(8,128)S(1)} %collective-permute-done.1.refs_1_.refs_3_, ...), custom_call_target="tpu_custom_call" | custom-call | flops 1 | bytes 1 | tf_op jit(solution)/shard_map/sums/pallas_call | solution.py:236
  44.7 0.0 collective-permute-done.12
  44.7 0.2 collective-permute-start.13
  44.9 3.4 %collective-permute-done.16.refs_2_ = f32[778,128]{1,0:T(8,128)S(1)} collective-permute-done((f32[778,128]{1,0:T(8,128)S(1)}, f32[778,128]{1,0:T(8,128)S(1)}, u32[]{:S(2)}, u32[]{:S(2)}) %collective-permute-start.16) | collective-permute-done | bytes 398368 | tf_op jit(solution)/shard_map/ppermute | solution.py:33
  48.3 0.0 collective-permute-done.13.refs_0_
  48.3 1.0 %finish.2.refs_1_ = f32[2,9,128,128]{3,2,1,0:T(8,128)} custom-call(f32[2,9,128,128]{3,2,1,0:T(8,128)S(1)} %sums.9.base, f32[768,128]{1,0:T(8,128)S(1)} %collective-permute-done.13.refs_0_, f32[778,128]{1,0:T(8,128)S(1)} %add.6.refs_1_, f32[778,128]{1,0:T(8,128)S(1)} %collective-permute-done.16.refs_2_), custom_call_target="tpu_custom_call" | custom-call | flops 1 | bytes 1 | tf_op jit(solution)/shard_map/finish/pallas_call | solution.py:327
  49.3 2.7 %collective-permute-done.11.refs_0_ = f32[777,128]{1,0:T(8,128)S(1)} collective-permute-done((f32[777,128]{1,0:T(8,128)S(1)}, f32[777,128]{1,0:T(8,128)S(1)}, u32[]{:S(2)}, u32[]{:S(2)}) %collective-permute-start.11) | collective-permute-done | bytes 397856 | tf_op jit(solution)/shard_map/ppermute | solution.py:16
  51.9 0.8 %finish.3 = f32[2,9,128,128]{3,2,1,0:T(8,128)} custom-call(f32[2,9,128,128]{3,2,1,0:T(8,128)S(1)} %sums.9.base, f32[777,128]{1,0:T(8,128)S(1)} %collective-permute-done.11.refs_0_, f32[2,9,128,128]{3,2,1,0:T(8,128)} %finish.2.refs_1_), custom_call_target="tpu_custom_call", output_to_operand_aliasing={{}: (2, {})} | custom-call | flops 1 | bytes 1 | tf_op jit(solution)/shard_map/finish/pallas_call | solution.py:327
  (5 shorter events, 0.2 us)
Async XLA Ops:
  2.1 8.2 %collective-permute-start.3 = (f32[783,128]{1,0:T(8,128)S(1)}, f32[783,128]{1,0:T(8,128)S(1)}, u32[]{:S(2)}, u32[]{:S(2)}) collective-permute-start(f32[783,128]{1,0:T(8,128)S(1)} %get-tuple-element.22.refs_0_), channel_id=1, source_target_pairs={{0,1},{1,0},{2,3},{3,2},{4,5},{5,4},{6,7},{7,6},{8,9},{9,8},{10,11... | collective-permute-start | bytes 1202696 | tf_op jit(solution)/shard_map/ppermute | solution.py:33
  2.6 7.6 %collective-permute-start.4 = (f32[783,128]{1,0:T(8,128)S(1)}, f32[783,128]{1,0:T(8,128)S(1)}, u32[]{:S(2)}, u32[]{:S(2)}) collective-permute-start(f32[783,128]{1,0:T(8,128)S(1)} %get-tuple-element.21.refs_2_.refs_3_), channel_id=1, source_target_pairs={{0,1},{1,0},{2,3},{3,2},{4,5},{5,4},{6,7},{7,6},{8,9},{9,8},{10,11... | collective-permute-start | bytes 1202696 | tf_op jit(solution)/shard_map/ppermute | solution.py:33
  2.7 7.6 %collective-permute-start.5 = (f32[783,128]{1,0:T(8,128)S(1)}, f32[783,128]{1,0:T(8,128)S(1)}, u32[]{:S(2)}, u32[]{:S(2)}) collective-permute-start(f32[783,128]{1,0:T(8,128)S(1)} %get-tuple-element.24.refs_4_.refs_0_), channel_id=1, source_target_pairs={{0,1},{1,0},{2,3},{3,2},{4,5},{5,4},{6,7},{7,6},{8,9},{9,8},{10,11... | collective-permute-start | bytes 1202696 | tf_op jit(solution)/shard_map/ppermute | solution.py:33
  3.2 12.4 %collective-permute-start = (f32[783,128]{1,0:T(8,128)S(1)}, f32[783,128]{1,0:T(8,128)S(1)}, u32[]{:S(2)}, u32[]{:S(2)}) collective-permute-start(f32[783,128]{1,0:T(8,128)S(1)} %get-tuple-element.21.refs_2_.refs_3_), channel_id=1, source_target_pairs={{0,2},{1,3},{2,0},{3,1},{4,6},{5,7},{6,4},{7,5},{8,10},{9,11},{10,... | collective-permute-start | bytes 1202696 | tf_op jit(solution)/shard_map/ppermute | solution.py:33
  5.7 20.0 %collective-permute-start.8 = (f32[783,128]{1,0:T(8,128)S(1)}, f32[783,128]{1,0:T(8,128)S(1)}, u32[]{:S(2)}, u32[]{:S(2)}) collective-permute-start(f32[783,128]{1,0:T(8,128)S(1)} %get-tuple-element.22.refs_0_), channel_id=1, source_target_pairs={{0,28},{4,0},{8,4},{12,8},{16,12},{20,16},{24,20},{28,24},{1,29},{... | collective-permute-start | bytes 1202696 | tf_op jit(solution)/shard_map/ppermute | solution.py:16
  10.3 15.4 %collective-permute-start.7 = (f32[783,128]{1,0:T(8,128)S(1)}, f32[783,128]{1,0:T(8,128)S(1)}, u32[]{:S(2)}, u32[]{:S(2)}) collective-permute-start(f32[783,128]{1,0:T(8,128)S(1)} %get-tuple-element.24.refs_4_.refs_0_), channel_id=1, source_target_pairs={{0,4},{4,8},{8,12},{12,16},{16,20},{20,24},{24,28},{28,0},{1,5},{5... | collective-permute-start | bytes 1202696 | tf_op jit(solution)/shard_map/ppermute | solution.py:16
  12.0 13.7 %collective-permute-start.6 = (f32[783,128]{1,0:T(8,128)S(1)}, f32[783,128]{1,0:T(8,128)S(1)}, u32[]{:S(2)}, u32[]{:S(2)}) collective-permute-start(f32[783,128]{1,0:T(8,128)S(1)} %get-tuple-element.24.refs_4_.refs_0_), channel_id=1, source_target_pairs={{0,2},{1,3},{2,0},{3,1},{4,6},{5,7},{6,4},{7,5},{8,10},{9,11},{10,... | collective-permute-start | bytes 1202696 | tf_op jit(solution)/shard_map/ppermute | solution.py:33
  15.6 1.8 %collective-permute-start.1 = (f32[776,128]{1,0:T(8,128)S(1)}, f32[776,128]{1,0:T(8,128)S(1)}, u32[]{:S(2)}, u32[]{:S(2)}) collective-permute-start(f32[776,128]{1,0:T(8,128)S(1)} %slice.16.refs_5_.refs_2_), channel_id=1, source_target_pairs={{0,1},{1,0},{2,3},{3,2},{4,5},{5,4},{6,7},{7,6},{8,9},{9,8},{10,11... | collective-permute-start | bytes 1191944 | tf_op jit(solution)/shard_map/ppermute | solution.py:33
  17.4 17.0 %collective-permute-start.2 = (f32[783,128]{1,0:T(8,128)S(1)}, f32[783,128]{1,0:T(8,128)S(1)}, u32[]{:S(2)}, u32[]{:S(2)}) collective-permute-start(f32[783,128]{1,0:T(8,128)S(1)} %get-tuple-element.22.refs_0_), channel_id=1, source_target_pairs={{0,2},{1,3},{2,0},{3,1},{4,6},{5,7},{6,4},{7,5},{8,10},{9,11},{10,... | collective-permute-start | bytes 1202696 | tf_op jit(solution)/shard_map/ppermute | solution.py:33
  25.7 2.2 %collective-permute-start.9 = (f32[776,128]{1,0:T(8,128)S(1)}, f32[776,128]{1,0:T(8,128)S(1)}, u32[]{:S(2)}, u32[]{:S(2)}) collective-permute-start(f32[776,128]{1,0:T(8,128)S(1)} %slice.13.refs_2_.refs_4_), channel_id=1, source_target_pairs={{0,1},{1,0},{2,3},{3,2},{4,5},{5,4},{6,7},{7,6},{8,9},{9,8},{10,11... | collective-permute-start | bytes 1191944 | tf_op jit(solution)/shard_map/ppermute | solution.py:33
  28.9 15.8 %collective-permute-start.12 = (f32[790,128]{1,0:T(8,128)S(1)}, f32[790,128]{1,0:T(8,128)S(1)}, u32[]{:S(2)}, u32[]{:S(2)}) collective-permute-start(f32[790,128]{1,0:T(8,128)S(1)} %sums.8), channel_id=1, source_target_pairs={{0,5},{1,4},{2,7},{3,6},{4,9},{5,8},{6,11},{7,10},{8,13},{9,12},{1... | collective-permute-start | bytes 1213448 | tf_op jit(solution)/shard_map/ppermute | solution.py:28
  32.4 4.4 %collective-permute-start.14 = (f32[778,128]{1,0:T(8,128)S(1)}, f32[778,128]{1,0:T(8,128)S(1)}, u32[]{:S(2)}, u32[]{:S(2)}) collective-permute-start(f32[778,128]{1,0:T(8,128)S(1)} %get-tuple-element.31), channel_id=1, source_target_pairs={{0,1},{1,0},{2,3},{3,2},{4,5},{5,4},{6,7},{7,6},{8,9},{9,8},{10,11... | collective-permute-start | bytes 1195016 | tf_op jit(solution)/shard_map/ppermute | solution.py:33
  34.3 2.5 %collective-permute-start.15 = (f32[778,128]{1,0:T(8,128)S(1)}, f32[778,128]{1,0:T(8,128)S(1)}, u32[]{:S(2)}, u32[]{:S(2)}) collective-permute-start(f32[778,128]{1,0:T(8,128)S(1)} %get-tuple-element.33), channel_id=1, source_target_pairs={{0,1},{1,0},{2,3},{3,2},{4,5},{5,4},{6,7},{7,6},{8,9},{9,8},{10,11... | collective-permute-start | bytes 1195016 | tf_op jit(solution)/shard_map/ppermute | solution.py:33
  34.5 2.8 %collective-permute-start.10 = (f32[776,128]{1,0:T(8,128)S(1)}, f32[776,128]{1,0:T(8,128)S(1)}, u32[]{:S(2)}, u32[]{:S(2)}) collective-permute-start(f32[776,128]{1,0:T(8,128)S(1)} %slice.14.refs_0_.refs_2_), channel_id=1, source_target_pairs={{0,1},{1,0},{2,3},{3,2},{4,5},{5,4},{6,7},{7,6},{8,9},{9,8},{10,11... | collective-permute-start | bytes 1191944 | tf_op jit(solution)/shard_map/ppermute | solution.py:33
  36.9 11.3 %collective-permute-start.16 = (f32[778,128]{1,0:T(8,128)S(1)}, f32[778,128]{1,0:T(8,128)S(1)}, u32[]{:S(2)}, u32[]{:S(2)}) collective-permute-start(f32[778,128]{1,0:T(8,128)S(1)} %add.7), channel_id=1, source_target_pairs={{0,2},{1,3},{2,0},{3,1},{4,6},{5,7},{6,4},{7,5},{8,10},{9,11},{10,... | collective-permute-start | bytes 1195016 | tf_op jit(solution)/shard_map/ppermute | solution.py:33
  38.5 13.4 %collective-permute-start.11 = (f32[777,128]{1,0:T(8,128)S(1)}, f32[777,128]{1,0:T(8,128)S(1)}, u32[]{:S(2)}, u32[]{:S(2)}) collective-permute-start(f32[777,128]{1,0:T(8,128)S(1)} %sums.11), channel_id=1, source_target_pairs={{0,28},{4,0},{8,4},{12,8},{16,12},{20,16},{24,20},{28,24},{1,29},{... | collective-permute-start | bytes 1193480 | tf_op jit(solution)/shard_map/ppermute | solution.py:16
  44.7 3.6 %collective-permute-start.13 = (f32[768,128]{1,0:T(8,128)S(1)}, f32[768,128]{1,0:T(8,128)S(1)}, u32[]{:S(2)}, u32[]{:S(2)}) collective-permute-start(f32[768,128]{1,0:T(8,128)S(1)} %slice.15), channel_id=1, source_target_pairs={{0,1},{1,0},{2,3},{3,2},{4,5},{5,4},{6,7},{7,6},{8,9},{9,8},{10,11... | collective-permute-start | bytes 1179656 | tf_op jit(solution)/shard_map/ppermute | solution.py:33
